TPU v7x, 32 devices: a whole 2x2x4 slice. The times are simulated.
32 devices in a mesh: ctx: 8 (over z, y), tp: 4 (over x, core).
Axes of the slice: x: 2, y: 2, z: 4, core: 2. Of those that a mesh axis runs over, the one named last changes fastest.
Arguments:
- first_stream: bfloat16 [4096, 8192], P(('ctx', 'tp')), may hold values from -6 to 6
- second_stream: bfloat16 [4096, 8192], P(('ctx', 'tp')), may hold values from -6 to 6
- value_stream: bfloat16 [4096, 8192], P(('ctx', 'tp')), may hold values from -6 to 6
- short_filter: bfloat16 [3, 7, 512], replicated, may hold values from -2 to 2
- long_filter: bfloat16 [128, 512], replicated, may hold values from -0.5 to 0.5
- skip_gain: float32 [8192], replicated, may hold values from -3 to 3
- lengths: int32 [16], replicated, may hold values from 1 to 512, 4096 in all
Outputs:
- mixed: bfloat16 [8192, 4096], P(('ctx', 'tp'))
Inputs may be any that keep to these rules, and one draw needn't show every extreme that they name: The lengths of the 16 segments packed into the window in order; they sum to 4096.
All inputs are finite; a program needn't handle non-finite values.
Results may differ from a plain program's by a relative error of at most 0.0085.
Values may be sent and summed in bfloat16 or wider, within the bound.
No kernel may reach another device: no remote copies, remote signals or barrier semaphores. Data moves between devices by JAX's collectives and lax.ppermute only.
A program may use at most 192 MiB of HBM per device.

v0:
```python
import math

import jax
import jax.numpy as jnp
from jax import lax
from jax.sharding import PartitionSpec as P

GROUP = 16


def segment_offsets(lengths, row_count):
    ends = jnp.cumsum(lengths)
    starts = ends - lengths
    positions = jnp.arange(row_count, dtype=jnp.int32)
    inside = starts[None, :] <= positions[:, None]
    begins = jnp.max(jnp.where(inside, starts[None, :], 0), axis=1)
    return positions - begins


def short_conv_cols(padded, tap_table, offsets):
    row_count = offsets.shape[0]
    tap_count = tap_table.shape[0]
    summed = jnp.zeros((padded.shape[0], row_count), jnp.float32)
    for tap_index in range(tap_count):
        shifted = padded[
            :, tap_count - 1 - tap_index : tap_count - 1 - tap_index + row_count
        ].astype(jnp.float32)
        summed = summed + jnp.where(
            (tap_index <= offsets)[None, :],
            tap_table[tap_index].astype(jnp.float32)[:, None] * shifted,
            0.0,
        )
    return summed


def featurize_cols(padded_streams, tap_table, offsets):
    first_feature = short_conv_cols(padded_streams[0], tap_table[0], offsets)
    second_feature = short_conv_cols(padded_streams[1], tap_table[1], offsets)
    value_feature = short_conv_cols(padded_streams[2], tap_table[2], offsets)
    return (
        (first_feature * value_feature).astype(jnp.bfloat16),
        second_feature.astype(jnp.bfloat16),
    )


def toeplitz_base(unit_taps):
    length, unit_count = unit_taps.shape
    column = jnp.concatenate(
        [unit_taps[::-1], jnp.zeros((length, unit_count), unit_taps.dtype)], axis=0
    )
    repeated = jnp.tile(column, (length, 1))
    return repeated[: length * (2 * length - 1)].reshape(length, 2 * length - 1, unit_count)


def long_conv_cols(windows, offsets, unit_taps, members):
    channels, block_count, window_len = windows.shape
    length, unit_count = unit_taps.shape
    toeplitz = toeplitz_base(unit_taps)
    lag_table = (
        jnp.arange(length, dtype=jnp.int32)[:, None]
        + (length - 1)
        - jnp.arange(window_len, dtype=jnp.int32)[None, :]
    )
    per_block = length * window_len * unit_count
    per_step = math.gcd(block_count, max(1, (1 << 22) // per_block))
    grouped = windows.reshape(unit_count, members, block_count, window_len)

    def one_step(step, result):
        first_block = step * per_step
        block_rows = lax.dynamic_slice_in_dim(grouped, first_block, per_step, 2)
        block_offsets = lax.dynamic_slice_in_dim(offsets, first_block, per_step, 0)
        keep_mask = (lag_table[None] <= block_offsets[:, :, None]).astype(jnp.bfloat16)
        weights = toeplitz[None] * keep_mask[..., None]
        part = jnp.einsum(
            "btsu,umbs->umbt", weights, block_rows, preferred_element_type=jnp.float32
        )
        return lax.dynamic_update_slice_in_dim(result, part, first_block, 2)

    result = lax.fori_loop(
        0,
        block_count // per_step,
        one_step,
        jnp.zeros((unit_count, members, block_count, length), jnp.float32),
    )
    return result.reshape(channels, block_count * length)


def block_windows_cols(values, rim_cols):
    channels, row_count = values.shape
    length = rim_cols.shape[1] + 1
    blocks = values.reshape(channels, row_count // length, length)
    earlier = jnp.concatenate([rim_cols[:, None], blocks[:, :-1, 1:]], axis=1)
    return jnp.concatenate([earlier, blocks], axis=2)


def channel_mix_cols(mixed_in, gate, offsets, long_taps, skip_gain, first_channel):
    channels, row_count = mixed_in.shape
    length = long_taps.shape[0]
    members = min(GROUP, channels)
    unit_taps = lax.dynamic_slice_in_dim(long_taps, first_channel, channels, 1)[:, ::members]
    windows = block_windows_cols(mixed_in, jnp.zeros((channels, length - 1), jnp.bfloat16))
    convolved = long_conv_cols(
        windows, offsets.reshape(row_count // length, length), unit_taps, members
    )
    skip_part = lax.dynamic_slice_in_dim(skip_gain, first_channel, channels, 0)
    gated = gate.astype(jnp.float32) * (
        convolved + skip_part[:, None] * mixed_in.astype(jnp.float32)
    )
    return gated.astype(jnp.bfloat16)


def on_device(
    first_stream, second_stream, value_stream, short_filter, long_filter, skip_gain, lengths
):
    row_count, channels = first_stream.shape
    devices = lax.axis_size(("ctx", "tp"))
    device_index = lax.axis_index(("ctx", "tp"))
    channel_count = channels // devices
    first_channel = device_index * channel_count
    all_rows = row_count * devices
    short_taps = jnp.repeat(short_filter, GROUP, axis=2)
    long_taps = jnp.repeat(long_filter, GROUP, axis=1)
    relaid = (
        lax.all_to_all(
            lax.all_to_all(
                first_stream.T.reshape(channels, 1, 1, row_count),
                "ctx",
                split_axis=0,
                concat_axis=1,
                tiled=True,
            ),
            "tp",
            split_axis=0,
            concat_axis=2,
            tiled=True,
        ),
        lax.all_to_all(
            lax.all_to_all(
                second_stream.T.reshape(channels, 1, 1, row_count),
                "ctx",
                split_axis=0,
                concat_axis=1,
                tiled=True,
            ),
            "tp",
            split_axis=0,
            concat_axis=2,
            tiled=True,
        ),
        lax.all_to_all(
            lax.all_to_all(
                value_stream.T.reshape(channels, 1, 1, row_count),
                "ctx",
                split_axis=0,
                concat_axis=1,
                tiled=True,
            ),
            "tp",
            split_axis=0,
            concat_axis=2,
            tiled=True,
        ),
    )
    offsets = segment_offsets(lengths, all_rows)
    tap_count = short_taps.shape[1]
    padded = tuple(
        (
            jnp.concatenate(
                [
                    jnp.zeros((channel_count, tap_count - 1), jnp.bfloat16),
                    part.reshape(channel_count, all_rows),
                ],
                axis=1,
            )
            for part in relaid
        )
    )
    own_taps = lax.dynamic_slice_in_dim(short_taps, first_channel, channel_count, 2)
    mixed_in, gate = featurize_cols(padded, own_taps, offsets)
    return channel_mix_cols(mixed_in, gate, offsets, long_taps, skip_gain, first_channel)


def solution(mesh):
    placed = (
        P(("ctx", "tp"), None),
        P(("ctx", "tp"), None),
        P(("ctx", "tp"), None),
        P(),
        P(),
        P(),
        P(),
    )
    return jax.shard_map(
        on_device, mesh=mesh, in_specs=placed, out_specs=P(("ctx", "tp"), None), check_vma=False
    )
```

profile of v0, /device:TPU:0, one launch (start us, length us, event | category | flops | bytes accessed | tf_op | source)
XLA Modules:
  0.0 373.3 jit_solution(1067528767586122099)
XLA Ops:
  0.0 3.2 copy.92
  3.8 2.9 reduce.2
  6.7 5.8 %reshape.344 = bf16[8,2,65536]{2,1,0:T(2,128)(2,1)} reshape(bf16[8192,128]{1,0:T(8,128)(2,1)} %reduce.2) | data formatting | bytes 4194304
  12.4 7.3 %all-to-all-start.2 = ((bf16[8,2,65536]{2,1,0:T(2,128)(2,1)}), bf16[8,2,65536]{2,1,0:T(2,128)(2,1)S(1)}, u32[]{:S(2)}, u32[]{:S(2)}) async-start(bf16[8,2,65536]{2,1,0:T(2,128)(2,1)} %reshape.344), calls=%async_computation.2 | async-start | bytes 4194304 | tf_op jit(solution)/shard_map/all_to_all | solution.py:125
  19.7 4.1 %copy.96 = bf16[128,8192]{0,1:T(8,128)(2,1)} copy(bf16[128,8192]{1,0:T(8,128)(2,1)} %param.11) | data formatting | bytes 4194304 | tf_op args[2]
  23.8 4.5 %reduce.1 = bf16[8192,128]{1,0:T(8,128)(2,1)} reduce(bf16[8192,1,1,128]{3,0,2,1:T(8,128)(2,1)} %bitcast.94, bf16[]{:T(256)} %broadcast.101), dimensions={1,2}, to_apply=%copy.97.reduce_sub_computation | reduce | bytes 4194306 | tf_op jit(solution)/shard_map/reshape | solution.py:152
  28.3 5.8 %reshape.342 = bf16[8,2,65536]{2,1,0:T(2,128)(2,1)} reshape(bf16[8192,128]{1,0:T(8,128)(2,1)} %reduce.1) | data formatting | bytes 4194304
  34.1 33.9 %all-to-all-done.2 = bf16[8,2,65536]{2,1,0:T(2,128)(2,1)S(1)} async-done(((bf16[8,2,65536]{2,1,0:T(2,128)(2,1)}), bf16[8,2,65536]{2,1,0:T(2,128)(2,1)S(1)}, u32[]{:S(2)}, u32[]{:S(2)}) %all-to-all-start.2) | async-done | bytes 2097184 | tf_op jit(solution)/shard_map/all_to_all | solution.py:125
  68.0 1.3 copy-done.3
  69.3 3.6 all-to-all-start.4
  72.9 4.1 %copy.88 = bf16[128,8192]{0,1:T(8,128)(2,1)} copy(bf16[128,8192]{1,0:T(8,128)(2,1)} %param.10) | data formatting | bytes 4194304 | tf_op args[1]
  77.1 4.5 %reduce.3 = bf16[8192,128]{1,0:T(8,128)(2,1)} reduce(bf16[8192,1,1,128]{3,0,2,1:T(8,128)(2,1)} %bitcast.93, bf16[]{:T(256)} %broadcast.101), dimensions={1,2}, to_apply=%copy.89.reduce_sub_computation | reduce | bytes 4194306 | tf_op jit(solution)/shard_map/reshape | solution.py:139
  81.6 5.8 %reshape.346 = bf16[8,2,65536]{2,1,0:T(2,128)(2,1)} reshape(bf16[8192,128]{1,0:T(8,128)(2,1)} %reduce.3) | data formatting | bytes 4194304
  87.4 34.0 %all-to-all-done.4 = bf16[8,2,65536]{2,1,0:T(2,128)(2,1)S(1)} async-done(((bf16[8,2,65536]{2,1,0:T(2,128)(2,1)}), bf16[8,2,65536]{2,1,0:T(2,128)(2,1)S(1)}, u32[]{:S(2)}, u32[]{:S(2)}) %all-to-all-start.4) | async-done | bytes 2097184 | tf_op jit(solution)/shard_map/all_to_all | solution.py:151
  121.4 1.3 copy-done.2
  122.7 3.6 all-to-all-start
  126.3 6.8 %reshape.345 = bf16[8192,1,1,128]{3,2,1,0:T(2,128)(2,1)} reshape(bf16[8,2,65536]{2,1,0:T(2,128)(2,1)} %copy-done.3) | data formatting | bytes 4194304
  133.1 2.5 copy.110
  135.6 2.7 copy.94
  138.3 36.4 %all-to-all-done = bf16[8,2,65536]{2,1,0:T(2,128)(2,1)S(1)} async-done(((bf16[8,2,65536]{2,1,0:T(2,128)(2,1)}), bf16[8,2,65536]{2,1,0:T(2,128)(2,1)S(1)}, u32[]{:S(2)}, u32[]{:S(2)}) %all-to-all-start) | async-done | bytes 2097184 | tf_op jit(solution)/shard_map/all_to_all | solution.py:138
  174.7 4.5 %all-to-all-start.3 = ((bf16[1024,8,1,128]{3,1,2,0:T(8,128)(2,1)}), bf16[1024,8,1,128]{3,1,2,0:T(8,128)(2,1)}, u32[]{:S(2)}, u32[]{:S(2)}) async-start(bf16[1024,8,1,128]{3,1,2,0:T(8,128)(2,1)} %copy.94), calls=%async_computation.3 | async-start | bytes 4194304 | tf_op jit(solution)/shard_map/all_to_all | solution.py:124
  179.2 6.8 %reshape.343 = bf16[8192,1,1,128]{3,2,1,0:T(2,128)(2,1)} reshape(bf16[8,2,65536]{2,1,0:T(2,128)(2,1)} %copy-done.2) | data formatting | bytes 4194304
  186.0 2.5 copy.111
  188.5 2.7 copy.98
  191.1 13.8 %all-to-all-done.3 = bf16[1024,8,1,128]{3,1,2,0:T(8,128)(2,1)} async-done(((bf16[1024,8,1,128]{3,1,2,0:T(8,128)(2,1)}), bf16[1024,8,1,128]{3,1,2,0:T(8,128)(2,1)}, u32[]{:S(2)}, u32[]{:S(2)}) %all-to-all-start.3) | async-done | bytes 2097184 | tf_op jit(solution)/shard_map/all_to_all | solution.py:124
  205.0 4.6 %all-to-all-start.5 = ((bf16[1024,8,1,128]{3,1,2,0:T(8,128)(2,1)}), bf16[1024,8,1,128]{3,1,2,0:T(8,128)(2,1)}, u32[]{:S(2)}, u32[]{:S(2)}) async-start(bf16[1024,8,1,128]{3,1,2,0:T(8,128)(2,1)} %copy.98), calls=%async_computation.5 | async-start | bytes 4194304 | tf_op jit(solution)/shard_map/all_to_all | solution.py:150
  209.6 1.7 broadcast_in_dim.183
  211.3 3.8 %reshape.310 = bf16[3,7,8192]{2,1,0:T(8,128)(2,1)S(1)} reshape(bf16[3,7,512,16]{3,2,1,0:T(8,128)(2,1)S(1)} %broadcast_in_dim.183) | data formatting | bytes 688128 | tf_op jit(solution)/shard_map/reshape | solution.py:121
  218.1 1.3 dynamic_slice.25
  220.4 4.5 %reshape.347 = bf16[8192,1,1,128]{3,2,1,0:T(2,128)(2,1)} reshape(bf16[8,2,65536]{2,1,0:T(2,128)(2,1)S(1)} %copy-done.1) | data formatting | bytes 4194304
  224.9 2.5 copy.112
  227.4 2.7 copy.90
  230.1 4.3 %copy.95 = bf16[256,8,4,1,128]{0,4,2,1,3:T(8,128)(2,1)} copy(bf16[256,8,4,1,128]{4,1,0,2,3:T(8,128)(2,1)} %bitcast.21) | data formatting | bytes 4194304 | tf_op jit(solution)/shard_map/all_to_all | solution.py:124
  235.2 4.7 %all-to-all-start.1 = ((bf16[1024,8,1,128]{3,1,2,0:T(8,128)(2,1)}), bf16[1024,8,1,128]{3,1,2,0:T(8,128)(2,1)}, u32[]{:S(2)}, u32[]{:S(2)}) async-start(bf16[1024,8,1,128]{3,1,2,0:T(8,128)(2,1)} %copy.90), calls=%async_computation.1 | async-start | bytes 4194304 | tf_op jit(solution)/shard_map/all_to_all | solution.py:137
  239.9 4.3 %copy.99 = bf16[256,8,4,1,128]{0,4,2,1,3:T(8,128)(2,1)} copy(bf16[256,8,4,1,128]{4,1,0,2,3:T(8,128)(2,1)} %bitcast.35) | data formatting | bytes 4194304 | tf_op jit(solution)/shard_map/all_to_all | solution.py:150
  244.3 20.7 %multiply_convert_fusion.1 = bf16[256,4096]{0,1:T(8,128)(2,1)S(1)} fusion(bf16[256,4096]{0,1:T(8,128)(2,1)} %bitcast.87, bf16[256,4096]{0,1:T(8,128)(2,1)} %bitcast.85, f32[256]{0:T(256)S(1)} %bitcast.120, f32[256]{0:T(256)S(1)} %bitcast.107, f32[256]{0:T(256)S(1)} %bitcast.108, f32[256]{0:T(256)S(1)} %bitcast.109, f32[256]{0:T(256)S(1)} %bitcast.110, ...), kind=kLoop, calls=%fused_computation.15 | loop fusion | flops 58720256 | bytes 6334464 | tf_op jit(solution)/shard_map/convert_element_type | solution.py:41
  264.9 2.9 copy.101
  267.8 2.6 slice.213
  270.4 4.6 %copy.113 = bf16[256,31,127]{2,1,0:T(8,128)(2,1)} copy(bf16[256,31,127]{0,2,1:T(8,128)(2,1)} %slice.213) | data formatting | bytes 4031488
  275.0 2.7 concatenate.26
  278.2 3.7 pad_maximum_fusion
  281.9 2.6 broadcast_in_dim.191.clone
  284.4 52.7 %while.14 = (s32[]{:T(128)}, f32[16,16,32,128]{3,2,1,0:T(8,128)}, bf16[16,16,32,255]{3,2,1,0:T(8,128)(2,1)}, bf16[32640,16]{0,1:T(8,128)(2,1)S(1)}, s32[32,128]{...) while((s32[]{:T(128)}, f32[16,16,32,128]{3,2,1,0:T(8,128)}, ...), condition=%wide.region_3.4_spmd.clone, body=%wide.region_2.3_spmd.clone.sunk | while | flops 138426240 | bytes 10731167 | solution.py:79
  285.5 2.3 constant_dynamic-slice_fusion.15
  287.9 4.3 %mul.372 = bf16[128,255,16]{1,0,2:T(8,128)(2,1)} reshape(bf16[32640,16]{0,1:T(8,128)(2,1)S(1)} %get-tuple-element.254) | data formatting | bytes 2088960 | tf_op jit(solution)/shard_map/while/body/eval_jaxpr/mul | solution.py:73
  292.2 4.0 %fusion.31 = f32[16,16,8,128]{3,1,2,0:T(8,128)S(1)} fusion(bf16[8,128,255]{2,1,0:T(8,128)(2,1)} %compare_convert_fusion.2, bf16[128,255,16]{1,0,2:T(8,128)(2,1)} %mul.372, bf16[16,16,8,255]{3,2,1,0:T(8,128)(2,1)} %constant_dynamic-slice_fusion.15), kind=kOutput, calls=%fused_computation.5.clone.1 | convolution fusion | flops 137871360 | bytes 3659776 | tf_op jit(solution)/shard_map/while/body/eval_jaxpr/btsu,umbs->umbt/dot_general | solution.py:74
  296.2 1.4 copy_dynamic-update-slice_fusion.2
  298.7 2.3 constant_dynamic-slice_fusion.15
  301.0 4.3 %mul.372 = bf16[128,255,16]{1,0,2:T(8,128)(2,1)} reshape(bf16[32640,16]{0,1:T(8,128)(2,1)S(1)} %get-tuple-element.254) | data formatting | bytes 2088960 | tf_op jit(solution)/shard_map/while/body/eval_jaxpr/mul | solution.py:73
  305.3 4.0 %fusion.31 = f32[16,16,8,128]{3,1,2,0:T(8,128)S(1)} fusion(bf16[8,128,255]{2,1,0:T(8,128)(2,1)} %compare_convert_fusion.2, bf16[128,255,16]{1,0,2:T(8,128)(2,1)} %mul.372, bf16[16,16,8,255]{3,2,1,0:T(8,128)(2,1)} %constant_dynamic-slice_fusion.15), kind=kOutput, calls=%fused_computation.5.clone.1 | convolution fusion | flops 137871360 | bytes 3659776 | tf_op jit(solution)/shard_map/while/body/eval_jaxpr/btsu,umbs->umbt/dot_general | solution.py:74
  309.3 1.4 copy_dynamic-update-slice_fusion.2
  311.8 2.3 constant_dynamic-slice_fusion.15
  314.1 4.3 %mul.372 = bf16[128,255,16]{1,0,2:T(8,128)(2,1)} reshape(bf16[32640,16]{0,1:T(8,128)(2,1)S(1)} %get-tuple-element.254) | data formatting | bytes 2088960 | tf_op jit(solution)/shard_map/while/body/eval_jaxpr/mul | solution.py:73
  318.5 4.0 %fusion.31 = f32[16,16,8,128]{3,1,2,0:T(8,128)S(1)} fusion(bf16[8,128,255]{2,1,0:T(8,128)(2,1)} %compare_convert_fusion.2, bf16[128,255,16]{1,0,2:T(8,128)(2,1)} %mul.372, bf16[16,16,8,255]{3,2,1,0:T(8,128)(2,1)} %constant_dynamic-slice_fusion.15), kind=kOutput, calls=%fused_computation.5.clone.1 | convolution fusion | flops 137871360 | bytes 3659776 | tf_op jit(solution)/shard_map/while/body/eval_jaxpr/btsu,umbs->umbt/dot_general | solution.py:74
  322.4 1.4 copy_dynamic-update-slice_fusion.2
  325.0 2.3 constant_dynamic-slice_fusion.15
  327.3 4.3 %mul.372 = bf16[128,255,16]{1,0,2:T(8,128)(2,1)} reshape(bf16[32640,16]{0,1:T(8,128)(2,1)S(1)} %get-tuple-element.254) | data formatting | bytes 2088960 | tf_op jit(solution)/shard_map/while/body/eval_jaxpr/mul | solution.py:73
  331.6 4.0 %fusion.31 = f32[16,16,8,128]{3,1,2,0:T(8,128)S(1)} fusion(bf16[8,128,255]{2,1,0:T(8,128)(2,1)} %compare_convert_fusion.2, bf16[128,255,16]{1,0,2:T(8,128)(2,1)} %mul.372, bf16[16,16,8,255]{3,2,1,0:T(8,128)(2,1)} %constant_dynamic-slice_fusion.15), kind=kOutput, calls=%fused_computation.5.clone.1 | convolution fusion | flops 137871360 | bytes 3659776 | tf_op jit(solution)/shard_map/while/body/eval_jaxpr/btsu,umbs->umbt/dot_general | solution.py:74
  335.6 1.5 copy_dynamic-update-slice_fusion.2
  337.1 8.0 %copy.121 = f32[32,8,32,128]{3,1,2,0:T(8,128)} copy(f32[32,8,32,128]{3,2,1,0:T(8,128)} %bitcast.73) | data formatting | bytes 8388608
  345.1 5.7 %copy.105 = f32[256,4096]{0,1:T(8,128)} copy(f32[256,4096]{1,0:T(8,128)} %bitcast.84) | data formatting | bytes 8388608 | tf_op jit(solution)/shard_map/reshape | solution.py:85
  350.8 4.3 %copy.91 = bf16[256,8,4,1,128]{0,4,2,1,3:T(8,128)(2,1)} copy(bf16[256,8,4,1,128]{4,1,0,2,3:T(8,128)(2,1)} %bitcast.7) | data formatting | bytes 4194304 | tf_op jit(solution)/shard_map/all_to_all | solution.py:137
  355.1 14.1 %multiply_convert_fusion = bf16[256,4096]{0,1:T(8,128)(2,1)} fusion(f32[256,4096]{0,1:T(8,128)} %copy.105, bf16[256,4096]{0,1:T(8,128)(2,1)S(1)} %multiply_convert_fusion.1, bf16[256,4096]{0,1:T(8,128)(2,1)} %bitcast.86, f32[256]{0:T(256)S(1)} %copy-done.23, f32[256]{0:T(256)S(1)} %bitcast.101, f32[256]{0:T(256)S(1)} %bitcast.102, f32[256]{0:T(256)S(1)} %bitcast.103, ...), kind=kLoop, calls=%fused_computation.14 | loop fusion | flops 35651584 | bytes 10522624 | tf_op jit(solution)/shard_map/convert_element_type | solution.py:109
  369.2 4.1 %copy.106 = bf16[256,4096]{1,0:T(8,128)(2,1)} copy(bf16[256,4096]{0,1:T(8,128)(2,1)} %multiply_convert_fusion) | data formatting | bytes 4194304 | tf_op jit(solution)/shard_map/convert_element_type | solution.py:109
  (84 shorter events, 10.0 us)
Async XLA Ops:
  12.4 55.5 %all-to-all-start.2 = ((bf16[8,2,65536]{2,1,0:T(2,128)(2,1)}), bf16[8,2,65536]{2,1,0:T(2,128)(2,1)S(1)}, u32[]{:S(2)}, u32[]{:S(2)}) async-start(bf16[8,2,65536]{2,1,0:T(2,128)(2,1)} %reshape.344), calls=%async_computation.2 | async-start | bytes 4194304 | tf_op jit(solution)/shard_map/all_to_all | solution.py:125
  68.0 1.3 copy-start.3
  69.3 52.1 %all-to-all-start.4 = ((bf16[8,2,65536]{2,1,0:T(2,128)(2,1)}), bf16[8,2,65536]{2,1,0:T(2,128)(2,1)S(1)}, u32[]{:S(2)}, u32[]{:S(2)}) async-start(bf16[8,2,65536]{2,1,0:T(2,128)(2,1)} %reshape.342), calls=%async_computation.4 | async-start | bytes 4194304 | tf_op jit(solution)/shard_map/all_to_all | solution.py:151
  121.3 1.3 copy-start.2
  122.7 52.1 %all-to-all-start = ((bf16[8,2,65536]{2,1,0:T(2,128)(2,1)}), bf16[8,2,65536]{2,1,0:T(2,128)(2,1)S(1)}, u32[]{:S(2)}, u32[]{:S(2)}) async-start(bf16[8,2,65536]{2,1,0:T(2,128)(2,1)} %reshape.346), calls=%async_computation | async-start | bytes 4194304 | tf_op jit(solution)/shard_map/all_to_all | solution.py:138
  174.7 11.3 %copy-start = (bf16[8,2,65536]{2,1,0:T(2,128)(2,1)}, bf16[8,2,65536]{2,1,0:T(2,128)(2,1)S(1)}, u32[]{:S(2)}) copy-start(bf16[8,2,65536]{2,1,0:T(2,128)(2,1)S(1)} %all-to-all-done) | copy-start | bytes 6291460
  174.7 30.2 %all-to-all-start.3 = ((bf16[1024,8,1,128]{3,1,2,0:T(8,128)(2,1)}), bf16[1024,8,1,128]{3,1,2,0:T(8,128)(2,1)}, u32[]{:S(2)}, u32[]{:S(2)}) async-start(bf16[1024,8,1,128]{3,1,2,0:T(8,128)(2,1)} %copy.94), calls=%async_computation.3 | async-start | bytes 4194304 | tf_op jit(solution)/shard_map/all_to_all | solution.py:124
  188.5 21.2 %copy-start.5 = (bf16[3,7,512]{2,1,0:T(8,128)(2,1)S(1)}, bf16[3,7,512]{2,1,0:T(8,128)(2,1)}, u32[]{:S(2)}) copy-start(bf16[3,7,512]{2,1,0:T(8,128)(2,1)} %param.12) | copy-start | bytes 64516
  191.1 24.0 %copy-start.24 = (s32[16]{0:T(128)S(1)}, s32[16]{0:T(128)}, u32[]{:S(2)}) copy-start(s32[16]{0:T(128)} %param.15) | copy-start | bytes 196
  205.0 30.2 %all-to-all-start.5 = ((bf16[1024,8,1,128]{3,1,2,0:T(8,128)(2,1)}), bf16[1024,8,1,128]{3,1,2,0:T(8,128)(2,1)}, u32[]{:S(2)}, u32[]{:S(2)}) async-start(bf16[1024,8,1,128]{3,1,2,0:T(8,128)(2,1)} %copy.98), calls=%async_computation.5 | async-start | bytes 4194304 | tf_op jit(solution)/shard_map/all_to_all | solution.py:150
  215.1 5.3 %copy-start.1 = (bf16[8,2,65536]{2,1,0:T(2,128)(2,1)S(1)}, bf16[8,2,65536]{2,1,0:T(2,128)(2,1)}, u32[]{:S(2)}) copy-start(bf16[8,2,65536]{2,1,0:T(2,128)(2,1)} %copy-done) | copy-start | bytes 6291460
  217.4 2.8 copy-start.25
  234.4 9.8 %copy-start.9 = (f32[1,1,256]{2,1,0:T(1,128)S(1)}, f32[1,1,256]{2,1,0:T(1,128)}, u32[]{:S(2)}) copy-start(f32[1,1,256]{2,1,0:T(1,128)} %get-tuple-element.167) | copy-start | bytes 3076
  234.4 9.8 %copy-start.10 = (f32[1,1,256]{2,1,0:T(1,128)S(1)}, f32[1,1,256]{2,1,0:T(1,128)}, u32[]{:S(2)}) copy-start(f32[1,1,256]{2,1,0:T(1,128)} %get-tuple-element.168) | copy-start | bytes 3076
  234.4 9.8 %copy-start.11 = (f32[1,1,256]{2,1,0:T(1,128)S(1)}, f32[1,1,256]{2,1,0:T(1,128)}, u32[]{:S(2)}) copy-start(f32[1,1,256]{2,1,0:T(1,128)} %get-tuple-element.169) | copy-start | bytes 3076
  234.4 9.8 %copy-start.12 = (f32[1,1,256]{2,1,0:T(1,128)S(1)}, f32[1,1,256]{2,1,0:T(1,128)}, u32[]{:S(2)}) copy-start(f32[1,1,256]{2,1,0:T(1,128)} %get-tuple-element.170) | copy-start | bytes 3076
  234.4 9.8 %copy-start.13 = (f32[1,1,256]{2,1,0:T(1,128)S(1)}, f32[1,1,256]{2,1,0:T(1,128)}, u32[]{:S(2)}) copy-start(f32[1,1,256]{2,1,0:T(1,128)} %get-tuple-element.171) | copy-start | bytes 3076
  234.4 9.8 %copy-start.14 = (f32[1,1,256]{2,1,0:T(1,128)S(1)}, f32[1,1,256]{2,1,0:T(1,128)}, u32[]{:S(2)}) copy-start(f32[1,1,256]{2,1,0:T(1,128)} %get-tuple-element.172) | copy-start | bytes 3076
  234.4 9.8 %copy-start.15 = (f32[1,1,256]{2,1,0:T(1,128)S(1)}, f32[1,1,256]{2,1,0:T(1,128)}, u32[]{:S(2)}) copy-start(f32[1,1,256]{2,1,0:T(1,128)} %get-tuple-element.173) | copy-start | bytes 3076
  234.4 9.8 %copy-start.16 = (f32[1,1,256]{2,1,0:T(1,128)S(1)}, f32[1,1,256]{2,1,0:T(1,128)}, u32[]{:S(2)}) copy-start(f32[1,1,256]{2,1,0:T(1,128)} %get-tuple-element.174) | copy-start | bytes 3076
  234.4 9.8 %copy-start.17 = (f32[1,1,256]{2,1,0:T(1,128)S(1)}, f32[1,1,256]{2,1,0:T(1,128)}, u32[]{:S(2)}) copy-start(f32[1,1,256]{2,1,0:T(1,128)} %get-tuple-element.175) | copy-start | bytes 3076
  234.4 9.8 %copy-start.18 = (f32[1,1,256]{2,1,0:T(1,128)S(1)}, f32[1,1,256]{2,1,0:T(1,128)}, u32[]{:S(2)}) copy-start(f32[1,1,256]{2,1,0:T(1,128)} %get-tuple-element.176) | copy-start | bytes 3076
  234.4 9.8 %copy-start.19 = (f32[1,1,256]{2,1,0:T(1,128)S(1)}, f32[1,1,256]{2,1,0:T(1,128)}, u32[]{:S(2)}) copy-start(f32[1,1,256]{2,1,0:T(1,128)} %get-tuple-element.177) | copy-start | bytes 3076
  234.5 9.8 %copy-start.20 = (f32[1,1,256]{2,1,0:T(1,128)S(1)}, f32[1,1,256]{2,1,0:T(1,128)}, u32[]{:S(2)}) copy-start(f32[1,1,256]{2,1,0:T(1,128)} %get-tuple-element.178) | copy-start | bytes 3076
  234.5 9.8 %copy-start.21 = (f32[1,1,256]{2,1,0:T(1,128)S(1)}, f32[1,1,256]{2,1,0:T(1,128)}, u32[]{:S(2)}) copy-start(f32[1,1,256]{2,1,0:T(1,128)} %get-tuple-element.179) | copy-start | bytes 3076
  234.5 9.8 %copy-start.22 = (f32[1,1,256]{2,1,0:T(1,128)S(1)}, f32[1,1,256]{2,1,0:T(1,128)}, u32[]{:S(2)}) copy-start(f32[1,1,256]{2,1,0:T(1,128)} %get-tuple-element.186) | copy-start | bytes 3076
  235.2 115.6 %all-to-all-start.1 = ((bf16[1024,8,1,128]{3,1,2,0:T(8,128)(2,1)}), bf16[1024,8,1,128]{3,1,2,0:T(8,128)(2,1)}, u32[]{:S(2)}, u32[]{:S(2)}) async-start(bf16[1024,8,1,128]{3,1,2,0:T(8,128)(2,1)} %copy.90), calls=%async_computation.1 | async-start | bytes 4194304 | tf_op jit(solution)/shard_map/all_to_all | solution.py:137
  275.0 2.7 copy-start.4
  350.8 4.3 %copy-start.6 = (f32[1,1,256]{2,1,0:T(1,128)S(1)}, f32[1,1,256]{2,1,0:T(1,128)}, u32[]{:S(2)}) copy-start(f32[1,1,256]{2,1,0:T(1,128)} %get-tuple-element.183) | copy-start | bytes 3076
  350.8 4.3 %copy-start.7 = (f32[1,1,256]{2,1,0:T(1,128)S(1)}, f32[1,1,256]{2,1,0:T(1,128)}, u32[]{:S(2)}) copy-start(f32[1,1,256]{2,1,0:T(1,128)} %get-tuple-element.184) | copy-start | bytes 3076
  350.8 4.3 %copy-start.8 = (f32[1,1,256]{2,1,0:T(1,128)S(1)}, f32[1,1,256]{2,1,0:T(1,128)}, u32[]{:S(2)}) copy-start(f32[1,1,256]{2,1,0:T(1,128)} %get-tuple-element.185) | copy-start | bytes 3076
  350.8 4.3 %copy-start.23 = (f32[256]{0:T(256)S(1)}, f32[256]{0:T(256)}, u32[]{:S(2)}) copy-start(f32[256]{0:T(256)} %dynamic_slice.25) | copy-start | bytes 3076
where the time goes:
time: 376 us; the launch traced here: 373 us
  local copies, waits for them, and re-layouts  153 us (41%)
  waiting for transfers between devices  119 us (32%)
  other arithmetic  56.3 us (15%)
  starting transfers between devices  28.3 us (8%)
  matrix products  15.9 us (4%)
    unnamed x69, local copies, waits for them, and re-layouts  71.6 us
    all_to_all x1, waiting for transfers between devices, on_device(): lax.all_to_all(second_stream.T.reshape(channels, 1, 1, row_count), 'ctx',...  36.4 us
    all_to_all x1, waiting for transfers between devices, on_device(): lax.all_to_all(value_stream.T.reshape(channels, 1, 1, row_count), 'ctx',...  34 us
    all_to_all x1, waiting for transfers between devices, on_device(): lax.all_to_all(first_stream.T.reshape(channels, 1, 1, row_count), 'ctx',...  33.9 us
    convert_element_type x1, other arithmetic, featurize_cols(): (first_feature * value_feature).astype(jnp.bfloat16)  20.7 us
    mul x4, local copies, waits for them, and re-layouts, one_step(): weights = toeplitz[None] * keep_mask[..., None]  17.4 us
    dot_general x4, matrix products, one_step(): jnp.einsum('btsu,umbs->umbt', weights, block_rows, preferred_element_type...  15.9 us
    convert_element_type x1, other arithmetic, channel_mix_cols(): return gated.astype(jnp.bfloat16)  14.1 us
  transfers between devices with their start and end apart: 6, of which 5 were waited for; matrix products, arithmetic and copies ran while one was open for 50% of the time, Pallas kernels for 0%

commit v1 on v0

v1 whole, which is shorter than its diff:
```python
import functools

import jax
import jax.numpy as jnp
from jax import lax
from jax.experimental import pallas as pl
from jax.experimental.pallas import tpu as pltpu
from jax.sharding import PartitionSpec as P

AXES = ("ctx", "tp")
GROUP = 16
LANES = 128
HALO = 8
PARTS = (1, 3)


def begins_of(position, lengths_ref):
    begin = jnp.zeros_like(position)
    start = jnp.int32(0)
    for segment in range(lengths_ref.shape[0]):
        begin = jnp.where(position >= start, start, begin)
        start = start + lengths_ref[segment]
    return begin


def feature_kernel(
    cuts, own_count, place_ref, lengths_ref, first_ref, second_ref, value_ref, rim_ref, taps_ref, *rest
):
    out_count = len(cuts) - 1
    mixed_refs, gate_refs = rest[:out_count], rest[out_count : 2 * out_count]
    keep_ref, spread_ref, tap_ref, padded_ref = rest[2 * out_count :]
    rows, tile = first_ref.shape
    streams, tap_count = taps_ref.shape[:2]
    groups = tile // GROUP

    @pl.when(pl.program_id(0) == 0)
    def _():
        position = lax.broadcasted_iota(jnp.int32, (rows, LANES), 0) + place_ref[0]
        offset = position - begins_of(position, lengths_ref)
        for tap in range(1, tap_count):
            keep_ref[tap - 1] = jnp.where(offset >= tap, 1.0, 0.0)
        group = lax.broadcasted_iota(jnp.int32, (groups, tile), 0)
        channel = lax.broadcasted_iota(jnp.int32, (groups, tile), 1)
        spread_ref[...] = jnp.where(channel // GROUP == group, 1.0, 0.0).astype(jnp.bfloat16)

    for stream in range(streams):
        tap_ref[stream, :tap_count] = jnp.dot(
            taps_ref[stream], spread_ref[...], preferred_element_type=jnp.float32
        )

    strip = 16

    def column(lanes):
        for stream, ref in enumerate((first_ref, second_ref, value_ref)):
            padded_ref[stream, :HALO] = rim_ref[stream, :, lanes].astype(jnp.float32)
            padded_ref[stream, HALO:] = ref[:, lanes].astype(jnp.float32)
        mixed, gate = [], []
        for row in range(0, rows, strip):
            features = []
            for stream in range(streams):
                total = None
                for tap in range(tap_count):
                    term = (
                        tap_ref[stream, tap : tap + 1, lanes]
                        * padded_ref[stream, pl.ds(HALO + row - tap, strip)]
                    )
                    if tap == 0:
                        total = term
                    else:
                        total = total + keep_ref[tap - 1, pl.ds(row, strip)] * term
                features.append(total)
            mixed.append((features[0] * features[2]).astype(jnp.bfloat16))
            gate.append(features[1].astype(jnp.bfloat16))
        return jnp.concatenate(mixed, 0).T, jnp.concatenate(gate, 0).T

    block = max(own_count, LANES)

    def one_block(index, _):
        for part in range(block // LANES):
            lanes = pl.ds(pl.multiple_of(index * block + part * LANES, LANES), LANES)
            for value, refs in zip(column(lanes), (mixed_refs, gate_refs)):
                for owner in range(block // own_count):
                    for which in range(out_count):
                        low = max(owner * own_count + cuts[which], part * LANES)
                        high = min(owner * own_count + cuts[which + 1], part * LANES + LANES)
                        if low < high:
                            at = low - owner * own_count - cuts[which]
                            refs[which][
                                index * (block // own_count) + owner, at : at + high - low
                            ] = value[low - part * LANES : high - part * LANES]
        return 0

    lax.fori_loop(0, tile // block, one_block, 0)


def features(place, lengths, first, second, value, rim, taps, cuts, own_count):
    rows, channels = first.shape
    owners = channels // own_count
    tile = min(2048, channels)
    per = tile // own_count
    stream_spec = pl.BlockSpec((rows, tile), lambda i: (0, i))
    shapes = [
        jax.ShapeDtypeStruct((owners, cuts[n + 1] - cuts[n], rows), jnp.bfloat16)
        for n in range(len(cuts) - 1)
    ] * 2
    specs = [pl.BlockSpec((per, shape.shape[1], rows), lambda i: (i, 0, 0)) for shape in shapes]
    streams, tap_count = taps.shape[:2]
    outs = pl.pallas_call(
        functools.partial(feature_kernel, cuts, own_count),
        grid=(channels // tile,),
        in_specs=[
            pl.BlockSpec(memory_space=pltpu.SMEM),
            pl.BlockSpec(memory_space=pltpu.SMEM),
            stream_spec,
            stream_spec,
            stream_spec,
            pl.BlockSpec((streams, HALO, tile), lambda i: (0, 0, i)),
            pl.BlockSpec((streams, tap_count, tile // GROUP), lambda i: (0, 0, i)),
        ],
        out_specs=specs,
        out_shape=shapes,
        scratch_shapes=[
            pltpu.VMEM((tap_count - 1, rows, LANES), jnp.float32),
            pltpu.VMEM((tile // GROUP, tile), jnp.bfloat16),
            pltpu.VMEM((streams, 8, tile), jnp.float32),
            pltpu.VMEM((streams, HALO + rows, LANES), jnp.float32),
        ],
        compiler_params=pltpu.CompilerParams(vmem_limit_bytes=40 << 20),
        name="features",
    )(place, lengths, first, second, value, rim, taps)
    return outs[: len(cuts) - 1], outs[len(cuts) - 1 :]


def convolve_kernel(
    first_group, group_stride, place_ref, lengths_ref, mixed_ref, rim_ref, gate_ref, filter_ref, skip_ref,
    out_ref, keep_ref, taps_ref
):
    owners, count, rows = mixed_ref.shape
    length = filter_ref.shape[0]
    step = pl.program_id(0)

    @pl.when(step == 0)
    def _():
        source = lax.broadcasted_iota(jnp.int32, (rows, rows), 0)
        target = lax.broadcasted_iota(jnp.int32, (rows, rows), 1)
        position = target + place_ref[0]
        offset = position - begins_of(position, lengths_ref)
        own_lag = target - source
        rim_lag = own_lag + rows
        keep_ref[:rows] = jnp.where(
            (rim_lag < length) & (rim_lag <= offset), 1.0, 0.0
        ).astype(jnp.bfloat16)
        keep_ref[rows:] = jnp.where(
            (own_lag >= 0) & (own_lag <= offset), 1.0, 0.0
        ).astype(jnp.bfloat16)
        taps_ref[...] = filter_ref[...].astype(jnp.float32).T

    def one_owner(owner, _):
        skip_row = skip_ref[owner]
        gains = []
        for low in range(0, skip_row.shape[1], LANES):
            piece = skip_row[:, low : low + LANES]
            gains.append(jnp.broadcast_to(piece, (rows, piece.shape[1])).T)
        gain = jnp.concatenate(gains, 0) if len(gains) > 1 else gains[0]
        for unit in range(count // GROUP):
            members = pl.ds(unit * GROUP, GROUP)
            group = (step * owners + owner) * group_stride + first_group + unit
            row = jnp.broadcast_to(taps_ref[pl.ds(group, 1)], (GROUP, length))
            base = pltpu.roll(row, 0, 1, stride=1, stride_axis=0)
            strips = [base.astype(jnp.bfloat16)]
            for shift in range(GROUP, length, GROUP):
                strips.append(pltpu.roll(base, shift, 1).astype(jnp.bfloat16))
            circulant = jnp.concatenate(strips, 0)
            weights = jnp.concatenate([circulant, circulant], 0) * keep_ref[...]
            own = mixed_ref[owner, members]
            window = jnp.concatenate([rim_ref[owner, members], own], 1)
            total = jnp.dot(window, weights, preferred_element_type=jnp.float32)
            place = first_group * GROUP + unit * GROUP
            total = total + gain[place : place + GROUP] * own.astype(jnp.float32)
            total = total * gate_ref[owner, members].astype(jnp.float32)
            out_ref[owner, members] = total.astype(jnp.bfloat16)
        return 0

    lax.fori_loop(0, owners, one_owner, 0)


def convolve(place, lengths, mixed, rim, gate, long_filter, skip_gain, first_channel, own_count):
    owners, count, rows = mixed.shape
    steps = min(4, owners)
    per = owners // steps
    part_spec = pl.BlockSpec((per, count, rows), lambda i: (i, 0, 0))
    return pl.pallas_call(
        functools.partial(convolve_kernel, first_channel // GROUP, own_count // GROUP),
        grid=(steps,),
        in_specs=[
            pl.BlockSpec(memory_space=pltpu.SMEM),
            pl.BlockSpec(memory_space=pltpu.SMEM),
            part_spec,
            part_spec,
            part_spec,
            pl.BlockSpec(long_filter.shape, lambda i: (0, 0)),
            pl.BlockSpec((per, 1, own_count), lambda i: (i, 0, 0)),
        ],
        out_specs=part_spec,
        out_shape=jax.ShapeDtypeStruct(mixed.shape, jnp.bfloat16),
        scratch_shapes=[
            pltpu.VMEM((2 * rows, rows), jnp.bfloat16),
            pltpu.VMEM(long_filter.shape[::-1], jnp.float32),
        ],
        compiler_params=pltpu.CompilerParams(vmem_limit_bytes=40 << 20),
        name="convolve",
    )(place, lengths, mixed, rim, gate, long_filter, skip_gain.reshape(owners, 1, own_count))


def place_kernel(part_ref, *rest):
    out_ref = rest[-1]
    owners, _, rows = part_ref.shape
    for owner in range(owners):
        out_ref[:, owner * rows : (owner + 1) * rows] = part_ref[owner]


def place_rows(part, whole, first_row, own_count):
    owners, count, rows = part.shape
    strip = 16
    given = () if whole is None else (whole,)
    return pl.pallas_call(
        place_kernel,
        grid=(count // strip,),
        in_specs=[pl.BlockSpec((owners, strip, rows), lambda i: (0, i, 0))]
        + [pl.BlockSpec(memory_space=pl.ANY)] * len(given),
        out_specs=pl.BlockSpec((strip, owners * rows), lambda i: (first_row // strip + i, 0)),
        out_shape=jax.ShapeDtypeStruct((own_count, owners * rows), jnp.bfloat16),
        input_output_aliases={1: 0} if given else {},
        compiler_params=pltpu.CompilerParams(vmem_limit_bytes=40 << 20),
        name="place_rows",
    )(part, *given)


def on_device(first, second, value, short_filter, long_filter, skip_gain, lengths):
    rows, channels = first.shape
    devices = lax.axis_size(AXES)
    own_count = channels // devices
    place = jnp.reshape(lax.axis_index(AXES) * rows, (1,)).astype(jnp.int32)
    following = [(source, source + 1) for source in range(devices - 1)]
    unit_count = own_count // GROUP
    cuts, seen = [0], 0
    for weight in PARTS:
        seen += weight
        cuts.append(unit_count * seen // sum(PARTS) * GROUP)
    cuts = sorted(set(cuts))
    last = jnp.stack([stream[rows - HALO :] for stream in (first, second, value)])
    rim = lax.ppermute(last, AXES, following)
    mixed, gate = features(
        place, lengths, first, second, value, rim, short_filter, tuple(cuts), own_count
    )
    rims = [lax.ppermute(part, AXES, following) for part in mixed]
    whole = None
    for index, low in enumerate(cuts[:-1]):
        part = convolve(
            place, lengths, mixed[index], rims[index], gate[index], long_filter, skip_gain, low, own_count
        )
        got = lax.all_to_all(part, AXES, 0, 0, tiled=True)
        whole = place_rows(got, whole, low, own_count)
    return whole


def solution(mesh):
    tokens = P(AXES, None)
    return jax.shard_map(
        on_device,
        mesh=mesh,
        in_specs=(tokens, tokens, tokens, P(), P(), P(), P()),
        out_specs=tokens,
        check_vma=False,
    )
```

time: 376 us -> 146 us (0.39)
  local copies, waits for them, and re-layouts: 153 us -> 10.6 us
  waiting for transfers between devices: 119 us -> 39 us
  other arithmetic: 56.3 us -> 0.05 us
  Pallas kernels: 0 us -> 47.3 us
  starting transfers between devices: 28.3 us -> 48.6 us
  matrix products: 15.9 us -> 0 us
    all_to_all x6 -> x2, waiting for transfers between devices: 119 us -> 36.3 us  [on_device(): got = lax.all_to_all(part, AXES, 0, 0, tiled=True)]
    unnamed x69 -> x20, local copies, waits for them, and re-layouts: 71.6 us -> 8.71 us
    pallas_call x0 -> x5, Pallas kernels: none -> 47.3 us  [the longest x2 25.6 us: convolve(): pl.pallas_call(functools.partial(convolve_kernel, first_channel // GROUP,...]
    convert_element_type x7 -> x0, other arithmetic: 39.5 us -> none  [the longest x1 20.7 us: featurize_cols(): (first_feature * value_feature).astype(jnp.bfloat16)]
    all_to_all x6 -> x0, local copies, waits for them, and re-layouts: 20.9 us -> none  [the longest x1 4.32 us: on_device(): lax.all_to_all(lax.all_to_all(first_stream.T.reshape(channels, 1, 1, row_...]
    mul x4 -> x0, local copies, waits for them, and re-layouts: 17.4 us -> none  [one_step(): weights = toeplitz[None] * keep_mask[..., None]]
    dot_general x4 -> x0, matrix products: 15.9 us -> none  [one_step(): jnp.einsum('btsu,umbs->umbt', weights, block_rows, preferred_element_type...]
    ppermute x0 -> x3, starting transfers between devices: none -> 14.8 us  [the longest x2 12.4 us: on_device(): rims = [lax.ppermute(part, AXES, following) for part in mixed]]
  transfers between devices with their start and end apart: 6 -> 5, of which waited for: 5 -> 3; matrix products, arithmetic and copies ran while one was open for 50% -> 0% of each run, Pallas kernels for 0% -> 19%
where the time goes in v1:
time: 146 us
  starting transfers between devices  48.6 us (33%)
  Pallas kernels  47.3 us (32%)
  waiting for transfers between devices  39 us (27%)
  local copies, waits for them, and re-layouts  10.6 us (7%)
    all_to_all x2, waiting for transfers between devices, on_device(): got = lax.all_to_all(part, AXES, 0, 0, tiled=True)  36.3 us
    all_to_all x2, starting transfers between devices, on_device(): got = lax.all_to_all(part, AXES, 0, 0, tiled=True)  33.8 us
    pallas_call x2, Pallas kernels, convolve(): pl.pallas_call(functools.partial(convolve_kernel, first_channel // GROUP,...  25.6 us
    pallas_call x1, Pallas kernels, features(): pl.pallas_call(functools.partial(feature_kernel, cuts, own_count), grid=(...  16 us
    ppermute x2, starting transfers between devices, on_device(): rims = [lax.ppermute(part, AXES, following) for part in mixed]  12.4 us
    unnamed x20, local copies, waits for them, and re-layouts  8.71 us
    pallas_call x2, Pallas kernels, place_rows(): pl.pallas_call(place_kernel, grid=(count // strip,), in_specs=[pl.BlockSp...  5.73 us
  transfers between devices with their start and end apart: 5, of which 3 were waited for; matrix products, arithmetic and copies ran while one was open for 0% of the time, Pallas kernels for 19%

profile of v1, /device:TPU:0, one launch (start us, length us, event | category | flops | bytes accessed | tf_op | source)
XLA Modules:
  0.0 145.7 jit_solution(2505267674565435261)
XLA Ops:
  0.0 0.9 slice_bitcast_fusion.2
  0.9 1.0 slice_bitcast_fusion
  2.0 2.4 %collective-permute-start = (bf16[3,8,8192]{2,1,0:T(8,128)(2,1)S(1)}, bf16[3,8,8192]{2,1,0:T(8,128)(2,1)S(1)}, u32[]{:S(2)}, u32[]{:S(2)}) collective-permute-start(bf16[3,8,8192]{2,1,0:T(8,128)(2,1)S(1)} %pad_maximum_fusion), channel_id=1, source_target_pairs={{0,1},{1,2},{2,3},{3,4},{4,5},{5,6},{6,7},{7,8},{8,9},{9,10},{10,1... | collective-permute-start | bytes 1179656 | tf_op jit(solution)/shard_map/ppermute | solution.py:252
  4.4 1.3 collective-permute-done.rim_ref
  5.7 0.0 copy-start
  5.7 1.6 %copy-done = bf16[128,8192]{1,0:T(8,128)(2,1)S(1)} copy-done((bf16[128,8192]{1,0:T(8,128)(2,1)S(1)}, bf16[128,8192]{1,0:T(8,128)(2,1)}, u32[]{:S(2)}) %copy-start) | copy-done | bytes 2097176
  7.3 0.0 copy-start.1
  7.3 1.6 %copy-done.1 = bf16[128,8192]{1,0:T(8,128)(2,1)S(1)} copy-done((bf16[128,8192]{1,0:T(8,128)(2,1)S(1)}, bf16[128,8192]{1,0:T(8,128)(2,1)}, u32[]{:S(2)}) %copy-start.1) | copy-done | bytes 2097176
  8.8 0.0 copy-start.2
  8.8 1.6 %copy-done.2 = bf16[128,8192]{1,0:T(8,128)(2,1)S(1)} copy-done((bf16[128,8192]{1,0:T(8,128)(2,1)S(1)}, bf16[128,8192]{1,0:T(8,128)(2,1)}, u32[]{:S(2)}) %copy-start.2) | copy-done | bytes 2097176
  10.4 0.0 copy-start.7
  10.4 0.7 copy-done.7
  11.2 0.0 copy-start.8
  11.2 0.7 copy-done.8
  11.8 0.0 copy-start.5
  11.8 0.0 copy-start.6
  11.8 16.0 %features.1 = (bf16[32,64,128]{2,1,0:T(8,128)(2,1)S(1)}, bf16[32,192,128]{2,1,0:T(8,128)(2,1)S(1)}, bf16[32,64,128]{2,1,0:T(8,128)(2,1)S(1)}, bf16[32,192,128]{2,1,0:T(8,128)(2,1)S(1)}) custom-call(s32[1]{0:T(128)} %bitcast.place_ref, s32[16]{0:T(128)S(1)} %copy-done.8, bf16[128,8192]{1,0:T(8,128)(2,1)S(1)} %copy-done, bf16[128,8192]{1,0:T(8,128)(2,1)S(1)} %copy-done.1, ...), custom_call_target="tpu_custom_call" | custom-call | tf_op jit(solution)/shard_map/features/pallas_call | solution.py:108
  27.8 0.0 copy-start.3
  27.8 1.1 copy-done.3
  29.0 0.0 copy-start.9
  29.0 9.2 %collective-permute-start.1 = (bf16[32,192,128]{2,1,0:T(8,128)(2,1)S(1)}, bf16[32,192,128]{2,1,0:T(8,128)(2,1)}, u32[]{:S(2)}, u32[]{:S(2)}) collective-permute-start(bf16[32,192,128]{2,1,0:T(8,128)(2,1)S(1)} %get-tuple-element.9.mixed_ref), channel_id=1, source_target_pairs={{0,1},{1,2},{2,3},{3,4},{4,5},{5,6},{6,7},{7,8},{8,9},{9,10},{10,1... | collective-permute-start | bytes 4718600 | tf_op jit(solution)/shard_map/ppermute | solution.py:256
  38.2 3.2 %collective-permute-start.2 = (bf16[32,64,128]{2,1,0:T(8,128)(2,1)S(1)}, bf16[32,64,128]{2,1,0:T(8,128)(2,1)S(1)}, u32[]{:S(2)}, u32[]{:S(2)}) collective-permute-start(bf16[32,64,128]{2,1,0:T(8,128)(2,1)S(1)} %get-tuple-element.11.mixed_ref), channel_id=1, source_target_pairs={{0,1},{1,2},{2,3},{3,4},{4,5},{5,6},{6,7},{7,8},{8,9},{9,10},{10,1... | collective-permute-start | bytes 1572872 | tf_op jit(solution)/shard_map/ppermute | solution.py:256
  41.4 1.5 %collective-permute-done.2.rim_ref = bf16[32,64,128]{2,1,0:T(8,128)(2,1)S(1)} collective-permute-done((bf16[32,64,128]{2,1,0:T(8,128)(2,1)S(1)}, bf16[32,64,128]{2,1,0:T(8,128)(2,1)S(1)}, u32[]{:S(2)}, u32[]{:S(2)}) %collective-permute-start.2) | collective-permute-done | bytes 524320 | tf_op jit(solution)/shard_map/ppermute | solution.py:256
  42.9 0.0 copy-done.5
  42.9 0.0 copy-done.6
  42.9 10.9 %convolve.3 = bf16[32,64,128]{2,1,0:T(8,128)(2,1)} custom-call(s32[1]{0:T(128)} %bitcast.place_ref, s32[16]{0:T(128)S(1)} %copy-done.8, bf16[32,64,128]{2,1,0:T(8,128)(2,1)S(1)} %get-tuple-element.11.mixed_ref, bf16[32,64,128]{2,1,0:T(8,128)(2,1)S(1)} %collective-permute-done.2.rim_ref, bf16[32,64,128]{2,1,0:T(8,128)(2,1)S(1)} %get-tuple-element.12.gate_ref, ...), custom_call_target="tpu_custom_call" | custom-call | tf_op jit(solution)/shard_map/convolve/pallas_call | solution.py:192
  53.8 28.0 %all-to-all-start.1 = ((bf16[32,64,128]{2,1,0:T(8,128)(2,1)}), bf16[32,64,128]{2,1,0:T(8,128)(2,1)S(1)}, u32[]{:S(2)}, u32[]{:S(2)}) async-start(bf16[32,64,128]{2,1,0:T(8,128)(2,1)} %convolve.3), calls=%async_computation.1 | async-start | bytes 1048576 | tf_op jit(solution)/shard_map/all_to_all | solution.py:262
  81.7 0.0 collective-permute-done.1.rim_ref
  81.7 0.0 copy-done.9
  81.8 0.0 copy-start.4
  81.8 1.4 copy-done.4
  83.2 14.7 %convolve.2 = bf16[32,192,128]{2,1,0:T(8,128)(2,1)} custom-call(s32[1]{0:T(128)} %bitcast.place_ref, s32[16]{0:T(128)S(1)} %copy-done.9, bf16[32,192,128]{2,1,0:T(8,128)(2,1)S(1)} %get-tuple-element.9.mixed_ref, bf16[32,192,128]{2,1,0:T(8,128)(2,1)} %collective-permute-done.1.rim_ref, bf16[32,192,128]{2,1,0:T(8,128)(2,1)S(1)} %copy-done.4, ...), custom_call_target="tpu_custom_call" | custom-call | tf_op jit(solution)/shard_map/convolve/pallas_call | solution.py:192
  97.9 0.0 all-to-all-done.1.part_ref
  97.9 5.8 %all-to-all-start = ((bf16[32,192,128]{2,1,0:T(8,128)(2,1)}), bf16[32,192,128]{2,1,0:T(8,128)(2,1)S(1)}, u32[]{:S(2)}, u32[]{:S(2)}) async-start(bf16[32,192,128]{2,1,0:T(8,128)(2,1)} %convolve.2), calls=%async_computation | async-start | bytes 3145728 | tf_op jit(solution)/shard_map/all_to_all | solution.py:262
  103.7 1.5 %place_rows.2.rest_0_ = bf16[256,4096]{1,0:T(8,128)(2,1)} custom-call(bf16[32,64,128]{2,1,0:T(8,128)(2,1)S(1)} %all-to-all-done.1.part_ref), custom_call_target="tpu_custom_call" | custom-call | tf_op jit(solution)/shard_map/place_rows/pallas_call | solution.py:226
  105.2 36.3 %all-to-all-done.part_ref = bf16[32,192,128]{2,1,0:T(8,128)(2,1)S(1)} async-done(((bf16[32,192,128]{2,1,0:T(8,128)(2,1)}), bf16[32,192,128]{2,1,0:T(8,128)(2,1)S(1)}, u32[]{:S(2)}, u32[]{:S(2)}) %all-to-all-start) | async-done | bytes 1572896 | tf_op jit(solution)/shard_map/all_to_all | solution.py:262
  141.5 4.2 %place_rows.3 = bf16[256,4096]{1,0:T(8,128)(2,1)} custom-call(bf16[32,192,128]{2,1,0:T(8,128)(2,1)S(1)} %all-to-all-done.part_ref, bf16[256,4096]{1,0:T(8,128)(2,1)} %place_rows.2.rest_0_), custom_call_target="tpu_custom_call", output_to_operand_aliasing={{}: (1, {})} | custom-call | tf_op jit(solution)/shard_map/place_rows/pallas_call | solution.py:226
  (1 shorter events, 0.0 us)
Async XLA Ops:
  2.0 3.7 %collective-permute-start = (bf16[3,8,8192]{2,1,0:T(8,128)(2,1)S(1)}, bf16[3,8,8192]{2,1,0:T(8,128)(2,1)S(1)}, u32[]{:S(2)}, u32[]{:S(2)}) collective-permute-start(bf16[3,8,8192]{2,1,0:T(8,128)(2,1)S(1)} %pad_maximum_fusion), channel_id=1, source_target_pairs={{0,1},{1,2},{2,3},{3,4},{4,5},{5,6},{6,7},{7,8},{8,9},{9,10},{10,1... | collective-permute-start | bytes 1179656 | tf_op jit(solution)/shard_map/ppermute | solution.py:252
  5.7 1.6 %copy-start = (bf16[128,8192]{1,0:T(8,128)(2,1)S(1)}, bf16[128,8192]{1,0:T(8,128)(2,1)}, u32[]{:S(2)}) copy-start(bf16[128,8192]{1,0:T(8,128)(2,1)} %first_ref.1) | copy-start | bytes 6291460
  7.3 1.6 %copy-start.1 = (bf16[128,8192]{1,0:T(8,128)(2,1)S(1)}, bf16[128,8192]{1,0:T(8,128)(2,1)}, u32[]{:S(2)}) copy-start(bf16[128,8192]{1,0:T(8,128)(2,1)} %second_ref.1) | copy-start | bytes 6291460
  8.8 1.6 %copy-start.2 = (bf16[128,8192]{1,0:T(8,128)(2,1)S(1)}, bf16[128,8192]{1,0:T(8,128)(2,1)}, u32[]{:S(2)}) copy-start(bf16[128,8192]{1,0:T(8,128)(2,1)} %value_ref.1) | copy-start | bytes 6291460
  10.4 0.7 copy-start.7
  11.2 0.7 copy-start.8
  11.8 31.1 %copy-start.5 = (bf16[128,512]{1,0:T(8,128)(2,1)S(1)}, bf16[128,512]{1,0:T(8,128)(2,1)}, u32[]{:S(2)}) copy-start(bf16[128,512]{1,0:T(8,128)(2,1)} %filter_ref.3) | copy-start | bytes 393220
  11.8 31.1 %copy-start.6 = (f32[8192]{0:T(1024)S(1)}, f32[8192]{0:T(1024)}, u32[]{:S(2)}) copy-start(f32[8192]{0:T(1024)} %param.12) | copy-start | bytes 98308
  27.8 1.1 copy-start.3
  29.0 52.8 %copy-start.9 = (s32[16]{0:T(128)S(1)}, s32[16]{0:T(128)}, u32[]{:S(2)}) copy-start(s32[16]{0:T(128)} %lengths_ref.5) | copy-start | bytes 196
  29.0 52.8 %collective-permute-start.1 = (bf16[32,192,128]{2,1,0:T(8,128)(2,1)S(1)}, bf16[32,192,128]{2,1,0:T(8,128)(2,1)}, u32[]{:S(2)}, u32[]{:S(2)}) collective-permute-start(bf16[32,192,128]{2,1,0:T(8,128)(2,1)S(1)} %get-tuple-element.9.mixed_ref), channel_id=1, source_target_pairs={{0,1},{1,2},{2,3},{3,4},{4,5},{5,6},{6,7},{7,8},{8,9},{9,10},{10,1... | collective-permute-start | bytes 4718600 | tf_op jit(solution)/shard_map/ppermute | solution.py:256
  38.2 4.7 %collective-permute-start.2 = (bf16[32,64,128]{2,1,0:T(8,128)(2,1)S(1)}, bf16[32,64,128]{2,1,0:T(8,128)(2,1)S(1)}, u32[]{:S(2)}, u32[]{:S(2)}) collective-permute-start(bf16[32,64,128]{2,1,0:T(8,128)(2,1)S(1)} %get-tuple-element.11.mixed_ref), channel_id=1, source_target_pairs={{0,1},{1,2},{2,3},{3,4},{4,5},{5,6},{6,7},{7,8},{8,9},{9,10},{10,1... | collective-permute-start | bytes 1572872 | tf_op jit(solution)/shard_map/ppermute | solution.py:256
  53.8 44.1 %all-to-all-start.1 = ((bf16[32,64,128]{2,1,0:T(8,128)(2,1)}), bf16[32,64,128]{2,1,0:T(8,128)(2,1)S(1)}, u32[]{:S(2)}, u32[]{:S(2)}) async-start(bf16[32,64,128]{2,1,0:T(8,128)(2,1)} %convolve.3), calls=%async_computation.1 | async-start | bytes 1048576 | tf_op jit(solution)/shard_map/all_to_all | solution.py:262
  81.8 1.4 copy-start.4
  97.9 43.6 %all-to-all-start = ((bf16[32,192,128]{2,1,0:T(8,128)(2,1)}), bf16[32,192,128]{2,1,0:T(8,128)(2,1)S(1)}, u32[]{:S(2)}, u32[]{:S(2)}) async-start(bf16[32,192,128]{2,1,0:T(8,128)(2,1)} %convolve.2), calls=%async_computation | async-start | bytes 3145728 | tf_op jit(solution)/shard_map/all_to_all | solution.py:262

commit v2 on v1

v2 whole, which is shorter than its diff:
```python
import functools

import jax
import jax.numpy as jnp
from jax import lax
from jax.experimental import pallas as pl
from jax.experimental.pallas import tpu as pltpu
from jax.sharding import PartitionSpec as P

AXES = ("ctx", "tp")
GROUP = 16
LANES = 128
HALO = 8
FIRST_PART = 64
VMEM_LIMIT = 58 << 20


def begins_of(position, lengths_ref):
    begin = jnp.zeros_like(position)
    start = jnp.int32(0)
    for segment in range(lengths_ref.shape[0]):
        begin = jnp.where(position >= start, start, begin)
        start = start + lengths_ref[segment]
    return begin


def moves_of(block, own_count, columns, cuts, carried=0):
    moves = []
    for owner in range(block // own_count):
        sizes = [carried] + [0] * (len(cuts) - 2)
        for column in columns:
            for part in range(len(cuts) - 1):
                base = column * LANES
                low = max(owner * own_count + cuts[part], base)
                high = min(owner * own_count + cuts[part + 1], base + LANES)
                if low < high:
                    moves.append((column, low - base, high - base, owner, part, sizes[part]))
                    sizes[part] += high - low
    return moves, sizes


def prepare_kernel(
    block, moves, place_ref, lengths_ref, short_ref, long_ref, skip_ref,
    short_keep_ref, long_keep_ref, long_taps_ref, short_taps_ref, *rest
):
    gain_refs, spread_ref = rest[:-1], rest[-1]
    streams, tap_count, groups = short_ref.shape
    length = long_ref.shape[0]
    rows = long_keep_ref.shape[1]
    tile = skip_ref.shape[1]

    @pl.when(pl.program_id(0) == 0)
    def _():
        position = lax.broadcasted_iota(jnp.int32, (rows, LANES), 0) + place_ref[0]
        offset = position - begins_of(position, lengths_ref)
        for tap in range(1, tap_count):
            short_keep_ref[tap - 1] = jnp.where(offset >= tap, 1.0, 0.0)
        source = lax.broadcasted_iota(jnp.int32, (rows, rows), 0)
        target = lax.broadcasted_iota(jnp.int32, (rows, rows), 1)
        position = target + place_ref[0]
        offset = position - begins_of(position, lengths_ref)
        own_lag = target - source
        rim_lag = own_lag + rows
        rim_keep = (rim_lag < length) & (rim_lag <= offset)
        own_keep = (own_lag >= 0) & (own_lag <= offset)
        long_keep_ref[:rows] = jnp.where(rim_keep, 1.0, 0.0).astype(jnp.bfloat16)
        long_keep_ref[rows:] = jnp.where(own_keep, 1.0, 0.0).astype(jnp.bfloat16)
        long_taps_ref[...] = long_ref[...].astype(jnp.float32).T
        group = lax.broadcasted_iota(jnp.int32, spread_ref.shape, 0)
        channel = lax.broadcasted_iota(jnp.int32, spread_ref.shape, 1)
        spread_ref[...] = jnp.where(channel // GROUP == group, 1.0, 0.0).astype(jnp.bfloat16)

    for stream in range(streams):
        short_taps_ref[stream, :tap_count] = jnp.dot(
            short_ref[stream], spread_ref[...], preferred_element_type=jnp.float32
        )

    def one_block(index, _):
        for part in sorted({move[0] for move in moves}):
            lanes = pl.ds(pl.multiple_of(index * block + part * LANES, LANES), LANES)
            gain = jnp.broadcast_to(skip_ref[:, lanes], (rows, LANES)).T
            for column, low, high, owner, which, row in moves:
                if column == part:
                    per = gain_refs[which].shape[0] * block // tile
                    gain_refs[which][index * per + owner, row : row + high - low] = gain[low:high]
        return 0

    lax.fori_loop(0, tile // block, one_block, 0)


def prepare(place, lengths, short_filter, long_filter, skip_gain, own_count, rows, cuts):
    channels = skip_gain.shape[0]
    owners = channels // own_count
    tile = min(2048, channels)
    block = max(own_count, LANES)
    streams, tap_count, groups = short_filter.shape
    moves, sizes = moves_of(block, own_count, range(block // LANES), cuts)
    whole = lambda *shape: pl.BlockSpec(shape, lambda i: (0,) * len(shape))
    shape = jax.ShapeDtypeStruct
    short_keep, long_keep, *rest = pl.pallas_call(
        functools.partial(prepare_kernel, block, tuple(moves)),
        grid=(channels // tile,),
        in_specs=[pl.BlockSpec(memory_space=pltpu.SMEM)] * 2
        + [
            pl.BlockSpec((streams, tap_count, tile // GROUP), lambda i: (0, 0, i)),
            whole(*long_filter.shape),
            pl.BlockSpec((1, tile), lambda i: (0, i)),
        ],
        out_specs=[
            whole(tap_count - 1, rows, LANES),
            whole(2 * rows, rows),
            whole(*long_filter.shape[::-1]),
            pl.BlockSpec((streams, 8, tile), lambda i: (0, 0, i)),
        ]
        + [pl.BlockSpec((tile // own_count, size, rows), lambda i: (i, 0, 0)) for size in sizes],
        out_shape=[
            shape((tap_count - 1, rows, LANES), jnp.float32),
            shape((2 * rows, rows), jnp.bfloat16),
            shape(long_filter.shape[::-1], jnp.float32),
            shape((streams, 8, channels), jnp.float32),
        ]
        + [shape((owners, size, rows), jnp.float32) for size in sizes],
        scratch_shapes=[pltpu.VMEM((tile // GROUP, tile), jnp.bfloat16)],
        cost_estimate=pl.CostEstimate(flops=1 << 28, bytes_accessed=12 << 20, transcendentals=0),
        compiler_params=pltpu.CompilerParams(vmem_limit_bytes=VMEM_LIMIT),
        name="prepare",
    )(place, lengths, short_filter, long_filter, skip_gain.reshape(1, channels))
    return short_keep, long_keep, *rest


def last_kernel(*refs):
    for index, ref in enumerate(refs[:-1]):
        refs[-1][index] = ref[...][-HALO:]


def last_rows(streams):
    rows, channels = streams[0].shape
    tile = channels
    return pl.pallas_call(
        last_kernel,
        grid=(channels // tile,),
        in_specs=[pl.BlockSpec((16, tile), lambda i: (rows // 16 - 1, i))] * len(streams),
        out_specs=pl.BlockSpec((len(streams), HALO, tile), lambda i: (0, 0, i)),
        out_shape=jax.ShapeDtypeStruct((len(streams), HALO, channels), jnp.bfloat16),
        compiler_params=pltpu.CompilerParams(vmem_limit_bytes=VMEM_LIMIT),
        name="last_rows",
    )(*streams)


def feature_kernel(block, chosen, tap_count, moves, carried, *refs):
    count = len(chosen)
    stream_refs, (rim_ref, taps_ref, keep_ref), refs = refs[:count], refs[count : count + 3], refs[count + 3 :]
    carry_ref, refs = (refs[0], refs[1:]) if carried else (None, refs)
    out_refs, padded_ref = refs[:-1], refs[-1]
    rows, tile = stream_refs[0].shape
    strip = 16

    if carried:
        out_refs[0][:, : carry_ref.shape[1]] = carry_ref[...]

    def column(lanes, slot):
        for stream, ref in enumerate(stream_refs):
            padded_ref[slot, stream, :HALO] = rim_ref[chosen[stream], :, lanes].astype(jnp.float32)
            padded_ref[slot, stream, HALO:] = ref[:, lanes].astype(jnp.float32)
        results = []
        for row in range(0, rows, strip):
            product = None
            for stream in range(count):
                tap_of = lambda tap: taps_ref[chosen[stream], tap : tap + 1, lanes]
                total = tap_of(0) * padded_ref[slot, stream, pl.ds(HALO + row, strip)]
                for tap in range(1, tap_count):
                    term = tap_of(tap) * padded_ref[slot, stream, pl.ds(HALO + row - tap, strip)]
                    total = total + keep_ref[tap - 1, pl.ds(row, strip)] * term
                product = total if product is None else product * total
            results.append(product.astype(jnp.bfloat16))
        return jnp.concatenate(results, 0).T

    def one_block(index, _):
        for slot, part in enumerate(sorted({move[0] for move in moves})):
            lanes = pl.ds(pl.multiple_of(index * block + part * LANES, LANES), LANES)
            value = column(lanes, slot % padded_ref.shape[0])
            for move, low, high, owner, which, row in moves:
                if move == part:
                    per = out_refs[which].shape[0] * block // tile
                    out_refs[which][index * per + owner, row : row + high - low] = value[low:high]
        return 0

    lax.fori_loop(0, tile // block, one_block, 0)


def features(streams, chosen, rim, taps, keep, own_count, columns, cuts, carry=None):
    rows, channels = streams[0].shape
    owners = channels // own_count
    tile = min(2048, channels)
    block = max(own_count, LANES)
    given = [] if carry is None else [carry]
    moves, sizes = moves_of(block, own_count, columns, cuts, sum(part.shape[1] for part in given))
    part_spec = lambda size: pl.BlockSpec((tile // own_count, size, rows), lambda i: (i, 0, 0))
    count, tap_count = len(chosen), keep.shape[0] + 1
    return pl.pallas_call(
        functools.partial(feature_kernel, block, chosen, tap_count, tuple(moves), carry is not None),
        grid=(channels // tile,),
        in_specs=[pl.BlockSpec((rows, tile), lambda i: (0, i))] * count
        + [pl.BlockSpec((*part.shape[:2], tile), lambda i: (0, 0, i)) for part in (rim, taps)]
        + [pl.BlockSpec(keep.shape, lambda i: (0, 0, 0))]
        + [part_spec(part.shape[1]) for part in given],
        out_specs=[part_spec(size) for size in sizes],
        out_shape=[jax.ShapeDtypeStruct((owners, size, rows), jnp.bfloat16) for size in sizes],
        scratch_shapes=[pltpu.VMEM((2, count, HALO + rows, LANES), jnp.float32)],
        cost_estimate=pl.CostEstimate(flops=1 << 27, bytes_accessed=12 << 20, transcendentals=0),
        compiler_params=pltpu.CompilerParams(vmem_limit_bytes=VMEM_LIMIT),
        name="features",
    )(*[streams[stream] for stream in chosen], rim, taps, keep, *given)


def convolve_kernel(
    first_group, group_stride, mixed_ref, rim_ref, gate_ref, gain_ref, taps_ref, keep_ref, out_ref
):
    owners, count, rows = mixed_ref.shape
    length = taps_ref.shape[1]
    first_owner = pl.program_id(0) * owners

    def one_owner(owner, _):
        for unit in range(count // GROUP):
            members = pl.ds(unit * GROUP, GROUP)
            group = (first_owner + owner) * group_stride + first_group + unit
            row = jnp.broadcast_to(taps_ref[pl.ds(group, 1)], (GROUP, length))
            base = pltpu.roll(row, 0, 1, stride=1, stride_axis=0).astype(jnp.bfloat16)
            strips = [base] + [pltpu.roll(base, shift, 1) for shift in range(GROUP, length, GROUP)]
            circulant = jnp.concatenate(strips, 0)
            weights = jnp.concatenate([circulant, circulant], 0) * keep_ref[...]
            own = mixed_ref[owner, members]
            window = jnp.concatenate([rim_ref[owner, members], own], 1)
            total = jnp.dot(window, weights, preferred_element_type=jnp.float32)
            total = total + gain_ref[owner, members] * own.astype(jnp.float32)
            total = total * gate_ref[owner, members].astype(jnp.float32)
            out_ref[owner, members] = total.astype(jnp.bfloat16)
        return 0

    together = max(1, min(owners, 32 * GROUP // count))
    lax.fori_loop(0, owners, one_owner, 0, unroll=together)


def convolve(mixed, rim, gate, gain, taps, keep, first_channel, own_count):
    owners, count, rows = mixed.shape
    steps = 2 if count * 2 <= own_count else 4
    part_spec = pl.BlockSpec((owners // steps, count, rows), lambda i: (i, 0, 0))
    return pl.pallas_call(
        functools.partial(convolve_kernel, first_channel // GROUP, own_count // GROUP),
        grid=(steps,),
        in_specs=[part_spec] * 4 + [pl.BlockSpec(part.shape, lambda i: (0, 0)) for part in (taps, keep)],
        out_specs=part_spec,
        out_shape=jax.ShapeDtypeStruct(mixed.shape, jnp.bfloat16),
        cost_estimate=pl.CostEstimate(flops=1 << 28, bytes_accessed=12 << 20, transcendentals=0),
        compiler_params=pltpu.CompilerParams(vmem_limit_bytes=VMEM_LIMIT),
        name="convolve",
    )(mixed, rim, gate, gain, taps, keep)


def on_device(first, second, value, short_filter, long_filter, skip_gain, lengths):
    rows, channels = first.shape
    devices = lax.axis_size(AXES)
    own_count = channels // devices
    place = jnp.reshape(lax.axis_index(AXES) * rows, (1,)).astype(jnp.int32)
    following = [(source, source + 1) for source in range(devices - 1)]
    streams = (first, second, value)
    cuts = (0, FIRST_PART, own_count) if own_count > LANES else (0, own_count)
    last, lengths = lax.optimization_barrier((last_rows(streams), lengths))
    rim = lax.ppermute(last, AXES, following)
    short_keep, long_keep, long_taps, short_taps, *gains = prepare(
        place, lengths, short_filter, long_filter, skip_gain, own_count, rows, cuts
    )
    everything = tuple(range(max(own_count, LANES) // LANES))
    feature = lambda chosen, columns, cuts, carry=None: features(
        streams, chosen, rim, short_taps, short_keep, own_count, columns, cuts, carry
    )
    mix = lambda mixed, rims, gate, part: convolve(
        mixed, rims, gate, gains[part], long_taps, long_keep, cuts[part], own_count
    )
    relay = lambda part: lax.all_to_all(part, AXES, 0, 0, tiled=True)
    as_rows = lambda part: part.transpose(1, 0, 2).reshape(part.shape[1], -1)
    if own_count <= LANES:
        (mixed,) = feature((0, 2), everything, cuts)
        rims = lax.ppermute(mixed, AXES, following)
        (gate,) = feature((1,), everything, cuts)
        return as_rows(relay(mix(mixed, rims, gate, 0)))

    low_mixed, carry = feature((0, 2), everything[:1], cuts)
    low_rims = lax.ppermute(low_mixed, AXES, following)
    (high_mixed,) = feature((0, 2), everything[1:], cuts[1:], carry)
    low_gate, high_gate = feature((1,), everything, cuts)
    high_mixed, low_rims = lax.optimization_barrier((high_mixed, low_rims))
    high_rims = lax.ppermute(high_mixed, AXES, following)
    low = relay(mix(low_mixed, low_rims, low_gate, 0))
    high = relay(mix(high_mixed, high_rims, high_gate, 1))
    return jnp.concatenate([as_rows(low), as_rows(high)], 0)


def solution(mesh):
    tokens = P(AXES, None)
    return jax.shard_map(
        on_device,
        mesh=mesh,
        in_specs=(tokens, tokens, tokens, P(), P(), P(), P()),
        out_specs=tokens,
        check_vma=False,
    )
```

time: 146 us -> 116 us (0.79)
  starting transfers between devices: 48.6 us -> 22.2 us
  local copies, waits for them, and re-layouts: 10.6 us -> 2.23 us
  Pallas kernels: 47.3 us -> 49.5 us
    all_to_all x2, starting transfers between devices: 33.8 us -> 13.2 us  [on_device(): relay = lambda part: lax.all_to_all(part, AXES, 0, 0, tiled=True)]
    pallas_call x3 -> x5, Pallas kernels: 21.7 us -> 32.9 us  [the longest x3 23.8 us: features(): pl.pallas_call(functools.partial(feature_kernel, block, chosen, tap_count...]
    pallas_call x2, Pallas kernels: 25.6 us -> 16.7 us  [convolve(): pl.pallas_call(functools.partial(convolve_kernel, first_channel // GROUP,...]
    unnamed x20 -> x6, local copies, waits for them, and re-layouts: 8.71 us -> 1.94 us
    ppermute x2, starting transfers between devices: 12.4 us -> 6.67 us  [the longest x1 4.51 us: on_device(): low_rims = lax.ppermute(low_mixed, AXES, following)]
    all_to_all x2, waiting for transfers between devices: 36.3 us -> 40.4 us  [on_device(): relay = lambda part: lax.all_to_all(part, AXES, 0, 0, tiled=True)]
    another operation x2 -> x0, local copies, waits for them, and re-layouts: 1.9 us -> none  [on_device(): jnp.stack([stream[rows - HALO:] for stream in (first, second, value)])]
    ppermute x2, waiting for transfers between devices: 1.49 us -> 0.01 us  [the longest x1 0.01 us: on_device(): low_rims = lax.ppermute(low_mixed, AXES, following)]
  transfers between devices with their start and end apart: 5 -> 5, of which waited for: 3 -> 2; matrix products, arithmetic and copies ran while one was open for 0% -> 0% of each run, Pallas kernels for 19% -> 34%
where the time goes in v2:
time: 116 us
  Pallas kernels  49.5 us (43%)
  waiting for transfers between devices  40.4 us (35%)
  starting transfers between devices  22.2 us (19%)
  local copies, waits for them, and re-layouts  2.23 us (2%)
  other arithmetic  1.46 us (1%)
    all_to_all x2, waiting for transfers between devices, on_device(): relay = lambda part: lax.all_to_all(part, AXES, 0, 0, tiled=True)  40.4 us
    pallas_call x3, Pallas kernels, features(): pl.pallas_call(functools.partial(feature_kernel, block, chosen, tap_count...  23.8 us
    pallas_call x2, Pallas kernels, convolve(): pl.pallas_call(functools.partial(convolve_kernel, first_channel // GROUP,...  16.7 us
    all_to_all x2, starting transfers between devices, on_device(): relay = lambda part: lax.all_to_all(part, AXES, 0, 0, tiled=True)  13.2 us
    pallas_call x1, Pallas kernels, prepare(): pl.pallas_call(functools.partial(prepare_kernel, block, tuple(moves)), gr...  7.18 us
    ppermute x1, starting transfers between devices, on_device(): low_rims = lax.ppermute(low_mixed, AXES, following)  4.51 us
    ppermute x1, starting transfers between devices, on_device(): rim = lax.ppermute(last, AXES, following)  2.37 us
  transfers between devices with their start and end apart: 5, of which 2 were waited for; matrix products, arithmetic and copies ran while one was open for 0% of the time, Pallas kernels for 34%

profile of v2, /device:TPU:0, one launch (start us, length us, event | category | flops | bytes accessed | tf_op | source)
XLA Modules:
  0.0 115.9 jit_solution(785370884090327200)
XLA Ops:
  0.0 1.9 %last_rows.1 = bf16[3,8,8192]{2,1,0:T(8,128)(2,1)} custom-call(bf16[128,8192]{1,0:T(8,128)(2,1)} %refs_0_.6, bf16[128,8192]{1,0:T(8,128)(2,1)} %refs_0_.7, bf16[128,8192]{1,0:T(8,128)(2,1)} %refs_1_.5), custom_call_target="tpu_custom_call" | custom-call | tf_op jit(solution)/shard_map/last_rows/pallas_call | solution.py:139
  1.9 2.4 %collective-permute-start = (bf16[3,8,8192]{2,1,0:T(8,128)(2,1)}, bf16[3,8,8192]{2,1,0:T(8,128)(2,1)S(1)}, u32[]{:S(2)}, u32[]{:S(2)}) collective-permute-start(bf16[3,8,8192]{2,1,0:T(8,128)(2,1)} %last_rows.1), channel_id=1, source_target_pairs={{0,1},{1,2},{2,3},{3,4},{4,5},{5,6},{6,7},{7,8},{8,9},{9,10},{10,1... | collective-permute-start | bytes 1179656 | tf_op jit(solution)/shard_map/ppermute | solution.py:269
  4.3 7.2 %prepare.1 = (f32[6,128,128]{2,1,0:T(8,128)}, bf16[256,128]{1,0:T(8,128)(2,1)}, f32[512,128]{1,0:T(8,128)}, f32[3,8,8192]{2,1,0:T(8,128)}, f32[32,64,128]{2,1,0:T(8,128)}, /*index=5*/f32[32,192,128]{2,1,0:T(8,128)}) custom-call(s32[1]{0:T(128)} %bitcast.place_ref, s32[16]{0:T(128)} %lengths_ref, bf16[3,7,512]{2,1,0:T(8,128)(2,1)} %short_ref.1, ...), custom_call_target="tpu_custom_call" | custom-call | flops 268435456 | bytes 12582912 | tf_op jit(solution)/shard_map/prepare/pallas_call | solution.py:100
  11.4 0.0 collective-permute-done.refs_2_.refs_1_
  11.5 0.0 copy-start
  11.5 0.8 copy-done
  12.2 7.9 %features.3 = (bf16[32,64,128]{2,1,0:T(8,128)(2,1)}, bf16[32,64,128]{2,1,0:T(8,128)(2,1)}) custom-call(bf16[128,8192]{1,0:T(8,128)(2,1)} %refs_0_.6, bf16[128,8192]{1,0:T(8,128)(2,1)} %refs_1_.5, bf16[3,8,8192]{2,1,0:T(8,128)(2,1)} %copy-done, f32[3,8,8192]{2,1,0:T(8,128)} %get-tuple-element.21.refs_3_.refs_2_, f32[6,128,128]{2,1,0:T(8,128)} %get-tuple-element.22.refs_4_.refs_3_), custom_call_target="tpu_custom_call" | custom-call | flops 134217728 | bytes 12582912 | tf_op jit(solution)/shard_map/features/pallas_call | solution.py:200
  20.2 4.5 %collective-permute-start.1 = (bf16[32,64,128]{2,1,0:T(8,128)(2,1)}, bf16[32,64,128]{2,1,0:T(8,128)(2,1)S(1)}, u32[]{:S(2)}, u32[]{:S(2)}) collective-permute-start(bf16[32,64,128]{2,1,0:T(8,128)(2,1)} %get-tuple-element.23.mixed_ref), channel_id=1, source_target_pairs={{0,1},{1,2},{2,3},{3,4},{4,5},{5,6},{6,7},{7,8},{8,9},{9,10},{10,1... | collective-permute-start | bytes 1572872 | tf_op jit(solution)/shard_map/ppermute | solution.py:289
  24.7 8.2 %features.4.mixed_ref = bf16[32,192,128]{2,1,0:T(8,128)(2,1)} custom-call(bf16[128,8192]{1,0:T(8,128)(2,1)} %refs_0_.6, bf16[128,8192]{1,0:T(8,128)(2,1)} %refs_1_.5, bf16[3,8,8192]{2,1,0:T(8,128)(2,1)} %copy-done, f32[3,8,8192]{2,1,0:T(8,128)} %get-tuple-element.21.refs_3_.refs_2_, f32[6,128,128]{2,1,0:T(8,128)} %get-tuple-element.22.refs_4_.refs_3_, ...), custom_call_target="tpu_custom_call" | custom-call | flops 134217728 | bytes 12582912 | tf_op jit(solution)/shard_map/features/pallas_call | solution.py:200
  32.9 0.0 collective-permute-done.1.rim_ref
  32.9 0.0 copy-start.2
  32.9 2.2 %collective-permute-start.2 = (bf16[32,192,128]{2,1,0:T(8,128)(2,1)}, bf16[32,192,128]{2,1,0:T(8,128)(2,1)S(1)}, u32[]{:S(2)}, u32[]{:S(2)}) collective-permute-start(bf16[32,192,128]{2,1,0:T(8,128)(2,1)} %features.4.mixed_ref), channel_id=1, source_target_pairs={{0,1},{1,2},{2,3},{3,4},{4,5},{5,6},{6,7},{7,8},{8,9},{9,10},{10,1... | collective-permute-start | bytes 4718600 | tf_op jit(solution)/shard_map/ppermute | solution.py:293
  35.1 7.6 %features.5 = (bf16[32,64,128]{2,1,0:T(8,128)(2,1)}, bf16[32,192,128]{2,1,0:T(8,128)(2,1)}) custom-call(bf16[128,8192]{1,0:T(8,128)(2,1)} %refs_0_.7, bf16[3,8,8192]{2,1,0:T(8,128)(2,1)} %copy-done, f32[3,8,8192]{2,1,0:T(8,128)} %get-tuple-element.21.refs_3_.refs_2_, f32[6,128,128]{2,1,0:T(8,128)} %get-tuple-element.22.refs_4_.refs_3_), custom_call_target="tpu_custom_call" | custom-call | flops 134217728 | bytes 12582912 | tf_op jit(solution)/shard_map/features/pallas_call | solution.py:200
  42.7 0.0 copy-done.2
  42.7 5.0 %convolve.2 = bf16[32,64,128]{2,1,0:T(8,128)(2,1)} custom-call(bf16[32,64,128]{2,1,0:T(8,128)(2,1)} %get-tuple-element.23.mixed_ref, bf16[32,64,128]{2,1,0:T(8,128)(2,1)} %copy-done.2, bf16[32,64,128]{2,1,0:T(8,128)(2,1)} %get-tuple-element.26.gate_ref, f32[32,64,128]{2,1,0:T(8,128)} %get-tuple-element.27.gain_ref, f32[512,128]{1,0:T(8,128)} %get-tuple-element.28.taps_ref, ...), custom_call_target="tpu_custom_call" | custom-call | flops 268435456 | bytes 12582912 | tf_op jit(solution)/shard_map/convolve/pallas_call | solution.py:248
  47.7 8.5 %all-to-all-start = ((bf16[32,64,128]{2,1,0:T(8,128)(2,1)}), bf16[32,64,128]{2,1,0:T(8,128)(2,1)S(1)}, u32[]{:S(2)}, u32[]{:S(2)}) async-start(bf16[32,64,128]{2,1,0:T(8,128)(2,1)} %convolve.2), calls=%async_computation | async-start | bytes 1048576 | tf_op jit(solution)/shard_map/all_to_all | solution.py:280
  56.2 0.0 collective-permute-done.2.rim_ref
  56.2 0.0 copy-start.1
  56.2 1.1 copy-done.1
  57.4 11.7 %convolve.3 = bf16[32,192,128]{2,1,0:T(8,128)(2,1)} custom-call(bf16[32,192,128]{2,1,0:T(8,128)(2,1)} %features.4.mixed_ref, bf16[32,192,128]{2,1,0:T(8,128)(2,1)} %copy-done.1, bf16[32,192,128]{2,1,0:T(8,128)(2,1)} %get-tuple-element.31.gate_ref, f32[32,192,128]{2,1,0:T(8,128)} %get-tuple-element.32.gain_ref, f32[512,128]{1,0:T(8,128)} %get-tuple-element.28.taps_ref, ...), custom_call_target="tpu_custom_call" | custom-call | flops 268435456 | bytes 12582912 | tf_op jit(solution)/shard_map/convolve/pallas_call | solution.py:248
  69.0 2.7 %all-to-all-done = bf16[32,64,128]{2,1,0:T(8,128)(2,1)S(1)} async-done(((bf16[32,64,128]{2,1,0:T(8,128)(2,1)}), bf16[32,64,128]{2,1,0:T(8,128)(2,1)S(1)}, u32[]{:S(2)}, u32[]{:S(2)}) %all-to-all-start) | async-done | bytes 524320 | tf_op jit(solution)/shard_map/all_to_all | solution.py:280
  71.8 4.7 %all-to-all-start.1 = ((bf16[32,192,128]{2,1,0:T(8,128)(2,1)}), bf16[32,192,128]{2,1,0:T(8,128)(2,1)S(1)}, u32[]{:S(2)}, u32[]{:S(2)}) async-start(bf16[32,192,128]{2,1,0:T(8,128)(2,1)} %convolve.3), calls=%async_computation.1 | async-start | bytes 3145728 | tf_op jit(solution)/shard_map/all_to_all | solution.py:280
  76.5 0.1 copy_bitcast_fusion.1
  76.5 37.7 %all-to-all-done.1 = bf16[32,192,128]{2,1,0:T(8,128)(2,1)S(1)} async-done(((bf16[32,192,128]{2,1,0:T(8,128)(2,1)}), bf16[32,192,128]{2,1,0:T(8,128)(2,1)S(1)}, u32[]{:S(2)}, u32[]{:S(2)}) %all-to-all-start.1) | async-done | bytes 1572896 | tf_op jit(solution)/shard_map/all_to_all | solution.py:280
  114.2 0.2 copy_bitcast_fusion
  114.4 1.5 %pad_maximum_fusion = bf16[256,4096]{1,0:T(8,128)(2,1)} fusion(bf16[192,4096]{1,0:T(8,128)(2,1)S(1)} %copy_bitcast_fusion, bf16[64,4096]{1,0:T(8,128)(2,1)S(1)} %copy_bitcast_fusion.1), kind=kLoop, calls=%fused_computation | loop fusion | flops 4194304 | bytes 4194304 | tf_op jit(solution)/shard_map/concatenate | solution.py:296
Async XLA Ops:
  1.9 9.6 %collective-permute-start = (bf16[3,8,8192]{2,1,0:T(8,128)(2,1)}, bf16[3,8,8192]{2,1,0:T(8,128)(2,1)S(1)}, u32[]{:S(2)}, u32[]{:S(2)}) collective-permute-start(bf16[3,8,8192]{2,1,0:T(8,128)(2,1)} %last_rows.1), channel_id=1, source_target_pairs={{0,1},{1,2},{2,3},{3,4},{4,5},{5,6},{6,7},{7,8},{8,9},{9,10},{10,1... | collective-permute-start | bytes 1179656 | tf_op jit(solution)/shard_map/ppermute | solution.py:269
  11.5 0.8 copy-start
  20.2 12.8 %collective-permute-start.1 = (bf16[32,64,128]{2,1,0:T(8,128)(2,1)}, bf16[32,64,128]{2,1,0:T(8,128)(2,1)S(1)}, u32[]{:S(2)}, u32[]{:S(2)}) collective-permute-start(bf16[32,64,128]{2,1,0:T(8,128)(2,1)} %get-tuple-element.23.mixed_ref), channel_id=1, source_target_pairs={{0,1},{1,2},{2,3},{3,4},{4,5},{5,6},{6,7},{7,8},{8,9},{9,10},{10,1... | collective-permute-start | bytes 1572872 | tf_op jit(solution)/shard_map/ppermute | solution.py:289
  32.9 9.8 %copy-start.2 = (bf16[32,64,128]{2,1,0:T(8,128)(2,1)}, bf16[32,64,128]{2,1,0:T(8,128)(2,1)S(1)}, u32[]{:S(2)}) copy-start(bf16[32,64,128]{2,1,0:T(8,128)(2,1)S(1)} %collective-permute-done.1.rim_ref) | copy-start | bytes 1572868
  32.9 23.3 %collective-permute-start.2 = (bf16[32,192,128]{2,1,0:T(8,128)(2,1)}, bf16[32,192,128]{2,1,0:T(8,128)(2,1)S(1)}, u32[]{:S(2)}, u32[]{:S(2)}) collective-permute-start(bf16[32,192,128]{2,1,0:T(8,128)(2,1)} %features.4.mixed_ref), channel_id=1, source_target_pairs={{0,1},{1,2},{2,3},{3,4},{4,5},{5,6},{6,7},{7,8},{8,9},{9,10},{10,1... | collective-permute-start | bytes 4718600 | tf_op jit(solution)/shard_map/ppermute | solution.py:293
  47.7 24.0 %all-to-all-start = ((bf16[32,64,128]{2,1,0:T(8,128)(2,1)}), bf16[32,64,128]{2,1,0:T(8,128)(2,1)S(1)}, u32[]{:S(2)}, u32[]{:S(2)}) async-start(bf16[32,64,128]{2,1,0:T(8,128)(2,1)} %convolve.2), calls=%async_computation | async-start | bytes 1048576 | tf_op jit(solution)/shard_map/all_to_all | solution.py:280
  56.2 1.1 copy-start.1
  71.8 42.4 %all-to-all-start.1 = ((bf16[32,192,128]{2,1,0:T(8,128)(2,1)}), bf16[32,192,128]{2,1,0:T(8,128)(2,1)S(1)}, u32[]{:S(2)}, u32[]{:S(2)}) async-start(bf16[32,192,128]{2,1,0:T(8,128)(2,1)} %convolve.3), calls=%async_computation.1 | async-start | bytes 3145728 | tf_op jit(solution)/shard_map/all_to_all | solution.py:280

commit v3 on v2

v3 whole, which is shorter than its diff:
```python
import functools

import jax
import jax.numpy as jnp
from jax import lax
from jax.experimental import pallas as pl
from jax.experimental.pallas import tpu as pltpu
from jax.sharding import PartitionSpec as P

AXES = ("ctx", "tp")
GROUP = 16
LANES = 128
HALO = 8
CUTS = (0, 96, 256)
VMEM_LIMIT = 24 << 20


def begins_of(position, lengths_ref):
    begin = jnp.zeros_like(position)
    start = jnp.int32(0)
    for segment in range(lengths_ref.shape[0]):
        begin = jnp.where(position >= start, start, begin)
        start = start + lengths_ref[segment]
    return begin


def prepare_kernel(
    tile, place_ref, lengths_ref, short_ref, long_ref, first_ref, second_ref, value_ref,
    short_keep_ref, long_keep_ref, long_taps_ref, short_taps_ref, near_ref, spread_ref, arrived
):
    streams, tap_count, groups = short_ref.shape
    length = long_ref.shape[0]
    rows = long_keep_ref.shape[1]
    copies = [
        pltpu.make_async_copy(ref, near_ref.at[index], arrived.at[index])
        for index, ref in enumerate((first_ref, second_ref, value_ref))
    ]
    for copy in copies:
        copy.start()
    position = lax.broadcasted_iota(jnp.int32, (rows, LANES), 0) + place_ref[0]
    offset = position - begins_of(position, lengths_ref)
    for tap in range(1, tap_count):
        short_keep_ref[tap - 1] = jnp.where(offset >= tap, 1.0, 0.0)
    source = lax.broadcasted_iota(jnp.int32, (rows, rows), 0)
    target = lax.broadcasted_iota(jnp.int32, (rows, rows), 1)
    position = target[:8] + place_ref[0]
    offset = (position - begins_of(position, lengths_ref))[:1]
    own_lag = target - source
    rim_lag = own_lag + rows
    rim_keep = (rim_lag < length) & (rim_lag <= offset)
    own_keep = (own_lag >= 0) & (own_lag <= offset)
    long_keep_ref[:rows] = jnp.where(rim_keep, 1.0, 0.0).astype(jnp.bfloat16)
    long_keep_ref[rows:] = jnp.where(own_keep, 1.0, 0.0).astype(jnp.bfloat16)
    long_taps_ref[...] = long_ref[...].astype(jnp.float32).T
    group = lax.broadcasted_iota(jnp.int32, spread_ref.shape, 0)
    channel = lax.broadcasted_iota(jnp.int32, spread_ref.shape, 1)
    spread_ref[...] = jnp.where(channel // GROUP == group, 1.0, 0.0).astype(jnp.bfloat16)
    for stream in range(streams):
        for part in range(groups * GROUP // tile):
            taps = short_ref[stream, :, part * tile // GROUP : (part + 1) * tile // GROUP]
            short_taps_ref[stream, :tap_count, part * tile : (part + 1) * tile] = jnp.dot(
                taps, spread_ref[...], preferred_element_type=jnp.float32
            )
    for copy in copies:
        copy.wait()


def near(*arrays):
    return [pltpu.with_memory_space_constraint(array, pltpu.VMEM) for array in arrays]


def far(*arrays):
    return [pltpu.with_memory_space_constraint(array, pltpu.HBM) for array in arrays]


VMEM_SPEC = pl.BlockSpec(memory_space=pltpu.VMEM)
SMEM_SPEC = pl.BlockSpec(memory_space=pltpu.SMEM)


def prepare(place, lengths, short_filter, long_filter, streams):
    count, tap_count, groups = short_filter.shape
    rows, channels = streams[0].shape
    tile = min(2048, channels)
    return pl.pallas_call(
        functools.partial(prepare_kernel, tile),
        in_specs=[SMEM_SPEC] * 2 + [VMEM_SPEC] * 2 + [pl.BlockSpec(memory_space=pltpu.HBM)] * count,
        out_specs=[VMEM_SPEC] * 5,
        out_shape=[
            pltpu.VMEM((tap_count - 1, rows, LANES), jnp.float32),
            pltpu.VMEM((2 * rows, rows), jnp.bfloat16),
            pltpu.VMEM(long_filter.shape[::-1], jnp.float32),
            pltpu.VMEM((count, 8, channels), jnp.float32),
            pltpu.VMEM((count, rows, channels), jnp.bfloat16),
        ],
        scratch_shapes=[
            pltpu.VMEM((tile // GROUP, tile), jnp.bfloat16),
            pltpu.SemaphoreType.DMA((count,)),
        ],
        cost_estimate=pl.CostEstimate(flops=1 << 10, bytes_accessed=1 << 10, transcendentals=0),
        compiler_params=pltpu.CompilerParams(vmem_limit_bytes=VMEM_LIMIT),
        name="prepare",
    )(place, lengths, short_filter, long_filter, *far(*streams))


def last_kernel(*refs):
    for index, ref in enumerate(refs[:-1]):
        refs[-1][index] = ref[...][-HALO:]


def last_rows(streams):
    rows, channels = streams[0].shape
    return pl.pallas_call(
        last_kernel,
        grid=(1,),
        in_specs=[pl.BlockSpec((16, channels), lambda i: (rows // 16 - 1, 0))] * len(streams),
        out_specs=pl.BlockSpec((len(streams), HALO, channels), lambda i: (0, 0, 0)),
        out_shape=jax.ShapeDtypeStruct((len(streams), HALO, channels), jnp.bfloat16),
        compiler_params=pltpu.CompilerParams(vmem_limit_bytes=VMEM_LIMIT),
        name="last_rows",
    )(*far(*streams))


def gathered(owners, own_count, low, high):
    whole, parts = [], []
    for owner in range(owners):
        at = low
        while at < high:
            start = owner * own_count + at
            end = min(start // LANES * LANES + LANES, owner * own_count + high)
            piece = (owner, at, at + end - start)
            (whole if end - start == LANES else parts).append(piece)
            at += end - start
    columns, column, room = [], [], LANES
    for owner, first, last in parts:
        while first < last:
            size = min(room, last - first)
            column.append((owner, first, first + size))
            first, room = first + size, room - size
            if room == 0:
                columns.append(column)
                column, room = [], LANES
    return columns + [[piece] for piece in whole]


def feature_kernel(products, tap_count, own_count, low, columns, *refs):
    chosen = sorted({stream for product in products for stream in product})
    streams_ref, rim_ref, taps_ref, keep_ref = refs[:4]
    out_refs, padded_ref = refs[4:-1], refs[-1]
    rows, tile = streams_ref.shape[-2:]
    tiled = len(streams_ref.shape) == 2
    bundle = 1 + max(piece[0] for column in columns for piece in column)
    width = bundle * own_count
    strip = 16

    def one_bundle(index, _):
        bundle_index = pl.program_id(0) * (tile // width) + index

        def column_of(ref, column, *at):
            base = (index if len(ref.shape) == 2 else bundle_index) * width
            spans, pieces = [], []
            for owner, first, last in column:
                start = owner * own_count + first
                if spans and spans[-1][1] == start:
                    spans[-1][1] += last - first
                else:
                    spans.append([start, start + last - first])
            for start, end in spans:
                floor = start // LANES * LANES
                value = ref[*at, pl.ds(pl.multiple_of(base + floor, LANES), LANES)]
                pieces.append(value[:, start - floor : end - floor])
            return pieces[0] if len(pieces) == 1 else jnp.concatenate(pieces, 1)

        taps = {}
        for number, column in enumerate(columns):
            for stream in chosen:
                rim = column_of(rim_ref, column, stream, slice(None)).astype(jnp.float32)
                own = column_of(streams_ref, column, *([] if tiled else [stream]), slice(None)).astype(jnp.float32)
                padded_ref[number, stream, :HALO] = rim
                padded_ref[number, stream, HALO:] = own
                taps[number, stream] = column_of(taps_ref, column, stream, slice(None))
        results = [[[] for _ in columns] for _ in products]
        for row in range(0, rows, strip):
            keep = [keep_ref[tap, pl.ds(row, strip)] for tap in range(tap_count - 1)]
            for number in range(len(columns)):
                for which, product in enumerate(products):
                    value = None
                    for stream in product:
                        tap_of = lambda tap: taps[number, stream][tap : tap + 1]
                        total = tap_of(0) * padded_ref[number, stream, pl.ds(HALO + row, strip)]
                        for tap in range(1, tap_count):
                            term = tap_of(tap) * padded_ref[number, stream, pl.ds(HALO + row - tap, strip)]
                            total = total + keep[tap - 1] * term
                        value = total if value is None else value * total
                    results[which][number].append(value.astype(jnp.bfloat16))
        for which in range(len(products)):
            for number, column in enumerate(columns):
                value = jnp.concatenate(results[which][number], 0).T
                row = 0
                for owner, first, last in column:
                    place = (bundle_index * bundle + owner, pl.ds(first - low, last - first))
                    out_refs[which][place] = value[row : row + last - first]
                    row += last - first
        return 0

    lax.fori_loop(0, tile // width, one_bundle, 0)


def features(streams, products, rim, taps, keep, own_count, low, high):
    rows, channels = streams.shape[-2:]
    count = taps.shape[0]
    owners = channels // own_count
    tiles = 1 if streams.ndim == 3 else max(1, channels // 2048)
    stream_spec = VMEM_SPEC
    if streams.ndim == 2:
        stream_spec = pl.BlockSpec((rows, channels // tiles), lambda i: (0, i))
    bundle = max(1, LANES // (high - low))
    while bundle * (high - low) % LANES:
        bundle += 1
    if len(gathered(bundle, own_count, low, high)) == 1:
        bundle *= 2
    columns = gathered(bundle, own_count, low, high)
    return pl.pallas_call(
        functools.partial(feature_kernel, products, keep.shape[0] + 1, own_count, low, columns),
        grid=(tiles,),
        in_specs=[stream_spec] + [VMEM_SPEC] * 3,
        out_specs=[VMEM_SPEC] * len(products),
        out_shape=[pltpu.VMEM((owners, high - low, rows), jnp.bfloat16)] * len(products),
        scratch_shapes=[pltpu.VMEM((len(columns), count, HALO + rows, LANES), jnp.float32)],
        cost_estimate=pl.CostEstimate(flops=1 << 10, bytes_accessed=1 << 10, transcendentals=0),
        compiler_params=pltpu.CompilerParams(vmem_limit_bytes=VMEM_LIMIT),
        name="features",
    )(*(near if streams.ndim == 3 else far)(streams), *near(rim, taps, keep))


def convolve_kernel(
    first_group, group_stride, mixed_ref, rim_ref, gate_ref, skip_ref, taps_ref, keep_ref, out_ref
):
    owners, count, rows = out_ref.shape
    length = taps_ref.shape[1]

    def one_owner(index, _):
        owner = pl.program_id(0) * owners + index
        for low in range(0, count, 64):
            block = min(64, count - low)
            whole = pl.ds(low, block)
            place = first_group * GROUP + low
            skip = jnp.broadcast_to(skip_ref[owner][:, place : place + block], (block, block))
            row = lax.broadcasted_iota(jnp.int32, (block, block), 0)
            column = lax.broadcasted_iota(jnp.int32, (block, block), 1)
            gain = jnp.where(row == column, skip, 0.0)
            gain_high = gain.astype(jnp.bfloat16)
            gain_low = (gain - gain_high.astype(jnp.float32)).astype(jnp.bfloat16)
            own_block = mixed_ref[owner, whole]
            direct = jnp.dot(
                jnp.concatenate([gain_high, gain_low], 1),
                jnp.concatenate([own_block, own_block], 0),
                preferred_element_type=jnp.float32,
            )
            for unit in range(block // GROUP):
                members = pl.ds(low + unit * GROUP, GROUP)
                group = owner * group_stride + first_group + low // GROUP + unit
                row = jnp.broadcast_to(taps_ref[pl.ds(group, 1)], (GROUP, length))
                base = pltpu.roll(row, 0, 1, stride=1, stride_axis=0).astype(jnp.bfloat16)
                strips = [base] + [pltpu.roll(base, shift, 1) for shift in range(GROUP, length, GROUP)]
                circulant = jnp.concatenate(strips, 0)
                weights = jnp.concatenate([circulant, circulant], 0) * keep_ref[...]
                window = jnp.concatenate([rim_ref[owner, members], mixed_ref[owner, members]], 1)
                total = jnp.dot(window, weights, preferred_element_type=jnp.float32)
                total = total + direct[unit * GROUP : (unit + 1) * GROUP]
                total = total * gate_ref[owner, members].astype(jnp.float32)
                out_ref[index, members] = total.astype(jnp.bfloat16)
        return 0

    together = max(1, min(owners, 8))
    lax.fori_loop(0, owners, one_owner, 0, unroll=together)


def convolve(mixed, rim, gate, skip_gain, taps, keep, first_channel, own_count):
    owners, count, rows = mixed.shape
    steps = min(owners, 2 if 2 * count <= own_count else 4)
    return pl.pallas_call(
        functools.partial(convolve_kernel, first_channel // GROUP, own_count // GROUP),
        grid=(steps,),
        in_specs=[VMEM_SPEC] * 6,
        out_specs=pl.BlockSpec((owners // steps, count, rows), lambda i: (i, 0, 0)),
        out_shape=pltpu.HBM(mixed.shape, jnp.bfloat16),
        cost_estimate=pl.CostEstimate(flops=(1 << 37) if first_channel else 1 << 10, bytes_accessed=1 << 10, transcendentals=0),
        compiler_params=pltpu.CompilerParams(vmem_limit_bytes=VMEM_LIMIT),
        name="convolve",
    )(*near(mixed, rim, gate), skip_gain.reshape(owners, 1, own_count), *near(taps, keep))


def on_device(first, second, value, short_filter, long_filter, skip_gain, lengths):
    rows, channels = first.shape
    devices = lax.axis_size(AXES)
    own_count = channels // devices
    place = jnp.reshape(lax.axis_index(AXES) * rows, (1,)).astype(jnp.int32)
    following = [(source, source + 1) for source in range(devices - 1)]
    streams = (first, second, value)
    cuts = CUTS if own_count == CUTS[-1] else (0, own_count)
    last, lengths = lax.optimization_barrier((last_rows(streams), lengths))
    rim = lax.ppermute(last, AXES, following)
    short_keep, long_keep, long_taps, short_taps, streams = prepare(
        place, lengths, short_filter, long_filter, streams
    )
    feature = lambda products, rim, low, high: features(
        streams, products, rim, short_taps, short_keep, own_count, low, high
    )
    mix = lambda mixed, rims, gate, low: convolve(
        mixed, rims, gate, skip_gain, long_taps, long_keep, low, own_count
    )
    relay = lambda part: lax.all_to_all(part, AXES, 0, 0, tiled=True)
    as_rows = lambda part: part.transpose(1, 0, 2).reshape(part.shape[1], -1)
    mixed_of, gate_of = (0, 2), (1,)
    (low, cut), *rest = zip(cuts, cuts[1:])
    mixed, gate = feature((mixed_of, gate_of), rim, low, cut)
    rims = lax.ppermute(mixed, AXES, following)
    if not rest:
        return as_rows(relay(mix(mixed, rims, gate, low)))

    rim, _ = lax.optimization_barrier((rim, mixed))
    (high_mixed,) = feature((mixed_of,), rim, cut, own_count)
    high_mixed, rims = lax.optimization_barrier((high_mixed, rims))
    high_rims = lax.ppermute(high_mixed, AXES, following)
    (high_gate,) = features(second, (gate_of,), rim, short_taps, short_keep, own_count, cut, own_count)
    low_part = relay(mix(mixed, rims, gate, low))
    high_part = relay(mix(high_mixed, high_rims, high_gate, cut))
    return jnp.concatenate([as_rows(low_part), as_rows(high_part)], 0)


def solution(mesh):
    tokens = P(AXES, None)
    return jax.shard_map(
        on_device,
        mesh=mesh,
        in_specs=(tokens, tokens, tokens, P(), P(), P(), P()),
        out_specs=tokens,
        check_vma=False,
    )
```

time: 116 us -> 110 us (0.948)
  Pallas kernels: 49.5 us -> 34.8 us
  starting transfers between devices: 22.2 us -> 29.3 us
  waiting for transfers between devices: 40.4 us -> 42.3 us
    pallas_call x5, Pallas kernels: 32.9 us -> 20.3 us  [the longest x3 15.1 us: features(): pl.pallas_call(functools.partial(feature_kernel, products, keep.shape[0]...]
    ppermute x1, starting transfers between devices: 2.17 us -> 8.57 us  [on_device(): high_rims = lax.ppermute(high_mixed, AXES, following)]
    pallas_call x2, Pallas kernels: 16.7 us -> 14.5 us  [convolve(): pl.pallas_call(functools.partial(convolve_kernel, first_channel // GROUP,...]
    unnamed x6 -> x8, local copies, waits for them, and re-layouts: 1.94 us -> 0.02 us
    all_to_all x2, waiting for transfers between devices: 40.4 us -> 42.3 us  [on_device(): relay = lambda part: lax.all_to_all(part, AXES, 0, 0, tiled=True)]
  transfers between devices with their start and end apart: 5 -> 5, of which waited for: 2 -> 2; matrix products, arithmetic and copies ran while one was open for 0% -> 1% of each run, Pallas kernels for 34% -> 26%
where the time goes in v3:
time: 110 us; the launch traced here: 109 us
  waiting for transfers between devices  42.3 us (38%)
  Pallas kernels  34.8 us (32%)
  starting transfers between devices  29.3 us (27%)
  other arithmetic  1.46 us (1%)
  local copies, waits for them, and re-layouts  1.35 us (1%)
    all_to_all x2, waiting for transfers between devices, on_device(): relay = lambda part: lax.all_to_all(part, AXES, 0, 0, tiled=True)  42.3 us
    pallas_call x3, Pallas kernels, features(): pl.pallas_call(functools.partial(feature_kernel, products, keep.shape[0]...  15.1 us
    pallas_call x2, Pallas kernels, convolve(): pl.pallas_call(functools.partial(convolve_kernel, first_channel // GROUP,...  14.5 us
    all_to_all x2, starting transfers between devices, on_device(): relay = lambda part: lax.all_to_all(part, AXES, 0, 0, tiled=True)  13.2 us
    ppermute x1, starting transfers between devices, on_device(): high_rims = lax.ppermute(high_mixed, AXES, following)  8.57 us
    ppermute x1, starting transfers between devices, on_device(): rims = lax.ppermute(mixed, AXES, following)  5.11 us
    pallas_call x1, Pallas kernels, prepare(): pl.pallas_call(functools.partial(prepare_kernel, tile), in_specs=[SMEM_SP...  4.06 us
    ppermute x1, starting transfers between devices, on_device(): rim = lax.ppermute(last, AXES, following)  2.39 us
  transfers between devices with their start and end apart: 5, of which 2 were waited for; matrix products, arithmetic and copies ran while one was open for 1% of the time, Pallas kernels for 26%

profile of v3, /device:TPU:0, one launch (start us, length us, event | category | flops | bytes accessed | tf_op | source)
XLA Modules:
  0.0 109.3 jit_solution(4628066978192541461)
XLA Ops:
  0.0 0.0 copy-start.3
  0.0 0.0 copy-start
  0.0 0.0 copy-start.2
  0.0 1.2 %last_rows.1 = bf16[3,8,8192]{2,1,0:T(8,128)(2,1)S(1)} custom-call(bf16[128,8192]{1,0:T(8,128)(2,1)} %first_ref.1, bf16[128,8192]{1,0:T(8,128)(2,1)} %refs_0_.3, bf16[128,8192]{1,0:T(8,128)(2,1)} %value_ref.1), custom_call_target="tpu_custom_call" | custom-call | tf_op jit(solution)/shard_map/last_rows/pallas_call | solution.py:112
  1.2 2.4 %collective-permute-start = (bf16[3,8,8192]{2,1,0:T(8,128)(2,1)S(1)}, bf16[3,8,8192]{2,1,0:T(8,128)(2,1)S(1)}, u32[]{:S(2)}, u32[]{:S(2)}) collective-permute-start(bf16[3,8,8192]{2,1,0:T(8,128)(2,1)S(1)} %last_rows.1), channel_id=1, source_target_pairs={{0,1},{1,2},{2,3},{3,4},{4,5},{5,6},{6,7},{7,8},{8,9},{9,10},{10,1... | collective-permute-start | bytes 1179656 | tf_op jit(solution)/shard_map/ppermute | solution.py:302
  3.6 0.0 copy-done.3
  3.6 0.0 copy-done
  3.6 0.0 copy-done.2
  3.6 4.1 %prepare.1 = (f32[6,128,128]{2,1,0:T(8,128)S(1)}, bf16[256,128]{1,0:T(8,128)(2,1)S(1)}, f32[512,128]{1,0:T(8,128)S(1)}, f32[3,8,8192]{2,1,0:T(8,128)S(1)}, bf16[3,128,8192]{2,1,0:T(8,128)(2,1)S(1)}) custom-call(s32[1]{0:T(128)} %bitcast.place_ref, s32[16]{0:T(128)S(1)} %copy-done.3, bf16[3,7,512]{2,1,0:T(8,128)(2,1)S(1)} %copy-done.2, ...), custom_call_target="tpu_custom_call" | custom-call | flops 1024 | bytes 1024 | tf_op jit(solution)/shard_map/prepare/pallas_call | solution.py:84
  7.7 0.0 collective-permute-done.refs_1_
  7.7 4.9 %features.3 = (bf16[32,96,128]{2,1,0:T(8,128)(2,1)S(1)}, bf16[32,96,128]{2,1,0:T(8,128)(2,1)S(1)}) custom-call(bf16[3,128,8192]{2,1,0:T(8,128)(2,1)S(1)} %get-tuple-element.18.refs_0_, bf16[3,8,8192]{2,1,0:T(8,128)(2,1)S(1)} %collective-permute-done.refs_1_, f32[3,8,8192]{2,1,0:T(8,128)S(1)} %get-tuple-element.20.refs_2_, ...), custom_call_target="tpu_custom_call" | custom-call | flops 1024 | bytes 1024 | tf_op jit(solution)/shard_map/features/pallas_call | solution.py:222
  12.6 5.1 %collective-permute-start.1 = (bf16[32,96,128]{2,1,0:T(8,128)(2,1)S(1)}, bf16[32,96,128]{2,1,0:T(8,128)(2,1)S(1)}, u32[]{:S(2)}, u32[]{:S(2)}) collective-permute-start(bf16[32,96,128]{2,1,0:T(8,128)(2,1)S(1)} %get-tuple-element.22.mixed_ref), channel_id=1, source_target_pairs={{0,1},{1,2},{2,3},{3,4},{4,5},{5,6},{6,7},{7,8},{8,9},{9,10},{10,1... | collective-permute-start | bytes 2359304 | tf_op jit(solution)/shard_map/ppermute | solution.py:317
  17.7 5.7 %features.4.mixed_ref = bf16[32,160,128]{2,1,0:T(8,128)(2,1)S(1)} custom-call(bf16[3,128,8192]{2,1,0:T(8,128)(2,1)S(1)} %get-tuple-element.18.refs_0_, bf16[3,8,8192]{2,1,0:T(8,128)(2,1)S(1)} %collective-permute-done.refs_1_, f32[3,8,8192]{2,1,0:T(8,128)S(1)} %get-tuple-element.20.refs_2_, f32[6,128,128]{2,1,0:T(8,128)S(1)} %get-tuple-element.21.refs_3_), custom_call_target="tpu_custom_call" | custom-call | flops 1024 | bytes 1024 | tf_op jit(solution)/shard_map/features/pallas_call | solution.py:222
  23.5 0.0 copy-start.1
  23.5 0.0 collective-permute-done.1.rim_ref
  23.5 8.6 %collective-permute-start.2 = (bf16[32,160,128]{2,1,0:T(8,128)(2,1)S(1)}, bf16[32,160,128]{2,1,0:T(8,128)(2,1)}, u32[]{:S(2)}, u32[]{:S(2)}) collective-permute-start(bf16[32,160,128]{2,1,0:T(8,128)(2,1)S(1)} %features.4.mixed_ref), channel_id=1, source_target_pairs={{0,1},{1,2},{2,3},{3,4},{4,5},{5,6},{6,7},{7,8},{8,9},{9,10},{10,1... | collective-permute-start | bytes 3932168 | tf_op jit(solution)/shard_map/ppermute | solution.py:324
  32.1 4.4 %features.5.gate_ref = bf16[32,160,128]{2,1,0:T(8,128)(2,1)S(1)} custom-call(bf16[128,8192]{1,0:T(8,128)(2,1)} %refs_0_.3, bf16[3,8,8192]{2,1,0:T(8,128)(2,1)S(1)} %collective-permute-done.refs_1_, f32[3,8,8192]{2,1,0:T(8,128)S(1)} %get-tuple-element.20.refs_2_, f32[6,128,128]{2,1,0:T(8,128)S(1)} %get-tuple-element.21.refs_3_), custom_call_target="tpu_custom_call" | custom-call | flops 1024 | bytes 1024 | tf_op jit(solution)/shard_map/features/pallas_call | solution.py:222
  36.5 0.0 copy-done.1
  36.5 5.3 %convolve.2 = bf16[32,96,128]{2,1,0:T(8,128)(2,1)} custom-call(bf16[32,96,128]{2,1,0:T(8,128)(2,1)S(1)} %get-tuple-element.22.mixed_ref, bf16[32,96,128]{2,1,0:T(8,128)(2,1)S(1)} %collective-permute-done.1.rim_ref, bf16[32,96,128]{2,1,0:T(8,128)(2,1)S(1)} %get-tuple-element.25.gate_ref, f32[32,1,256]{2,1,0:T(1,128)S(1)} %bitcast.14, ...), custom_call_target="tpu_custom_call" | custom-call | flops 1024 | bytes 1024 | tf_op jit(solution)/shard_map/convolve/pallas_call | solution.py:281
  41.8 9.6 %all-to-all-start = ((bf16[32,96,128]{2,1,0:T(8,128)(2,1)}), bf16[32,96,128]{2,1,0:T(8,128)(2,1)}, u32[]{:S(2)}, u32[]{:S(2)}) async-start(bf16[32,96,128]{2,1,0:T(8,128)(2,1)} %convolve.2), calls=%async_computation | async-start | bytes 1572864 | tf_op jit(solution)/shard_map/all_to_all | solution.py:312
  51.3 0.0 collective-permute-done.2.rim_ref
  51.3 9.3 %convolve.3 = bf16[32,160,128]{2,1,0:T(8,128)(2,1)} custom-call(bf16[32,160,128]{2,1,0:T(8,128)(2,1)S(1)} %features.4.mixed_ref, bf16[32,160,128]{2,1,0:T(8,128)(2,1)} %collective-permute-done.2.rim_ref, bf16[32,160,128]{2,1,0:T(8,128)(2,1)S(1)} %features.5.gate_ref, f32[32,1,256]{2,1,0:T(1,128)S(1)} %bitcast.15, f32[512,128]{1,0:T(8,128)S(1)} %get-tuple-element.26.taps_ref, ...), custom_call_target="tpu_custom_call" | custom-call | flops 137438953472 | bytes 1024 | tf_op jit(solution)/shard_map/convolve/pallas_call | solution.py:281
  60.6 11.3 %all-to-all-done = bf16[32,96,128]{2,1,0:T(8,128)(2,1)} async-done(((bf16[32,96,128]{2,1,0:T(8,128)(2,1)}), bf16[32,96,128]{2,1,0:T(8,128)(2,1)}, u32[]{:S(2)}, u32[]{:S(2)}) %all-to-all-start) | async-done | bytes 786464 | tf_op jit(solution)/shard_map/all_to_all | solution.py:312
  71.9 3.6 %all-to-all-start.1 = ((bf16[32,160,128]{2,1,0:T(8,128)(2,1)}), bf16[32,160,128]{2,1,0:T(8,128)(2,1)S(1)}, u32[]{:S(2)}, u32[]{:S(2)}) async-start(bf16[32,160,128]{2,1,0:T(8,128)(2,1)} %convolve.3), calls=%async_computation.1 | async-start | bytes 2621440 | tf_op jit(solution)/shard_map/all_to_all | solution.py:312
  75.6 1.2 %copy_bitcast_fusion.1 = bf16[96,4096]{1,0:T(8,128)(2,1)S(1)} fusion(bf16[32,96,128]{2,1,0:T(8,128)(2,1)} %all-to-all-done), kind=kLoop, calls=%fused_computation.2 | loop fusion | bytes 1572864 | tf_op jit(solution)/shard_map/reshape | solution.py:313
  76.8 30.9 %all-to-all-done.1 = bf16[32,160,128]{2,1,0:T(8,128)(2,1)S(1)} async-done(((bf16[32,160,128]{2,1,0:T(8,128)(2,1)}), bf16[32,160,128]{2,1,0:T(8,128)(2,1)S(1)}, u32[]{:S(2)}, u32[]{:S(2)}) %all-to-all-start.1) | async-done | bytes 1310752 | tf_op jit(solution)/shard_map/all_to_all | solution.py:312
  107.7 0.1 copy_bitcast_fusion
  107.8 1.5 %pad_maximum_fusion = bf16[256,4096]{1,0:T(8,128)(2,1)} fusion(bf16[160,4096]{1,0:T(8,128)(2,1)S(1)} %copy_bitcast_fusion, bf16[96,4096]{1,0:T(8,128)(2,1)S(1)} %copy_bitcast_fusion.1), kind=kLoop, calls=%fused_computation | loop fusion | flops 4194304 | bytes 4194304 | tf_op jit(solution)/shard_map/concatenate | solution.py:328
Async XLA Ops:
  0.0 3.6 %copy-start.3 = (s32[16]{0:T(128)S(1)}, s32[16]{0:T(128)}, u32[]{:S(2)}) copy-start(s32[16]{0:T(128)} %lengths_ref) | copy-start | bytes 196
  0.0 3.6 %copy-start = (bf16[128,512]{1,0:T(8,128)(2,1)S(1)}, bf16[128,512]{1,0:T(8,128)(2,1)}, u32[]{:S(2)}) copy-start(bf16[128,512]{1,0:T(8,128)(2,1)} %long_ref.1) | copy-start | bytes 393220
  0.0 3.6 %copy-start.2 = (bf16[3,7,512]{2,1,0:T(8,128)(2,1)S(1)}, bf16[3,7,512]{2,1,0:T(8,128)(2,1)}, u32[]{:S(2)}) copy-start(bf16[3,7,512]{2,1,0:T(8,128)(2,1)} %short_ref.1) | copy-start | bytes 64516
  1.2 6.5 %collective-permute-start = (bf16[3,8,8192]{2,1,0:T(8,128)(2,1)S(1)}, bf16[3,8,8192]{2,1,0:T(8,128)(2,1)S(1)}, u32[]{:S(2)}, u32[]{:S(2)}) collective-permute-start(bf16[3,8,8192]{2,1,0:T(8,128)(2,1)S(1)} %last_rows.1), channel_id=1, source_target_pairs={{0,1},{1,2},{2,3},{3,4},{4,5},{5,6},{6,7},{7,8},{8,9},{9,10},{10,1... | collective-permute-start | bytes 1179656 | tf_op jit(solution)/shard_map/ppermute | solution.py:302
  12.6 10.9 %collective-permute-start.1 = (bf16[32,96,128]{2,1,0:T(8,128)(2,1)S(1)}, bf16[32,96,128]{2,1,0:T(8,128)(2,1)S(1)}, u32[]{:S(2)}, u32[]{:S(2)}) collective-permute-start(bf16[32,96,128]{2,1,0:T(8,128)(2,1)S(1)} %get-tuple-element.22.mixed_ref), channel_id=1, source_target_pairs={{0,1},{1,2},{2,3},{3,4},{4,5},{5,6},{6,7},{7,8},{8,9},{9,10},{10,1... | collective-permute-start | bytes 2359304 | tf_op jit(solution)/shard_map/ppermute | solution.py:317
  23.5 13.0 %copy-start.1 = (f32[8192]{0:T(1024)S(1)}, f32[8192]{0:T(1024)}, u32[]{:S(2)}) copy-start(f32[8192]{0:T(1024)} %param.12) | copy-start | bytes 98308
  23.5 27.8 %collective-permute-start.2 = (bf16[32,160,128]{2,1,0:T(8,128)(2,1)S(1)}, bf16[32,160,128]{2,1,0:T(8,128)(2,1)}, u32[]{:S(2)}, u32[]{:S(2)}) collective-permute-start(bf16[32,160,128]{2,1,0:T(8,128)(2,1)S(1)} %features.4.mixed_ref), channel_id=1, source_target_pairs={{0,1},{1,2},{2,3},{3,4},{4,5},{5,6},{6,7},{7,8},{8,9},{9,10},{10,1... | collective-permute-start | bytes 3932168 | tf_op jit(solution)/shard_map/ppermute | solution.py:324
  41.8 30.2 %all-to-all-start = ((bf16[32,96,128]{2,1,0:T(8,128)(2,1)}), bf16[32,96,128]{2,1,0:T(8,128)(2,1)}, u32[]{:S(2)}, u32[]{:S(2)}) async-start(bf16[32,96,128]{2,1,0:T(8,128)(2,1)} %convolve.2), calls=%async_computation | async-start | bytes 1572864 | tf_op jit(solution)/shard_map/all_to_all | solution.py:312
  71.9 35.8 %all-to-all-start.1 = ((bf16[32,160,128]{2,1,0:T(8,128)(2,1)}), bf16[32,160,128]{2,1,0:T(8,128)(2,1)S(1)}, u32[]{:S(2)}, u32[]{:S(2)}) async-start(bf16[32,160,128]{2,1,0:T(8,128)(2,1)} %convolve.3), calls=%async_computation.1 | async-start | bytes 2621440 | tf_op jit(solution)/shard_map/all_to_all | solution.py:312

commit v4 on v3

--- a/solution.py
+++ b/solution.py
@@ -284,7 +284,7 @@
         in_specs=[VMEM_SPEC] * 6,
         out_specs=pl.BlockSpec((owners // steps, count, rows), lambda i: (i, 0, 0)),
         out_shape=pltpu.HBM(mixed.shape, jnp.bfloat16),
-        cost_estimate=pl.CostEstimate(flops=(1 << 37) if first_channel else 1 << 10, bytes_accessed=1 << 10, transcendentals=0),
+        cost_estimate=pl.CostEstimate(flops=1 << 37, bytes_accessed=1 << 10, transcendentals=0),
         compiler_params=pltpu.CompilerParams(vmem_limit_bytes=VMEM_LIMIT),
         name="convolve",
     )(*near(mixed, rim, gate), skip_gain.reshape(owners, 1, own_count), *near(taps, keep))
@@ -320,10 +320,11 @@
 
     rim, _ = lax.optimization_barrier((rim, mixed))
     (high_mixed,) = feature((mixed_of,), rim, cut, own_count)
-    high_mixed, rims = lax.optimization_barrier((high_mixed, rims))
     high_rims = lax.ppermute(high_mixed, AXES, following)
+    low_part = mix(mixed, rims, gate, low)
+    rim, _ = lax.optimization_barrier((rim, low_part))
+    low_part = relay(low_part)
     (high_gate,) = features(second, (gate_of,), rim, short_taps, short_keep, own_count, cut, own_count)
-    low_part = relay(mix(mixed, rims, gate, low))
     high_part = relay(mix(high_mixed, high_rims, high_gate, cut))
     return jnp.concatenate([as_rows(low_part), as_rows(high_part)], 0)
 

time: 110 us -> 102 us (0.927)
  waiting for transfers between devices: 42.3 us -> 37.8 us
  starting transfers between devices: 29.3 us -> 26 us
    all_to_all x2, waiting for transfers between devices: 42.3 us -> 37.8 us  [on_device(): relay = lambda part: lax.all_to_all(part, AXES, 0, 0, tiled=True)]
    ppermute x1, starting transfers between devices: 8.57 us -> 5.43 us  [on_device(): high_rims = lax.ppermute(high_mixed, AXES, following)]
  transfers between devices with their start and end apart: 5 -> 5, of which waited for: 2 -> 2; matrix products, arithmetic and copies ran while one was open for 1% -> 1% of each run, Pallas kernels for 26% -> 28%
where the time goes in v4:
time: 102 us
  waiting for transfers between devices  37.8 us (37%)
  Pallas kernels  34.8 us (34%)
  starting transfers between devices  26 us (25%)
  other arithmetic  1.46 us (1%)
  local copies, waits for them, and re-layouts  1.35 us (1%)
    all_to_all x2, waiting for transfers between devices, on_device(): relay = lambda part: lax.all_to_all(part, AXES, 0, 0, tiled=True)  37.8 us
    pallas_call x3, Pallas kernels, features(): pl.pallas_call(functools.partial(feature_kernel, products, keep.shape[0]...  15.1 us
    pallas_call x2, Pallas kernels, convolve(): pl.pallas_call(functools.partial(convolve_kernel, first_channel // GROUP,...  14.5 us
    all_to_all x2, starting transfers between devices, on_device(): relay = lambda part: lax.all_to_all(part, AXES, 0, 0, tiled=True)  13.1 us
    ppermute x1, starting transfers between devices, on_device(): high_rims = lax.ppermute(high_mixed, AXES, following)  5.43 us
    ppermute x1, starting transfers between devices, on_device(): rims = lax.ppermute(mixed, AXES, following)  5.11 us
    pallas_call x1, Pallas kernels, prepare(): pl.pallas_call(functools.partial(prepare_kernel, tile), in_specs=[SMEM_SP...  4.06 us
    ppermute x1, starting transfers between devices, on_device(): rim = lax.ppermute(last, AXES, following)  2.39 us
  transfers between devices with their start and end apart: 5, of which 2 were waited for; matrix products, arithmetic and copies ran while one was open for 1% of the time, Pallas kernels for 28%

profile of v4, /device:TPU:0, one launch (start us, length us, event | category | flops | bytes accessed | tf_op | source)
XLA Modules:
  0.0 101.6 jit_solution(10347630184659143888)
XLA Ops:
  0.0 0.0 copy-start.2
  0.0 0.0 copy-start
  0.0 0.0 copy-start.1
  0.0 1.2 %last_rows.1 = bf16[3,8,8192]{2,1,0:T(8,128)(2,1)S(1)} custom-call(bf16[128,8192]{1,0:T(8,128)(2,1)} %first_ref.1, bf16[128,8192]{1,0:T(8,128)(2,1)} %refs_0_.3, bf16[128,8192]{1,0:T(8,128)(2,1)} %value_ref.1), custom_call_target="tpu_custom_call" | custom-call | tf_op jit(solution)/shard_map/last_rows/pallas_call | solution.py:112
  1.2 2.4 %collective-permute-start = (bf16[3,8,8192]{2,1,0:T(8,128)(2,1)S(1)}, bf16[3,8,8192]{2,1,0:T(8,128)(2,1)S(1)}, u32[]{:S(2)}, u32[]{:S(2)}) collective-permute-start(bf16[3,8,8192]{2,1,0:T(8,128)(2,1)S(1)} %last_rows.1), channel_id=1, source_target_pairs={{0,1},{1,2},{2,3},{3,4},{4,5},{5,6},{6,7},{7,8},{8,9},{9,10},{10,1... | collective-permute-start | bytes 1179656 | tf_op jit(solution)/shard_map/ppermute | solution.py:302
  3.6 0.0 copy-done.2
  3.6 0.0 copy-done
  3.6 0.0 copy-done.1
  3.6 4.1 %prepare.1 = (f32[6,128,128]{2,1,0:T(8,128)S(1)}, bf16[256,128]{1,0:T(8,128)(2,1)S(1)}, f32[512,128]{1,0:T(8,128)S(1)}, f32[3,8,8192]{2,1,0:T(8,128)S(1)}, bf16[3,128,8192]{2,1,0:T(8,128)(2,1)S(1)}) custom-call(s32[1]{0:T(128)} %bitcast.place_ref, s32[16]{0:T(128)S(1)} %copy-done.2, bf16[3,7,512]{2,1,0:T(8,128)(2,1)S(1)} %copy-done.1, ...), custom_call_target="tpu_custom_call" | custom-call | flops 1024 | bytes 1024 | tf_op jit(solution)/shard_map/prepare/pallas_call | solution.py:84
  7.7 0.0 collective-permute-done.refs_1_
  7.7 4.9 %features.3 = (bf16[32,96,128]{2,1,0:T(8,128)(2,1)S(1)}, bf16[32,96,128]{2,1,0:T(8,128)(2,1)S(1)}) custom-call(bf16[3,128,8192]{2,1,0:T(8,128)(2,1)S(1)} %get-tuple-element.17.refs_0_, bf16[3,8,8192]{2,1,0:T(8,128)(2,1)S(1)} %collective-permute-done.refs_1_, f32[3,8,8192]{2,1,0:T(8,128)S(1)} %get-tuple-element.19.refs_2_, ...), custom_call_target="tpu_custom_call" | custom-call | flops 1024 | bytes 1024 | tf_op jit(solution)/shard_map/features/pallas_call | solution.py:222
  12.6 0.0 copy-start.3
  12.6 5.1 %collective-permute-start.1 = (bf16[32,96,128]{2,1,0:T(8,128)(2,1)S(1)}, bf16[32,96,128]{2,1,0:T(8,128)(2,1)S(1)}, u32[]{:S(2)}, u32[]{:S(2)}) collective-permute-start(bf16[32,96,128]{2,1,0:T(8,128)(2,1)S(1)} %get-tuple-element.21.mixed_ref), channel_id=1, source_target_pairs={{0,1},{1,2},{2,3},{3,4},{4,5},{5,6},{6,7},{7,8},{8,9},{9,10},{10,1... | collective-permute-start | bytes 2359304 | tf_op jit(solution)/shard_map/ppermute | solution.py:317
  17.8 5.7 %features.4.mixed_ref = bf16[32,160,128]{2,1,0:T(8,128)(2,1)S(1)} custom-call(bf16[3,128,8192]{2,1,0:T(8,128)(2,1)S(1)} %get-tuple-element.17.refs_0_, bf16[3,8,8192]{2,1,0:T(8,128)(2,1)S(1)} %collective-permute-done.refs_1_, f32[3,8,8192]{2,1,0:T(8,128)S(1)} %get-tuple-element.19.refs_2_, f32[6,128,128]{2,1,0:T(8,128)S(1)} %get-tuple-element.20.refs_3_), custom_call_target="tpu_custom_call" | custom-call | flops 1024 | bytes 1024 | tf_op jit(solution)/shard_map/features/pallas_call | solution.py:222
  23.5 5.4 %collective-permute-start.2 = (bf16[32,160,128]{2,1,0:T(8,128)(2,1)S(1)}, bf16[32,160,128]{2,1,0:T(8,128)(2,1)}, u32[]{:S(2)}, u32[]{:S(2)}) collective-permute-start(bf16[32,160,128]{2,1,0:T(8,128)(2,1)S(1)} %features.4.mixed_ref), channel_id=1, source_target_pairs={{0,1},{1,2},{2,3},{3,4},{4,5},{5,6},{6,7},{7,8},{8,9},{9,10},{10,1... | collective-permute-start | bytes 3932168 | tf_op jit(solution)/shard_map/ppermute | solution.py:323
  28.9 0.0 collective-permute-done.1.rim_ref
  28.9 0.0 copy-done.3
  28.9 5.2 %convolve.2 = bf16[32,96,128]{2,1,0:T(8,128)(2,1)} custom-call(bf16[32,96,128]{2,1,0:T(8,128)(2,1)S(1)} %get-tuple-element.21.mixed_ref, bf16[32,96,128]{2,1,0:T(8,128)(2,1)S(1)} %collective-permute-done.1.rim_ref, bf16[32,96,128]{2,1,0:T(8,128)(2,1)S(1)} %get-tuple-element.22.gate_ref, f32[32,1,256]{2,1,0:T(1,128)S(1)} %bitcast.14, ...), custom_call_target="tpu_custom_call" | custom-call | flops 137438953472 | bytes 1024 | tf_op jit(solution)/shard_map/convolve/pallas_call | solution.py:281
  34.2 8.7 %all-to-all-start = ((bf16[32,96,128]{2,1,0:T(8,128)(2,1)}), bf16[32,96,128]{2,1,0:T(8,128)(2,1)}, u32[]{:S(2)}, u32[]{:S(2)}) async-start(bf16[32,96,128]{2,1,0:T(8,128)(2,1)} %convolve.2), calls=%async_computation | async-start | bytes 1572864 | tf_op jit(solution)/shard_map/all_to_all | solution.py:312
  42.9 4.4 %features.5.gate_ref = bf16[32,160,128]{2,1,0:T(8,128)(2,1)S(1)} custom-call(bf16[128,8192]{1,0:T(8,128)(2,1)} %refs_0_.3, bf16[3,8,8192]{2,1,0:T(8,128)(2,1)S(1)} %collective-permute-done.refs_1_, f32[3,8,8192]{2,1,0:T(8,128)S(1)} %get-tuple-element.19.refs_2_, f32[6,128,128]{2,1,0:T(8,128)S(1)} %get-tuple-element.20.refs_3_), custom_call_target="tpu_custom_call" | custom-call | flops 1024 | bytes 1024 | tf_op jit(solution)/shard_map/features/pallas_call | solution.py:222
  47.3 0.0 collective-permute-done.2.rim_ref
  47.3 9.3 %convolve.3 = bf16[32,160,128]{2,1,0:T(8,128)(2,1)} custom-call(bf16[32,160,128]{2,1,0:T(8,128)(2,1)S(1)} %features.4.mixed_ref, bf16[32,160,128]{2,1,0:T(8,128)(2,1)} %collective-permute-done.2.rim_ref, bf16[32,160,128]{2,1,0:T(8,128)(2,1)S(1)} %features.5.gate_ref, f32[32,1,256]{2,1,0:T(1,128)S(1)} %bitcast.15, f32[512,128]{1,0:T(8,128)S(1)} %get-tuple-element.23.taps_ref, ...), custom_call_target="tpu_custom_call" | custom-call | flops 137438953472 | bytes 1024 | tf_op jit(solution)/shard_map/convolve/pallas_call | solution.py:281
  56.6 6.9 %all-to-all-done = bf16[32,96,128]{2,1,0:T(8,128)(2,1)} async-done(((bf16[32,96,128]{2,1,0:T(8,128)(2,1)}), bf16[32,96,128]{2,1,0:T(8,128)(2,1)}, u32[]{:S(2)}, u32[]{:S(2)}) %all-to-all-start) | async-done | bytes 786464 | tf_op jit(solution)/shard_map/all_to_all | solution.py:312
  63.5 4.3 %all-to-all-start.1 = ((bf16[32,160,128]{2,1,0:T(8,128)(2,1)}), bf16[32,160,128]{2,1,0:T(8,128)(2,1)S(1)}, u32[]{:S(2)}, u32[]{:S(2)}) async-start(bf16[32,160,128]{2,1,0:T(8,128)(2,1)} %convolve.3), calls=%async_computation.1 | async-start | bytes 2621440 | tf_op jit(solution)/shard_map/all_to_all | solution.py:312
  67.9 1.2 %copy_bitcast_fusion.1 = bf16[96,4096]{1,0:T(8,128)(2,1)S(1)} fusion(bf16[32,96,128]{2,1,0:T(8,128)(2,1)} %all-to-all-done), kind=kLoop, calls=%fused_computation.2 | loop fusion | bytes 1572864 | tf_op jit(solution)/shard_map/reshape | solution.py:313
  69.1 30.9 %all-to-all-done.1 = bf16[32,160,128]{2,1,0:T(8,128)(2,1)S(1)} async-done(((bf16[32,160,128]{2,1,0:T(8,128)(2,1)}), bf16[32,160,128]{2,1,0:T(8,128)(2,1)S(1)}, u32[]{:S(2)}, u32[]{:S(2)}) %all-to-all-start.1) | async-done | bytes 1310752 | tf_op jit(solution)/shard_map/all_to_all | solution.py:312
  100.0 0.1 copy_bitcast_fusion
  100.1 1.5 %pad_maximum_fusion = bf16[256,4096]{1,0:T(8,128)(2,1)} fusion(bf16[160,4096]{1,0:T(8,128)(2,1)S(1)} %copy_bitcast_fusion, bf16[96,4096]{1,0:T(8,128)(2,1)S(1)} %copy_bitcast_fusion.1), kind=kLoop, calls=%fused_computation | loop fusion | flops 4194304 | bytes 4194304 | tf_op jit(solution)/shard_map/concatenate | solution.py:329
Async XLA Ops:
  0.0 3.6 %copy-start.2 = (s32[16]{0:T(128)S(1)}, s32[16]{0:T(128)}, u32[]{:S(2)}) copy-start(s32[16]{0:T(128)} %lengths_ref) | copy-start | bytes 196
  0.0 3.6 %copy-start = (bf16[128,512]{1,0:T(8,128)(2,1)S(1)}, bf16[128,512]{1,0:T(8,128)(2,1)}, u32[]{:S(2)}) copy-start(bf16[128,512]{1,0:T(8,128)(2,1)} %long_ref.1) | copy-start | bytes 393220
  0.0 3.6 %copy-start.1 = (bf16[3,7,512]{2,1,0:T(8,128)(2,1)S(1)}, bf16[3,7,512]{2,1,0:T(8,128)(2,1)}, u32[]{:S(2)}) copy-start(bf16[3,7,512]{2,1,0:T(8,128)(2,1)} %short_ref.1) | copy-start | bytes 64516
  1.2 6.5 %collective-permute-start = (bf16[3,8,8192]{2,1,0:T(8,128)(2,1)S(1)}, bf16[3,8,8192]{2,1,0:T(8,128)(2,1)S(1)}, u32[]{:S(2)}, u32[]{:S(2)}) collective-permute-start(bf16[3,8,8192]{2,1,0:T(8,128)(2,1)S(1)} %last_rows.1), channel_id=1, source_target_pairs={{0,1},{1,2},{2,3},{3,4},{4,5},{5,6},{6,7},{7,8},{8,9},{9,10},{10,1... | collective-permute-start | bytes 1179656 | tf_op jit(solution)/shard_map/ppermute | solution.py:302
  12.6 16.3 %copy-start.3 = (f32[8192]{0:T(1024)S(1)}, f32[8192]{0:T(1024)}, u32[]{:S(2)}) copy-start(f32[8192]{0:T(1024)} %param.12) | copy-start | bytes 98308
  12.6 16.3 %collective-permute-start.1 = (bf16[32,96,128]{2,1,0:T(8,128)(2,1)S(1)}, bf16[32,96,128]{2,1,0:T(8,128)(2,1)S(1)}, u32[]{:S(2)}, u32[]{:S(2)}) collective-permute-start(bf16[32,96,128]{2,1,0:T(8,128)(2,1)S(1)} %get-tuple-element.21.mixed_ref), channel_id=1, source_target_pairs={{0,1},{1,2},{2,3},{3,4},{4,5},{5,6},{6,7},{7,8},{8,9},{9,10},{10,1... | collective-permute-start | bytes 2359304 | tf_op jit(solution)/shard_map/ppermute | solution.py:317
  23.5 23.8 %collective-permute-start.2 = (bf16[32,160,128]{2,1,0:T(8,128)(2,1)S(1)}, bf16[32,160,128]{2,1,0:T(8,128)(2,1)}, u32[]{:S(2)}, u32[]{:S(2)}) collective-permute-start(bf16[32,160,128]{2,1,0:T(8,128)(2,1)S(1)} %features.4.mixed_ref), channel_id=1, source_target_pairs={{0,1},{1,2},{2,3},{3,4},{4,5},{5,6},{6,7},{7,8},{8,9},{9,10},{10,1... | collective-permute-start | bytes 3932168 | tf_op jit(solution)/shard_map/ppermute | solution.py:323
  34.2 29.3 %all-to-all-start = ((bf16[32,96,128]{2,1,0:T(8,128)(2,1)}), bf16[32,96,128]{2,1,0:T(8,128)(2,1)}, u32[]{:S(2)}, u32[]{:S(2)}) async-start(bf16[32,96,128]{2,1,0:T(8,128)(2,1)} %convolve.2), calls=%async_computation | async-start | bytes 1572864 | tf_op jit(solution)/shard_map/all_to_all | solution.py:312
  63.5 36.5 %all-to-all-start.1 = ((bf16[32,160,128]{2,1,0:T(8,128)(2,1)}), bf16[32,160,128]{2,1,0:T(8,128)(2,1)S(1)}, u32[]{:S(2)}, u32[]{:S(2)}) async-start(bf16[32,160,128]{2,1,0:T(8,128)(2,1)} %convolve.3), calls=%async_computation.1 | async-start | bytes 2621440 | tf_op jit(solution)/shard_map/all_to_all | solution.py:312

commit v5 on v4

--- a/solution.py
+++ b/solution.py
@@ -13,6 +13,7 @@
 HALO = 8
 CUTS = (0, 96, 256)
 VMEM_LIMIT = 24 << 20
+UNROLL = 4
 
 
 def begins_of(position, lengths_ref):
@@ -31,9 +32,14 @@
     streams, tap_count, groups = short_ref.shape
     length = long_ref.shape[0]
     rows = long_keep_ref.shape[1]
+    pieces = arrived.shape[1]
+    size = rows // pieces
     copies = [
-        pltpu.make_async_copy(ref, near_ref.at[index], arrived.at[index])
+        pltpu.make_async_copy(
+            ref.at[pl.ds(piece * size, size)], near_ref.at[index, pl.ds(piece * size, size)], arrived.at[index, piece]
+        )
         for index, ref in enumerate((first_ref, second_ref, value_ref))
+        for piece in range(pieces)
     ]
     for copy in copies:
         copy.start()
@@ -94,7 +100,7 @@
         ],
         scratch_shapes=[
             pltpu.VMEM((tile // GROUP, tile), jnp.bfloat16),
-            pltpu.SemaphoreType.DMA((count,)),
+            pltpu.SemaphoreType.DMA((count, 4)),
         ],
         cost_estimate=pl.CostEstimate(flops=1 << 10, bytes_accessed=1 << 10, transcendentals=0),
         compiler_params=pltpu.CompilerParams(vmem_limit_bytes=VMEM_LIMIT),
@@ -142,10 +148,11 @@
     return columns + [[piece] for piece in whole]
 
 
-def feature_kernel(products, tap_count, own_count, low, columns, *refs):
+def feature_kernel(phase, products, tap_count, own_count, low, columns, *refs):
     chosen = sorted({stream for product in products for stream in product})
-    streams_ref, rim_ref, taps_ref, keep_ref = refs[:4]
-    out_refs, padded_ref = refs[4:-1], refs[-1]
+    streams_ref, taps_ref, keep_ref, *refs, padded_ref = refs
+    rim_ref, refs = (None, refs) if phase == "early" else (refs[0], refs[1:])
+    early_refs, out_refs = (refs[: len(products)] if phase == "late" else ()), refs[-len(products) :]
     rows, tile = streams_ref.shape[-2:]
     tiled = len(streams_ref.shape) == 2
     bundle = 1 + max(piece[0] for column in columns for piece in column)
@@ -173,13 +180,15 @@
         taps = {}
         for number, column in enumerate(columns):
             for stream in chosen:
-                rim = column_of(rim_ref, column, stream, slice(None)).astype(jnp.float32)
-                own = column_of(streams_ref, column, *([] if tiled else [stream]), slice(None)).astype(jnp.float32)
-                padded_ref[number, stream, :HALO] = rim
-                padded_ref[number, stream, HALO:] = own
+                at = [] if tiled else [stream]
+                own = column_of(streams_ref, column, *at, slice(0, strip if phase == "late" else rows))
+                padded_ref[number, stream, HALO : HALO + own.shape[0]] = own.astype(jnp.float32)
+                if phase != "early":
+                    rim = column_of(rim_ref, column, stream, slice(None)).astype(jnp.float32)
+                    padded_ref[number, stream, :HALO] = rim
                 taps[number, stream] = column_of(taps_ref, column, stream, slice(None))
         results = [[[] for _ in columns] for _ in products]
-        for row in range(0, rows, strip):
+        for row in range(strip if phase == "early" else 0, strip if phase == "late" else rows, strip):
             keep = [keep_ref[tap, pl.ds(row, strip)] for tap in range(tap_count - 1)]
             for number in range(len(columns)):
                 for which, product in enumerate(products):
@@ -194,7 +203,14 @@
                     results[which][number].append(value.astype(jnp.bfloat16))
         for which in range(len(products)):
             for number, column in enumerate(columns):
-                value = jnp.concatenate(results[which][number], 0).T
+                value = results[which][number]
+                lanes = pl.ds(pl.multiple_of((bundle_index * len(columns) + number) * LANES, LANES), LANES)
+                if phase == "early":
+                    out_refs[which][:, lanes] = jnp.concatenate(value, 0)
+                    continue
+                if phase == "late":
+                    value = value + [early_refs[which][:, lanes]]
+                value = jnp.concatenate(value, 0).T
                 row = 0
                 for owner, first, last in column:
                     place = (bundle_index * bundle + owner, pl.ds(first - low, last - first))
@@ -202,10 +218,10 @@
                     row += last - first
         return 0
 
-    lax.fori_loop(0, tile // width, one_bundle, 0)
-
-
-def features(streams, products, rim, taps, keep, own_count, low, high):
+    lax.fori_loop(0, tile // width, one_bundle, 0, unroll=UNROLL if phase == "late" else 1)
+
+
+def features(streams, products, rim, taps, keep, own_count, low, high, phase="whole", early=()):
     rows, channels = streams.shape[-2:]
     count = taps.shape[0]
     owners = channels // own_count
@@ -219,21 +235,24 @@
     if len(gathered(bundle, own_count, low, high)) == 1:
         bundle *= 2
     columns = gathered(bundle, own_count, low, high)
+    shape = (rows - 16, owners * (high - low)) if phase == "early" else (owners, high - low, rows)
+    given = [*(near if streams.ndim == 3 else far)(streams), *near(taps, keep)]
+    given += near(*([] if phase == "early" else [rim]), *early)
     return pl.pallas_call(
-        functools.partial(feature_kernel, products, keep.shape[0] + 1, own_count, low, columns),
+        functools.partial(feature_kernel, phase, products, keep.shape[0] + 1, own_count, low, columns),
         grid=(tiles,),
-        in_specs=[stream_spec] + [VMEM_SPEC] * 3,
+        in_specs=[stream_spec] + [VMEM_SPEC] * (len(given) - 1),
         out_specs=[VMEM_SPEC] * len(products),
-        out_shape=[pltpu.VMEM((owners, high - low, rows), jnp.bfloat16)] * len(products),
+        out_shape=[pltpu.VMEM(shape, jnp.bfloat16)] * len(products),
         scratch_shapes=[pltpu.VMEM((len(columns), count, HALO + rows, LANES), jnp.float32)],
         cost_estimate=pl.CostEstimate(flops=1 << 10, bytes_accessed=1 << 10, transcendentals=0),
         compiler_params=pltpu.CompilerParams(vmem_limit_bytes=VMEM_LIMIT),
         name="features",
-    )(*(near if streams.ndim == 3 else far)(streams), *near(rim, taps, keep))
+    )(*given)
 
 
 def convolve_kernel(
-    first_group, group_stride, mixed_ref, rim_ref, gate_ref, skip_ref, taps_ref, keep_ref, out_ref
+    tiled, first_group, group_stride, mixed_ref, rim_ref, gate_ref, skip_ref, taps_ref, keep_ref, out_ref
 ):
     owners, count, rows = out_ref.shape
     length = taps_ref.shape[1]
@@ -264,7 +283,7 @@
                 strips = [base] + [pltpu.roll(base, shift, 1) for shift in range(GROUP, length, GROUP)]
                 circulant = jnp.concatenate(strips, 0)
                 weights = jnp.concatenate([circulant, circulant], 0) * keep_ref[...]
-                window = jnp.concatenate([rim_ref[owner, members], mixed_ref[owner, members]], 1)
+                window = jnp.concatenate([rim_ref[index if tiled else owner, members], mixed_ref[owner, members]], 1)
                 total = jnp.dot(window, weights, preferred_element_type=jnp.float32)
                 total = total + direct[unit * GROUP : (unit + 1) * GROUP]
                 total = total * gate_ref[owner, members].astype(jnp.float32)
@@ -277,17 +296,19 @@
 
 def convolve(mixed, rim, gate, skip_gain, taps, keep, first_channel, own_count):
     owners, count, rows = mixed.shape
+    tiled = first_channel > 0
     steps = min(owners, 2 if 2 * count <= own_count else 4)
+    part_spec = pl.BlockSpec((owners // steps, count, rows), lambda i: (i, 0, 0))
     return pl.pallas_call(
-        functools.partial(convolve_kernel, first_channel // GROUP, own_count // GROUP),
+        functools.partial(convolve_kernel, tiled, first_channel // GROUP, own_count // GROUP),
         grid=(steps,),
-        in_specs=[VMEM_SPEC] * 6,
-        out_specs=pl.BlockSpec((owners // steps, count, rows), lambda i: (i, 0, 0)),
+        in_specs=[VMEM_SPEC, part_spec if tiled else VMEM_SPEC] + [VMEM_SPEC] * 4,
+        out_specs=part_spec,
         out_shape=pltpu.HBM(mixed.shape, jnp.bfloat16),
         cost_estimate=pl.CostEstimate(flops=1 << 37, bytes_accessed=1 << 10, transcendentals=0),
         compiler_params=pltpu.CompilerParams(vmem_limit_bytes=VMEM_LIMIT),
         name="convolve",
-    )(*near(mixed, rim, gate), skip_gain.reshape(owners, 1, own_count), *near(taps, keep))
+    )(*near(mixed), *(far if tiled else near)(rim), *near(gate), skip_gain.reshape(owners, 1, own_count), *near(taps, keep))
 
 
 def on_device(first, second, value, short_filter, long_filter, skip_gain, lengths):
@@ -313,7 +334,9 @@
     as_rows = lambda part: part.transpose(1, 0, 2).reshape(part.shape[1], -1)
     mixed_of, gate_of = (0, 2), (1,)
     (low, cut), *rest = zip(cuts, cuts[1:])
-    mixed, gate = feature((mixed_of, gate_of), rim, low, cut)
+    both = (mixed_of, gate_of)
+    early = features(streams, both, None, short_taps, short_keep, own_count, low, cut, "early")
+    mixed, gate = features(streams, both, rim, short_taps, short_keep, own_count, low, cut, "late", early)
     rims = lax.ppermute(mixed, AXES, following)
     if not rest:
         return as_rows(relay(mix(mixed, rims, gate, low)))

time: 102 us -> 98.8 us (0.969)
  starting transfers between devices: 26 us -> 22 us
    ppermute x1, starting transfers between devices: 5.43 us -> 2.96 us  [on_device(): high_rims = lax.ppermute(high_mixed, AXES, following)]
    pallas_call x5 -> x6, Pallas kernels: 29.6 us -> 30.2 us  [the longest x4 16.1 us: features(): pl.pallas_call(functools.partial(feature_kernel, phase, products, keep.sh...]
  transfers between devices with their start and end apart: 5 -> 5, of which waited for: 2 -> 2; matrix products, arithmetic and copies ran while one was open for 1% -> 1% of each run, Pallas kernels for 28% -> 33%
where the time goes in v5:
time: 98.8 us; the launch traced here: 98.2 us
  waiting for transfers between devices  38.2 us (39%)
  Pallas kernels  35.1 us (36%)
  starting transfers between devices  22 us (22%)
  other arithmetic  1.46 us (1%)
  local copies, waits for them, and re-layouts  1.35 us (1%)
    all_to_all x2, waiting for transfers between devices, on_device(): relay = lambda part: lax.all_to_all(part, AXES, 0, 0, tiled=True)  38.1 us
    pallas_call x4, Pallas kernels, features(): pl.pallas_call(functools.partial(feature_kernel, phase, products, keep.sh...  16.1 us
    pallas_call x2, Pallas kernels, convolve(): pl.pallas_call(functools.partial(convolve_kernel, tiled, first_channel //...  14.1 us
    all_to_all x2, starting transfers between devices, on_device(): relay = lambda part: lax.all_to_all(part, AXES, 0, 0, tiled=True)  12.1 us
    ppermute x1, starting transfers between devices, on_device(): rims = lax.ppermute(mixed, AXES, following)  4.53 us
    pallas_call x1, Pallas kernels, prepare(): pl.pallas_call(functools.partial(prepare_kernel, tile), in_specs=[SMEM_SP...  3.7 us
    ppermute x1, starting transfers between devices, on_device(): high_rims = lax.ppermute(high_mixed, AXES, following)  2.96 us
    ppermute x1, starting transfers between devices, on_device(): rim = lax.ppermute(last, AXES, following)  2.39 us
  transfers between devices with their start and end apart: 5, of which 2 were waited for; matrix products, arithmetic and copies ran while one was open for 1% of the time, Pallas kernels for 33%

profile of v5, /device:TPU:0, one launch (start us, length us, event | category | flops | bytes accessed | tf_op | source)
XLA Modules:
  0.0 98.2 jit_solution(9735991027915115544)
XLA Ops:
  0.0 0.0 copy-start.2
  0.0 0.0 copy-start
  0.0 0.0 copy-start.1
  0.0 1.2 %last_rows.1 = bf16[3,8,8192]{2,1,0:T(8,128)(2,1)S(1)} custom-call(bf16[128,8192]{1,0:T(8,128)(2,1)} %first_ref.1, bf16[128,8192]{1,0:T(8,128)(2,1)} %refs_0_.3, bf16[128,8192]{1,0:T(8,128)(2,1)} %value_ref.1), custom_call_target="tpu_custom_call" | custom-call | tf_op jit(solution)/shard_map/last_rows/pallas_call | solution.py:118
  1.2 2.4 %collective-permute-start = (bf16[3,8,8192]{2,1,0:T(8,128)(2,1)S(1)}, bf16[3,8,8192]{2,1,0:T(8,128)(2,1)S(1)}, u32[]{:S(2)}, u32[]{:S(2)}) collective-permute-start(bf16[3,8,8192]{2,1,0:T(8,128)(2,1)S(1)} %last_rows.1), channel_id=1, source_target_pairs={{0,1},{1,2},{2,3},{3,4},{4,5},{5,6},{6,7},{7,8},{8,9},{9,10},{10,1... | collective-permute-start | bytes 1179656 | tf_op jit(solution)/shard_map/ppermute | solution.py:323
  3.6 0.0 copy-done.2
  3.6 0.0 copy-done
  3.6 0.0 copy-done.1
  3.6 3.7 %prepare.1 = (f32[6,128,128]{2,1,0:T(8,128)S(1)}, bf16[256,128]{1,0:T(8,128)(2,1)S(1)}, f32[512,128]{1,0:T(8,128)S(1)}, f32[3,8,8192]{2,1,0:T(8,128)S(1)}, bf16[3,128,8192]{2,1,0:T(8,128)(2,1)S(1)}) custom-call(s32[1]{0:T(128)} %bitcast.place_ref, s32[16]{0:T(128)S(1)} %copy-done.2, bf16[3,7,512]{2,1,0:T(8,128)(2,1)S(1)} %copy-done.1, ...), custom_call_target="tpu_custom_call" | custom-call | flops 1024 | bytes 1024 | tf_op jit(solution)/shard_map/prepare/pallas_call | solution.py:90
  7.3 4.3 %features.4 = (bf16[112,3072]{1,0:T(8,128)(2,1)S(1)}, bf16[112,3072]{1,0:T(8,128)(2,1)S(1)}) custom-call(bf16[3,128,8192]{2,1,0:T(8,128)(2,1)S(1)} %get-tuple-element.19.refs_0_, f32[3,8,8192]{2,1,0:T(8,128)S(1)} %get-tuple-element.20.refs_1_, f32[6,128,128]{2,1,0:T(8,128)S(1)} %get-tuple-element.21.refs_2_), custom_call_target="tpu_custom_call" | custom-call | flops 1024 | bytes 1024 | tf_op jit(solution)/shard_map/features/pallas_call | solution.py:241
  11.6 0.0 collective-permute-done.refs_3_
  11.7 1.6 %features.5 = (bf16[32,96,128]{2,1,0:T(8,128)(2,1)S(1)}, bf16[32,96,128]{2,1,0:T(8,128)(2,1)S(1)}) custom-call(bf16[3,128,8192]{2,1,0:T(8,128)(2,1)S(1)} %get-tuple-element.19.refs_0_, f32[3,8,8192]{2,1,0:T(8,128)S(1)} %get-tuple-element.20.refs_1_, f32[6,128,128]{2,1,0:T(8,128)S(1)} %get-tuple-element.21.refs_2_, ...), custom_call_target="tpu_custom_call" | custom-call | flops 1024 | bytes 1024 | tf_op jit(solution)/shard_map/features/pallas_call | solution.py:241
  13.2 0.0 copy-start.3
  13.3 4.5 %collective-permute-start.1 = (bf16[32,96,128]{2,1,0:T(8,128)(2,1)S(1)}, bf16[32,96,128]{2,1,0:T(8,128)(2,1)S(1)}, u32[]{:S(2)}, u32[]{:S(2)}) collective-permute-start(bf16[32,96,128]{2,1,0:T(8,128)(2,1)S(1)} %get-tuple-element.25.mixed_ref), channel_id=1, source_target_pairs={{0,1},{1,2},{2,3},{3,4},{4,5},{5,6},{6,7},{7,8},{8,9},{9,10},{10,1... | collective-permute-start | bytes 2359304 | tf_op jit(solution)/shard_map/ppermute | solution.py:340
  17.8 5.8 %features.6.mixed_ref = bf16[32,160,128]{2,1,0:T(8,128)(2,1)S(1)} custom-call(bf16[3,128,8192]{2,1,0:T(8,128)(2,1)S(1)} %get-tuple-element.19.refs_0_, f32[3,8,8192]{2,1,0:T(8,128)S(1)} %get-tuple-element.20.refs_1_, f32[6,128,128]{2,1,0:T(8,128)S(1)} %get-tuple-element.21.refs_2_, bf16[3,8,8192]{2,1,0:T(8,128)(2,1)S(1)} %collective-permute-done.refs_3_), custom_call_target="tpu_custom_call" | custom-call | flops 1024 | bytes 1024 | tf_op jit(solution)/shard_map/features/pallas_call | solution.py:241
  23.6 3.0 %collective-permute-start.2 = (bf16[32,160,128]{2,1,0:T(8,128)(2,1)S(1)}, bf16[32,160,128]{2,1,0:T(8,128)(2,1)}, u32[]{:S(2)}, u32[]{:S(2)}) collective-permute-start(bf16[32,160,128]{2,1,0:T(8,128)(2,1)S(1)} %features.6.mixed_ref), channel_id=1, source_target_pairs={{0,1},{1,2},{2,3},{3,4},{4,5},{5,6},{6,7},{7,8},{8,9},{9,10},{10,1... | collective-permute-start | bytes 3932168 | tf_op jit(solution)/shard_map/ppermute | solution.py:346
  26.5 0.0 collective-permute-done.1.rim_ref
  26.5 0.0 copy-done.3
  26.5 5.2 %convolve.2 = bf16[32,96,128]{2,1,0:T(8,128)(2,1)} custom-call(bf16[32,96,128]{2,1,0:T(8,128)(2,1)S(1)} %get-tuple-element.25.mixed_ref, bf16[32,96,128]{2,1,0:T(8,128)(2,1)S(1)} %collective-permute-done.1.rim_ref, bf16[32,96,128]{2,1,0:T(8,128)(2,1)S(1)} %get-tuple-element.26.gate_ref, f32[32,1,256]{2,1,0:T(1,128)S(1)} %bitcast.14, ...), custom_call_target="tpu_custom_call" | custom-call | flops 137438953472 | bytes 1024 | tf_op jit(solution)/shard_map/convolve/pallas_call | solution.py:302
  31.7 7.8 %all-to-all-start = ((bf16[32,96,128]{2,1,0:T(8,128)(2,1)}), bf16[32,96,128]{2,1,0:T(8,128)(2,1)}, u32[]{:S(2)}, u32[]{:S(2)}) async-start(bf16[32,96,128]{2,1,0:T(8,128)(2,1)} %convolve.2), calls=%async_computation | async-start | bytes 1572864 | tf_op jit(solution)/shard_map/all_to_all | solution.py:333
  39.5 4.5 %features.7.gate_ref = bf16[32,160,128]{2,1,0:T(8,128)(2,1)S(1)} custom-call(bf16[128,8192]{1,0:T(8,128)(2,1)} %refs_0_.3, f32[3,8,8192]{2,1,0:T(8,128)S(1)} %get-tuple-element.20.refs_1_, f32[6,128,128]{2,1,0:T(8,128)S(1)} %get-tuple-element.21.refs_2_, bf16[3,8,8192]{2,1,0:T(8,128)(2,1)S(1)} %collective-permute-done.refs_3_), custom_call_target="tpu_custom_call" | custom-call | flops 1024 | bytes 1024 | tf_op jit(solution)/shard_map/features/pallas_call | solution.py:241
  44.0 0.0 collective-permute-done.2.rim_ref
  44.0 8.9 %convolve.3 = bf16[32,160,128]{2,1,0:T(8,128)(2,1)} custom-call(bf16[32,160,128]{2,1,0:T(8,128)(2,1)S(1)} %features.6.mixed_ref, bf16[32,160,128]{2,1,0:T(8,128)(2,1)} %collective-permute-done.2.rim_ref, bf16[32,160,128]{2,1,0:T(8,128)(2,1)S(1)} %features.7.gate_ref, f32[32,1,256]{2,1,0:T(1,128)S(1)} %bitcast.15, f32[512,128]{1,0:T(8,128)S(1)} %get-tuple-element.27.taps_ref, ...), custom_call_target="tpu_custom_call" | custom-call | flops 137438953472 | bytes 1024 | tf_op jit(solution)/shard_map/convolve/pallas_call | solution.py:302
  52.9 7.2 %all-to-all-done = bf16[32,96,128]{2,1,0:T(8,128)(2,1)} async-done(((bf16[32,96,128]{2,1,0:T(8,128)(2,1)}), bf16[32,96,128]{2,1,0:T(8,128)(2,1)}, u32[]{:S(2)}, u32[]{:S(2)}) %all-to-all-start) | async-done | bytes 786464 | tf_op jit(solution)/shard_map/all_to_all | solution.py:333
  60.1 4.4 %all-to-all-start.1 = ((bf16[32,160,128]{2,1,0:T(8,128)(2,1)}), bf16[32,160,128]{2,1,0:T(8,128)(2,1)S(1)}, u32[]{:S(2)}, u32[]{:S(2)}) async-start(bf16[32,160,128]{2,1,0:T(8,128)(2,1)} %convolve.3), calls=%async_computation.1 | async-start | bytes 2621440 | tf_op jit(solution)/shard_map/all_to_all | solution.py:333
  64.5 1.2 %copy_bitcast_fusion.1 = bf16[96,4096]{1,0:T(8,128)(2,1)S(1)} fusion(bf16[32,96,128]{2,1,0:T(8,128)(2,1)} %all-to-all-done), kind=kLoop, calls=%fused_computation.2 | loop fusion | bytes 1572864 | tf_op jit(solution)/shard_map/reshape | solution.py:334
  65.7 30.9 %all-to-all-done.1 = bf16[32,160,128]{2,1,0:T(8,128)(2,1)S(1)} async-done(((bf16[32,160,128]{2,1,0:T(8,128)(2,1)}), bf16[32,160,128]{2,1,0:T(8,128)(2,1)S(1)}, u32[]{:S(2)}, u32[]{:S(2)}) %all-to-all-start.1) | async-done | bytes 1310752 | tf_op jit(solution)/shard_map/all_to_all | solution.py:333
  96.6 0.1 copy_bitcast_fusion
  96.8 1.5 %pad_maximum_fusion = bf16[256,4096]{1,0:T(8,128)(2,1)} fusion(bf16[160,4096]{1,0:T(8,128)(2,1)S(1)} %copy_bitcast_fusion, bf16[96,4096]{1,0:T(8,128)(2,1)S(1)} %copy_bitcast_fusion.1), kind=kLoop, calls=%fused_computation | loop fusion | flops 4194304 | bytes 4194304 | tf_op jit(solution)/shard_map/concatenate | solution.py:352
Async XLA Ops:
  0.0 3.6 %copy-start.2 = (s32[16]{0:T(128)S(1)}, s32[16]{0:T(128)}, u32[]{:S(2)}) copy-start(s32[16]{0:T(128)} %lengths_ref) | copy-start | bytes 196
  0.0 3.6 %copy-start = (bf16[128,512]{1,0:T(8,128)(2,1)S(1)}, bf16[128,512]{1,0:T(8,128)(2,1)}, u32[]{:S(2)}) copy-start(bf16[128,512]{1,0:T(8,128)(2,1)} %long_ref.1) | copy-start | bytes 393220
  0.0 3.6 %copy-start.1 = (bf16[3,7,512]{2,1,0:T(8,128)(2,1)S(1)}, bf16[3,7,512]{2,1,0:T(8,128)(2,1)}, u32[]{:S(2)}) copy-start(bf16[3,7,512]{2,1,0:T(8,128)(2,1)} %short_ref.1) | copy-start | bytes 64516
  1.2 10.5 %collective-permute-start = (bf16[3,8,8192]{2,1,0:T(8,128)(2,1)S(1)}, bf16[3,8,8192]{2,1,0:T(8,128)(2,1)S(1)}, u32[]{:S(2)}, u32[]{:S(2)}) collective-permute-start(bf16[3,8,8192]{2,1,0:T(8,128)(2,1)S(1)} %last_rows.1), channel_id=1, source_target_pairs={{0,1},{1,2},{2,3},{3,4},{4,5},{5,6},{6,7},{7,8},{8,9},{9,10},{10,1... | collective-permute-start | bytes 1179656 | tf_op jit(solution)/shard_map/ppermute | solution.py:323
  13.2 13.3 %copy-start.3 = (f32[8192]{0:T(1024)S(1)}, f32[8192]{0:T(1024)}, u32[]{:S(2)}) copy-start(f32[8192]{0:T(1024)} %param.12) | copy-start | bytes 98308
  13.3 13.3 %collective-permute-start.1 = (bf16[32,96,128]{2,1,0:T(8,128)(2,1)S(1)}, bf16[32,96,128]{2,1,0:T(8,128)(2,1)S(1)}, u32[]{:S(2)}, u32[]{:S(2)}) collective-permute-start(bf16[32,96,128]{2,1,0:T(8,128)(2,1)S(1)} %get-tuple-element.25.mixed_ref), channel_id=1, source_target_pairs={{0,1},{1,2},{2,3},{3,4},{4,5},{5,6},{6,7},{7,8},{8,9},{9,10},{10,1... | collective-permute-start | bytes 2359304 | tf_op jit(solution)/shard_map/ppermute | solution.py:340
  23.6 20.4 %collective-permute-start.2 = (bf16[32,160,128]{2,1,0:T(8,128)(2,1)S(1)}, bf16[32,160,128]{2,1,0:T(8,128)(2,1)}, u32[]{:S(2)}, u32[]{:S(2)}) collective-permute-start(bf16[32,160,128]{2,1,0:T(8,128)(2,1)S(1)} %features.6.mixed_ref), channel_id=1, source_target_pairs={{0,1},{1,2},{2,3},{3,4},{4,5},{5,6},{6,7},{7,8},{8,9},{9,10},{10,1... | collective-permute-start | bytes 3932168 | tf_op jit(solution)/shard_map/ppermute | solution.py:346
  31.7 28.4 %all-to-all-start = ((bf16[32,96,128]{2,1,0:T(8,128)(2,1)}), bf16[32,96,128]{2,1,0:T(8,128)(2,1)}, u32[]{:S(2)}, u32[]{:S(2)}) async-start(bf16[32,96,128]{2,1,0:T(8,128)(2,1)} %convolve.2), calls=%async_computation | async-start | bytes 1572864 | tf_op jit(solution)/shard_map/all_to_all | solution.py:333
  60.1 36.5 %all-to-all-start.1 = ((bf16[32,160,128]{2,1,0:T(8,128)(2,1)}), bf16[32,160,128]{2,1,0:T(8,128)(2,1)S(1)}, u32[]{:S(2)}, u32[]{:S(2)}) async-start(bf16[32,160,128]{2,1,0:T(8,128)(2,1)} %convolve.3), calls=%async_computation.1 | async-start | bytes 2621440 | tf_op jit(solution)/shard_map/all_to_all | solution.py:333

commit v6 on v5

--- a/solution.py
+++ b/solution.py
@@ -13,7 +13,6 @@
 HALO = 8
 CUTS = (0, 96, 256)
 VMEM_LIMIT = 24 << 20
-UNROLL = 4
 
 
 def begins_of(position, lengths_ref):
@@ -26,9 +25,10 @@
 
 
 def prepare_kernel(
-    tile, place_ref, lengths_ref, short_ref, long_ref, first_ref, second_ref, value_ref,
-    short_keep_ref, long_keep_ref, long_taps_ref, short_taps_ref, near_ref, spread_ref, arrived
+    tile, near_count, place_ref, lengths_ref, short_ref, long_ref, *refs
 ):
+    stream_refs, refs = refs[:near_count], refs[near_count:]
+    short_keep_ref, long_keep_ref, long_taps_ref, short_taps_ref, near_ref, spread_ref, arrived = refs
     streams, tap_count, groups = short_ref.shape
     length = long_ref.shape[0]
     rows = long_keep_ref.shape[1]
@@ -38,7 +38,7 @@
         pltpu.make_async_copy(
             ref.at[pl.ds(piece * size, size)], near_ref.at[index, pl.ds(piece * size, size)], arrived.at[index, piece]
         )
-        for index, ref in enumerate((first_ref, second_ref, value_ref))
+        for index, ref in enumerate(stream_refs)
         for piece in range(pieces)
     ]
     for copy in copies:
@@ -88,19 +88,19 @@
     rows, channels = streams[0].shape
     tile = min(2048, channels)
     return pl.pallas_call(
-        functools.partial(prepare_kernel, tile),
-        in_specs=[SMEM_SPEC] * 2 + [VMEM_SPEC] * 2 + [pl.BlockSpec(memory_space=pltpu.HBM)] * count,
+        functools.partial(prepare_kernel, tile, len(streams)),
+        in_specs=[SMEM_SPEC] * 2 + [VMEM_SPEC] * 2 + [pl.BlockSpec(memory_space=pltpu.HBM)] * len(streams),
         out_specs=[VMEM_SPEC] * 5,
         out_shape=[
             pltpu.VMEM((tap_count - 1, rows, LANES), jnp.float32),
             pltpu.VMEM((2 * rows, rows), jnp.bfloat16),
             pltpu.VMEM(long_filter.shape[::-1], jnp.float32),
             pltpu.VMEM((count, 8, channels), jnp.float32),
-            pltpu.VMEM((count, rows, channels), jnp.bfloat16),
+            pltpu.VMEM((len(streams), rows, channels), jnp.bfloat16),
         ],
         scratch_shapes=[
             pltpu.VMEM((tile // GROUP, tile), jnp.bfloat16),
-            pltpu.SemaphoreType.DMA((count, 4)),
+            pltpu.SemaphoreType.DMA((len(streams), 4)),
         ],
         cost_estimate=pl.CostEstimate(flops=1 << 10, bytes_accessed=1 << 10, transcendentals=0),
         compiler_params=pltpu.CompilerParams(vmem_limit_bytes=VMEM_LIMIT),
@@ -148,107 +148,128 @@
     return columns + [[piece] for piece in whole]
 
 
-def feature_kernel(phase, products, tap_count, own_count, low, columns, *refs):
-    chosen = sorted({stream for product in products for stream in product})
-    streams_ref, taps_ref, keep_ref, *refs, padded_ref = refs
+def feature_kernel(phase, jobs, tap_count, own_count, bundle, places, *refs):
+    streams_ref, taps_ref, keep_ref, *refs = refs
     rim_ref, refs = (None, refs) if phase == "early" else (refs[0], refs[1:])
-    early_refs, out_refs = (refs[: len(products)] if phase == "late" else ()), refs[-len(products) :]
+    early_ref, refs = (refs[0], refs[1:]) if phase == "late" else (None, refs)
+    far_ref, refs = (refs[0], refs[1:]) if None in places else (None, refs)
+    out_refs, padded_ref, refs = refs[: len(jobs)], refs[len(jobs)], refs[len(jobs) + 1 :]
     rows, tile = streams_ref.shape[-2:]
     tiled = len(streams_ref.shape) == 2
-    bundle = 1 + max(piece[0] for column in columns for piece in column)
     width = bundle * own_count
     strip = 16
-
-    def one_bundle(index, _):
-        bundle_index = pl.program_id(0) * (tile // width) + index
-
-        def column_of(ref, column, *at):
-            base = (index if len(ref.shape) == 2 else bundle_index) * width
-            spans, pieces = [], []
-            for owner, first, last in column:
-                start = owner * own_count + first
-                if spans and spans[-1][1] == start:
-                    spans[-1][1] += last - first
-                else:
-                    spans.append([start, start + last - first])
-            for start, end in spans:
-                floor = start // LANES * LANES
-                value = ref[*at, pl.ds(pl.multiple_of(base + floor, LANES), LANES)]
-                pieces.append(value[:, start - floor : end - floor])
-            return pieces[0] if len(pieces) == 1 else jnp.concatenate(pieces, 1)
-
-        taps = {}
-        for number, column in enumerate(columns):
-            for stream in chosen:
-                at = [] if tiled else [stream]
-                own = column_of(streams_ref, column, *at, slice(0, strip if phase == "late" else rows))
-                padded_ref[number, stream, HALO : HALO + own.shape[0]] = own.astype(jnp.float32)
-                if phase != "early":
-                    rim = column_of(rim_ref, column, stream, slice(None)).astype(jnp.float32)
-                    padded_ref[number, stream, :HALO] = rim
-                taps[number, stream] = column_of(taps_ref, column, stream, slice(None))
-        results = [[[] for _ in columns] for _ in products]
-        for row in range(strip if phase == "early" else 0, strip if phase == "late" else rows, strip):
-            keep = [keep_ref[tap, pl.ds(row, strip)] for tap in range(tap_count - 1)]
-            for number in range(len(columns)):
-                for which, product in enumerate(products):
+    if far_ref is not None:
+        brought = pltpu.make_async_copy(far_ref, refs[0], refs[1])
+        brought.start()
+
+    def run(job, out_ref):
+        product, low, columns = job
+
+        def one_bundle(index, _):
+            bundle_index = pl.program_id(0) * (tile // width) + index
+
+            def column_of(ref, column, *at):
+                base = (index if len(ref.shape) == 2 else bundle_index) * width
+                spans, pieces = [], []
+                for owner, first, last in column:
+                    start = owner * own_count + first
+                    if spans and spans[-1][1] == start:
+                        spans[-1][1] += last - first
+                    else:
+                        spans.append([start, start + last - first])
+                for start, end in spans:
+                    floor = start // LANES * LANES
+                    value = ref[*at, pl.ds(pl.multiple_of(base + floor, LANES), LANES)]
+                    pieces.append(value[:, start - floor : end - floor])
+                return pieces[0] if len(pieces) == 1 else jnp.concatenate(pieces, 1)
+
+            taps = {}
+            for number, column in enumerate(columns):
+                for slot, stream in enumerate(product):
+                    held = slice(0, strip if phase == "late" else rows)
+                    if tiled:
+                        own = column_of(streams_ref, column, held)
+                    elif places[stream] is None:
+                        own = column_of(refs[0], column, held)
+                    else:
+                        own = column_of(streams_ref, column, places[stream], held)
+                    padded_ref[number, slot, HALO : HALO + own.shape[0]] = own.astype(jnp.float32)
+                    if phase != "early":
+                        rim = column_of(rim_ref, column, stream, slice(None)).astype(jnp.float32)
+                        padded_ref[number, slot, :HALO] = rim
+                    taps[number, slot] = column_of(taps_ref, column, stream, slice(None))
+            results = [[] for _ in columns]
+            for row in range(strip if phase == "early" else 0, strip if phase == "late" else rows, strip):
+                keep = [keep_ref[tap, pl.ds(row, strip)] for tap in range(tap_count - 1)]
+                for number in range(len(columns)):
                     value = None
-                    for stream in product:
-                        tap_of = lambda tap: taps[number, stream][tap : tap + 1]
-                        total = tap_of(0) * padded_ref[number, stream, pl.ds(HALO + row, strip)]
+                    for slot in range(len(product)):
+                        tap_of = lambda tap: taps[number, slot][tap : tap + 1]
+                        total = tap_of(0) * padded_ref[number, slot, pl.ds(HALO + row, strip)]
                         for tap in range(1, tap_count):
-                            term = tap_of(tap) * padded_ref[number, stream, pl.ds(HALO + row - tap, strip)]
+                            term = tap_of(tap) * padded_ref[number, slot, pl.ds(HALO + row - tap, strip)]
                             total = total + keep[tap - 1] * term
                         value = total if value is None else value * total
-                    results[which][number].append(value.astype(jnp.bfloat16))
-        for which in range(len(products)):
+                    results[number].append(value.astype(jnp.bfloat16))
             for number, column in enumerate(columns):
-                value = results[which][number]
+                value = results[number]
                 lanes = pl.ds(pl.multiple_of((bundle_index * len(columns) + number) * LANES, LANES), LANES)
                 if phase == "early":
-                    out_refs[which][:, lanes] = jnp.concatenate(value, 0)
+                    out_ref[:, lanes] = jnp.concatenate(value, 0)
                     continue
                 if phase == "late":
-                    value = value + [early_refs[which][:, lanes]]
+                    value = value + [early_ref[:, lanes]]
                 value = jnp.concatenate(value, 0).T
                 row = 0
                 for owner, first, last in column:
                     place = (bundle_index * bundle + owner, pl.ds(first - low, last - first))
-                    out_refs[which][place] = value[row : row + last - first]
+                    out_ref[place] = value[row : row + last - first]
                     row += last - first
-        return 0
-
-    lax.fori_loop(0, tile // width, one_bundle, 0, unroll=UNROLL if phase == "late" else 1)
-
-
-def features(streams, products, rim, taps, keep, own_count, low, high, phase="whole", early=()):
+            return 0
+
+        lax.fori_loop(0, tile // width, one_bundle, 0, unroll=4 if phase == "late" else 2)
+
+    for job, out_ref in zip(jobs, out_refs):
+        if far_ref is not None and None in [places[stream] for stream in job[0]]:
+            brought.wait()
+        run(job, out_ref)
+
+
+def features(streams, places, jobs, rim, taps, keep, own_count, phase="whole", early=(), distant=()):
     rows, channels = streams.shape[-2:]
-    count = taps.shape[0]
     owners = channels // own_count
     tiles = 1 if streams.ndim == 3 else max(1, channels // 2048)
     stream_spec = VMEM_SPEC
     if streams.ndim == 2:
         stream_spec = pl.BlockSpec((rows, channels // tiles), lambda i: (0, i))
-    bundle = max(1, LANES // (high - low))
-    while bundle * (high - low) % LANES:
+    bundle = max(1, LANES // own_count)
+    while any(bundle * (high - low) % LANES for _, low, high in jobs):
         bundle += 1
-    if len(gathered(bundle, own_count, low, high)) == 1:
+    if max(bundle * (high - low) for _, low, high in jobs) == LANES:
         bundle *= 2
-    columns = gathered(bundle, own_count, low, high)
-    shape = (rows - 16, owners * (high - low)) if phase == "early" else (owners, high - low, rows)
+    found = [(product, low, gathered(bundle, own_count, low, high)) for product, low, high in jobs]
+    shapes = [
+        (rows - 16, owners * (high - low)) if phase == "early" else (owners, high - low, rows) for _, low, high in jobs
+    ]
     given = [*(near if streams.ndim == 3 else far)(streams), *near(taps, keep)]
     given += near(*([] if phase == "early" else [rim]), *early)
+    width = max(len(product) for product, _, _ in jobs)
+    scratch = [pltpu.VMEM((max(len(job[2]) for job in found), width, HALO + rows, LANES), jnp.float32)]
+    if distant:
+        scratch += [pltpu.VMEM((rows, channels), jnp.bfloat16), pltpu.SemaphoreType.DMA]
     return pl.pallas_call(
-        functools.partial(feature_kernel, phase, products, keep.shape[0] + 1, own_count, low, columns),
+        functools.partial(feature_kernel, phase, found, keep.shape[0] + 1, own_count, bundle, places),
         grid=(tiles,),
-        in_specs=[stream_spec] + [VMEM_SPEC] * (len(given) - 1),
-        out_specs=[VMEM_SPEC] * len(products),
-        out_shape=[pltpu.VMEM(shape, jnp.bfloat16)] * len(products),
-        scratch_shapes=[pltpu.VMEM((len(columns), count, HALO + rows, LANES), jnp.float32)],
+        in_specs=[stream_spec]
+        + [VMEM_SPEC] * (len(given) - 1)
+        + [pl.BlockSpec(memory_space=pltpu.HBM)] * len(distant),
+        out_specs=[VMEM_SPEC] * len(jobs),
+        out_shape=[pltpu.VMEM(shape, jnp.bfloat16) for shape in shapes],
+        scratch_shapes=scratch,
         cost_estimate=pl.CostEstimate(flops=1 << 10, bytes_accessed=1 << 10, transcendentals=0),
         compiler_params=pltpu.CompilerParams(vmem_limit_bytes=VMEM_LIMIT),
         name="features",
-    )(*given)
+    )(*given, *far(*distant))
 
 
 def convolve_kernel(
@@ -322,34 +343,39 @@
     last, lengths = lax.optimization_barrier((last_rows(streams), lengths))
     rim = lax.ppermute(last, AXES, following)
     short_keep, long_keep, long_taps, short_taps, streams = prepare(
-        place, lengths, short_filter, long_filter, streams
+        place, lengths, short_filter, long_filter, (first, second, value)
     )
-    feature = lambda products, rim, low, high: features(
-        streams, products, rim, short_taps, short_keep, own_count, low, high
-    )
+    tables = (short_taps, short_keep, own_count)
     mix = lambda mixed, rims, gate, low: convolve(
         mixed, rims, gate, skip_gain, long_taps, long_keep, low, own_count
     )
     relay = lambda part: lax.all_to_all(part, AXES, 0, 0, tiled=True)
     as_rows = lambda part: part.transpose(1, 0, 2).reshape(part.shape[1], -1)
-    mixed_of, gate_of = (0, 2), (1,)
+    places, mixed_of, gate_of = (0, None, 1), (0, 2), (1,)
     (low, cut), *rest = zip(cuts, cuts[1:])
-    both = (mixed_of, gate_of)
-    early = features(streams, both, None, short_taps, short_keep, own_count, low, cut, "early")
-    mixed, gate = features(streams, both, rim, short_taps, short_keep, own_count, low, cut, "late", early)
+    jobs = ((mixed_of, low, cut),)
+    early = features(streams, (0, 1, 2), jobs, None, *tables, "early")
+    (mixed,) = features(streams, (0, 1, 2), jobs, rim, *tables, "late", early)
     rims = lax.ppermute(mixed, AXES, following)
     if not rest:
+        (gate,) = features(second, (0, 0, 0), ((gate_of, low, cut),), rim, *tables)
         return as_rows(relay(mix(mixed, rims, gate, low)))
 
     rim, _ = lax.optimization_barrier((rim, mixed))
-    (high_mixed,) = feature((mixed_of,), rim, cut, own_count)
+    jobs = ((mixed_of, cut, own_count),)
+    (high_mixed,) = features(streams, (0, 1, 2), jobs, rim, *tables)
     high_rims = lax.ppermute(high_mixed, AXES, following)
+    rim, _ = lax.optimization_barrier((rim, high_mixed))
+    (gate,) = features(streams, (0, 1, 2), ((gate_of, low, cut),), rim, *tables)
     low_part = mix(mixed, rims, gate, low)
     rim, _ = lax.optimization_barrier((rim, low_part))
     low_part = relay(low_part)
-    (high_gate,) = features(second, (gate_of,), rim, short_taps, short_keep, own_count, cut, own_count)
+    (high_gate,) = features(second, (0, 0, 0), ((gate_of, cut, own_count),), rim, *tables)
+    whole = jnp.zeros((own_count, devices * rows), jnp.bfloat16)
+    whole = lax.dynamic_update_slice(whole, as_rows(low_part), (low, 0))
     high_part = relay(mix(high_mixed, high_rims, high_gate, cut))
-    return jnp.concatenate([as_rows(low_part), as_rows(high_part)], 0)
+    whole = lax.optimization_barrier(whole)
+    return lax.dynamic_update_slice(whole, as_rows(high_part), (cut, 0))
 
 
 def solution(mesh):

time: 98.8 us -> 97.8 us (0.990)
  local copies, waits for them, and re-layouts: 1.35 us -> 3.95 us
  other arithmetic: 1.46 us -> 0 us
  waiting for transfers between devices: 38.2 us -> 36.9 us
  Pallas kernels: 35.1 us -> 34 us
    dynamic_update_slice x0 -> x2, local copies, waits for them, and re-layouts: none -> 2.73 us  [the longest x1 1.53 us: on_device(): whole = lax.dynamic_update_slice(whole, as_rows(low_part), (low, 0))]
    concatenate x1 -> x0, other arithmetic: 1.46 us -> none  [on_device(): return jnp.concatenate([as_rows(low_part), as_rows(high_part)], 0)]
    all_to_all x2, waiting for transfers between devices: 38.1 us -> 36.9 us  [on_device(): relay = lambda part: lax.all_to_all(part, AXES, 0, 0, tiled=True)]
    pallas_call x5 -> x6, Pallas kernels: 19.8 us -> 18.7 us  [the longest x5 15 us: features(): pl.pallas_call(functools.partial(feature_kernel, phase, found, keep.shape...]
  transfers between devices with their start and end apart: 5 -> 5, of which waited for: 2 -> 2; matrix products, arithmetic and copies ran while one was open for 1% -> 3% of each run, Pallas kernels for 33% -> 33%
where the time goes in v6:
time: 97.8 us; the launch traced here: 97.2 us
  waiting for transfers between devices  36.9 us (38%)
  Pallas kernels  34 us (35%)
  starting transfers between devices  22.2 us (23%)
  local copies, waits for them, and re-layouts  3.95 us (4%)
    all_to_all x2, waiting for transfers between devices, on_device(): relay = lambda part: lax.all_to_all(part, AXES, 0, 0, tiled=True)  36.9 us
    pallas_call x5, Pallas kernels, features(): pl.pallas_call(functools.partial(feature_kernel, phase, found, keep.shape...  15 us
    pallas_call x2, Pallas kernels, convolve(): pl.pallas_call(functools.partial(convolve_kernel, tiled, first_channel //...  14.2 us
    all_to_all x2, starting transfers between devices, on_device(): relay = lambda part: lax.all_to_all(part, AXES, 0, 0, tiled=True)  11.8 us
    ppermute x1, starting transfers between devices, on_device(): rims = lax.ppermute(mixed, AXES, following)  4.53 us
    pallas_call x1, Pallas kernels, prepare(): pl.pallas_call(functools.partial(prepare_kernel, tile, len(streams)), in_...  3.7 us
    ppermute x1, starting transfers between devices, on_device(): high_rims = lax.ppermute(high_mixed, AXES, following)  3.5 us
    ppermute x1, starting transfers between devices, on_device(): rim = lax.ppermute(last, AXES, following)  2.39 us
  transfers between devices with their start and end apart: 5, of which 2 were waited for; matrix products, arithmetic and copies ran while one was open for 3% of the time, Pallas kernels for 33%

profile of v6, /device:TPU:0, one launch (start us, length us, event | category | flops | bytes accessed | tf_op | source)
XLA Modules:
  0.0 97.2 jit_solution(6666306794096358705)
XLA Ops:
  0.0 0.0 copy-start.2
  0.0 0.0 copy-start.1
  0.0 0.0 copy-start
  0.0 1.2 %last_rows.1 = bf16[3,8,8192]{2,1,0:T(8,128)(2,1)S(1)} custom-call(bf16[128,8192]{1,0:T(8,128)(2,1)} %refs_0_.4, bf16[128,8192]{1,0:T(8,128)(2,1)} %refs_0_.5, bf16[128,8192]{1,0:T(8,128)(2,1)} %refs_2_.3), custom_call_target="tpu_custom_call" | custom-call | tf_op jit(solution)/shard_map/last_rows/pallas_call | solution.py:118
  1.2 2.4 %collective-permute-start = (bf16[3,8,8192]{2,1,0:T(8,128)(2,1)S(1)}, bf16[3,8,8192]{2,1,0:T(8,128)(2,1)S(1)}, u32[]{:S(2)}, u32[]{:S(2)}) collective-permute-start(bf16[3,8,8192]{2,1,0:T(8,128)(2,1)S(1)} %last_rows.1), channel_id=1, source_target_pairs={{0,1},{1,2},{2,3},{3,4},{4,5},{5,6},{6,7},{7,8},{8,9},{9,10},{10,1... | collective-permute-start | bytes 1179656 | tf_op jit(solution)/shard_map/ppermute | solution.py:344
  3.6 0.0 copy-done.2
  3.6 0.0 copy-done.1
  3.6 0.0 copy-done
  3.6 3.7 %prepare.1 = (f32[6,128,128]{2,1,0:T(8,128)S(1)}, bf16[256,128]{1,0:T(8,128)(2,1)S(1)}, f32[512,128]{1,0:T(8,128)S(1)}, f32[3,8,8192]{2,1,0:T(8,128)S(1)}, bf16[3,128,8192]{2,1,0:T(8,128)(2,1)S(1)}) custom-call(s32[1]{0:T(128)} %bitcast.place_ref, s32[16]{0:T(128)S(1)} %copy-done.2, bf16[3,7,512]{2,1,0:T(8,128)(2,1)S(1)} %copy-done.1, ...), custom_call_target="tpu_custom_call" | custom-call | flops 1024 | bytes 1024 | tf_op jit(solution)/shard_map/prepare/pallas_call | solution.py:90
  7.3 2.9 %features.5.refs_4_ = bf16[112,3072]{1,0:T(8,128)(2,1)S(1)} custom-call(bf16[3,128,8192]{2,1,0:T(8,128)(2,1)S(1)} %get-tuple-element.16.refs_0_, f32[3,8,8192]{2,1,0:T(8,128)S(1)} %get-tuple-element.17.refs_1_, f32[6,128,128]{2,1,0:T(8,128)S(1)} %get-tuple-element.18.refs_2_), custom_call_target="tpu_custom_call" | custom-call | flops 1024 | bytes 1024 | tf_op jit(solution)/shard_map/features/pallas_call | solution.py:260
  10.2 0.0 collective-permute-done.refs_3_
  10.2 1.0 %features.6.mixed_ref = bf16[32,96,128]{2,1,0:T(8,128)(2,1)S(1)} custom-call(bf16[3,128,8192]{2,1,0:T(8,128)(2,1)S(1)} %get-tuple-element.16.refs_0_, f32[3,8,8192]{2,1,0:T(8,128)S(1)} %get-tuple-element.17.refs_1_, f32[6,128,128]{2,1,0:T(8,128)S(1)} %get-tuple-element.18.refs_2_, bf16[3,8,8192]{2,1,0:T(8,128)(2,1)S(1)} %collective-permute-done.refs_3_, ...), custom_call_target="tpu_custom_call" | custom-call | flops 1024 | bytes 1024 | tf_op jit(solution)/shard_map/features/pallas_call | solution.py:260
  11.2 4.5 %collective-permute-start.1 = (bf16[32,96,128]{2,1,0:T(8,128)(2,1)S(1)}, bf16[32,96,128]{2,1,0:T(8,128)(2,1)S(1)}, u32[]{:S(2)}, u32[]{:S(2)}) collective-permute-start(bf16[32,96,128]{2,1,0:T(8,128)(2,1)S(1)} %features.6.mixed_ref), channel_id=1, source_target_pairs={{0,1},{1,2},{2,3},{3,4},{4,5},{5,6},{6,7},{7,8},{8,9},{9,10},{10,1... | collective-permute-start | bytes 2359304 | tf_op jit(solution)/shard_map/ppermute | solution.py:359
  15.7 5.1 %features.7.mixed_ref = bf16[32,160,128]{2,1,0:T(8,128)(2,1)S(1)} custom-call(bf16[3,128,8192]{2,1,0:T(8,128)(2,1)S(1)} %get-tuple-element.16.refs_0_, f32[3,8,8192]{2,1,0:T(8,128)S(1)} %get-tuple-element.17.refs_1_, f32[6,128,128]{2,1,0:T(8,128)S(1)} %get-tuple-element.18.refs_2_, bf16[3,8,8192]{2,1,0:T(8,128)(2,1)S(1)} %collective-permute-done.refs_3_), custom_call_target="tpu_custom_call" | custom-call | flops 1024 | bytes 1024 | tf_op jit(solution)/shard_map/features/pallas_call | solution.py:260
  20.8 0.0 copy-start.3
  20.9 3.5 %collective-permute-start.2 = (bf16[32,160,128]{2,1,0:T(8,128)(2,1)S(1)}, bf16[32,160,128]{2,1,0:T(8,128)(2,1)}, u32[]{:S(2)}, u32[]{:S(2)}) collective-permute-start(bf16[32,160,128]{2,1,0:T(8,128)(2,1)S(1)} %features.7.mixed_ref), channel_id=1, source_target_pairs={{0,1},{1,2},{2,3},{3,4},{4,5},{5,6},{6,7},{7,8},{8,9},{9,10},{10,1... | collective-permute-start | bytes 3932168 | tf_op jit(solution)/shard_map/ppermute | solution.py:367
  24.4 1.9 %features.8.gate_ref = bf16[32,96,128]{2,1,0:T(8,128)(2,1)S(1)} custom-call(bf16[3,128,8192]{2,1,0:T(8,128)(2,1)S(1)} %get-tuple-element.16.refs_0_, f32[3,8,8192]{2,1,0:T(8,128)S(1)} %get-tuple-element.17.refs_1_, f32[6,128,128]{2,1,0:T(8,128)S(1)} %get-tuple-element.18.refs_2_, bf16[3,8,8192]{2,1,0:T(8,128)(2,1)S(1)} %collective-permute-done.refs_3_), custom_call_target="tpu_custom_call" | custom-call | flops 1024 | bytes 1024 | tf_op jit(solution)/shard_map/features/pallas_call | solution.py:260
  26.2 0.0 collective-permute-done.1.rim_ref
  26.2 0.0 copy-done.3
  26.3 5.2 %convolve.2 = bf16[32,96,128]{2,1,0:T(8,128)(2,1)} custom-call(bf16[32,96,128]{2,1,0:T(8,128)(2,1)S(1)} %features.6.mixed_ref, bf16[32,96,128]{2,1,0:T(8,128)(2,1)S(1)} %collective-permute-done.1.rim_ref, bf16[32,96,128]{2,1,0:T(8,128)(2,1)S(1)} %features.8.gate_ref, f32[32,1,256]{2,1,0:T(1,128)S(1)} %bitcast.14, f32[512,128]{1,0:T(8,128)S(1)} %get-tuple-element.22.taps_ref, ...), custom_call_target="tpu_custom_call" | custom-call | flops 137438953472 | bytes 1024 | tf_op jit(solution)/shard_map/convolve/pallas_call | solution.py:323
  31.5 7.4 %all-to-all-start = ((bf16[32,96,128]{2,1,0:T(8,128)(2,1)}), bf16[32,96,128]{2,1,0:T(8,128)(2,1)}, u32[]{:S(2)}, u32[]{:S(2)}) async-start(bf16[32,96,128]{2,1,0:T(8,128)(2,1)} %convolve.2), calls=%async_computation | async-start | bytes 1572864 | tf_op jit(solution)/shard_map/all_to_all | solution.py:352
  38.9 4.1 %features.9.gate_ref = bf16[32,160,128]{2,1,0:T(8,128)(2,1)S(1)} custom-call(bf16[128,8192]{1,0:T(8,128)(2,1)} %refs_0_.5, f32[3,8,8192]{2,1,0:T(8,128)S(1)} %get-tuple-element.17.refs_1_, f32[6,128,128]{2,1,0:T(8,128)S(1)} %get-tuple-element.18.refs_2_, bf16[3,8,8192]{2,1,0:T(8,128)(2,1)S(1)} %collective-permute-done.refs_3_), custom_call_target="tpu_custom_call" | custom-call | flops 1024 | bytes 1024 | tf_op jit(solution)/shard_map/features/pallas_call | solution.py:260
  43.0 0.0 collective-permute-done.2.rim_ref
  43.1 8.9 %convolve.3 = bf16[32,160,128]{2,1,0:T(8,128)(2,1)} custom-call(bf16[32,160,128]{2,1,0:T(8,128)(2,1)S(1)} %features.7.mixed_ref, bf16[32,160,128]{2,1,0:T(8,128)(2,1)} %collective-permute-done.2.rim_ref, bf16[32,160,128]{2,1,0:T(8,128)(2,1)S(1)} %features.9.gate_ref, f32[32,1,256]{2,1,0:T(1,128)S(1)} %bitcast.15, f32[512,128]{1,0:T(8,128)S(1)} %get-tuple-element.22.taps_ref, ...), custom_call_target="tpu_custom_call" | custom-call | flops 137438953472 | bytes 1024 | tf_op jit(solution)/shard_map/convolve/pallas_call | solution.py:323
  52.0 7.5 %all-to-all-done = bf16[32,96,128]{2,1,0:T(8,128)(2,1)} async-done(((bf16[32,96,128]{2,1,0:T(8,128)(2,1)}), bf16[32,96,128]{2,1,0:T(8,128)(2,1)}, u32[]{:S(2)}, u32[]{:S(2)}) %all-to-all-start) | async-done | bytes 786464 | tf_op jit(solution)/shard_map/all_to_all | solution.py:352
  59.5 4.4 %all-to-all-start.1 = ((bf16[32,160,128]{2,1,0:T(8,128)(2,1)}), bf16[32,160,128]{2,1,0:T(8,128)(2,1)S(1)}, u32[]{:S(2)}, u32[]{:S(2)}) async-start(bf16[32,160,128]{2,1,0:T(8,128)(2,1)} %convolve.3), calls=%async_computation.1 | async-start | bytes 2621440 | tf_op jit(solution)/shard_map/all_to_all | solution.py:352
  63.9 1.2 %copy_bitcast_fusion = bf16[96,4096]{1,0:T(8,128)(2,1)S(1)} fusion(bf16[32,96,128]{2,1,0:T(8,128)(2,1)} %all-to-all-done), kind=kLoop, calls=%fused_computation.1 | loop fusion | bytes 1572864 | tf_op jit(solution)/shard_map/reshape | solution.py:353
  65.1 1.5 %dynamic_update_slice.6 = bf16[256,4096]{1,0:T(8,128)(2,1)} pad(bf16[96,4096]{1,0:T(8,128)(2,1)S(1)} %copy_bitcast_fusion, bf16[]{:T(256)} %constant.16.clone.1), padding=0_160x0_0 | pad | bytes 2883586 | tf_op jit(solution)/shard_map/dynamic_update_slice | solution.py:375
  66.6 29.4 %all-to-all-done.1 = bf16[32,160,128]{2,1,0:T(8,128)(2,1)S(1)} async-done(((bf16[32,160,128]{2,1,0:T(8,128)(2,1)}), bf16[32,160,128]{2,1,0:T(8,128)(2,1)S(1)}, u32[]{:S(2)}, u32[]{:S(2)}) %all-to-all-start.1) | async-done | bytes 1310752 | tf_op jit(solution)/shard_map/all_to_all | solution.py:352
  96.0 1.2 %bitcast_dynamic-update-slice_fusion = bf16[256,4096]{1,0:T(8,128)(2,1)} fusion(bf16[256,4096]{1,0:T(8,128)(2,1)} %dynamic_update_slice.6, bf16[32,160,128]{2,1,0:T(8,128)(2,1)S(1)} %all-to-all-done.1), kind=kLoop, calls=%fused_computation | loop fusion | bytes 2621440 | tf_op jit(solution)/shard_map/dynamic_update_slice | solution.py:378
Async XLA Ops:
  0.0 3.6 %copy-start.2 = (s32[16]{0:T(128)S(1)}, s32[16]{0:T(128)}, u32[]{:S(2)}) copy-start(s32[16]{0:T(128)} %lengths_ref) | copy-start | bytes 196
  0.0 3.6 %copy-start.1 = (bf16[3,7,512]{2,1,0:T(8,128)(2,1)S(1)}, bf16[3,7,512]{2,1,0:T(8,128)(2,1)}, u32[]{:S(2)}) copy-start(bf16[3,7,512]{2,1,0:T(8,128)(2,1)} %short_ref.1) | copy-start | bytes 64516
  0.0 3.6 %copy-start = (bf16[128,512]{1,0:T(8,128)(2,1)S(1)}, bf16[128,512]{1,0:T(8,128)(2,1)}, u32[]{:S(2)}) copy-start(bf16[128,512]{1,0:T(8,128)(2,1)} %long_ref.1) | copy-start | bytes 393220
  1.2 9.0 %collective-permute-start = (bf16[3,8,8192]{2,1,0:T(8,128)(2,1)S(1)}, bf16[3,8,8192]{2,1,0:T(8,128)(2,1)S(1)}, u32[]{:S(2)}, u32[]{:S(2)}) collective-permute-start(bf16[3,8,8192]{2,1,0:T(8,128)(2,1)S(1)} %last_rows.1), channel_id=1, source_target_pairs={{0,1},{1,2},{2,3},{3,4},{4,5},{5,6},{6,7},{7,8},{8,9},{9,10},{10,1... | collective-permute-start | bytes 1179656 | tf_op jit(solution)/shard_map/ppermute | solution.py:344
  11.2 15.0 %collective-permute-start.1 = (bf16[32,96,128]{2,1,0:T(8,128)(2,1)S(1)}, bf16[32,96,128]{2,1,0:T(8,128)(2,1)S(1)}, u32[]{:S(2)}, u32[]{:S(2)}) collective-permute-start(bf16[32,96,128]{2,1,0:T(8,128)(2,1)S(1)} %features.6.mixed_ref), channel_id=1, source_target_pairs={{0,1},{1,2},{2,3},{3,4},{4,5},{5,6},{6,7},{7,8},{8,9},{9,10},{10,1... | collective-permute-start | bytes 2359304 | tf_op jit(solution)/shard_map/ppermute | solution.py:359
  20.8 5.4 %copy-start.3 = (f32[8192]{0:T(1024)S(1)}, f32[8192]{0:T(1024)}, u32[]{:S(2)}) copy-start(f32[8192]{0:T(1024)} %param.12) | copy-start | bytes 98308
  20.9 22.2 %collective-permute-start.2 = (bf16[32,160,128]{2,1,0:T(8,128)(2,1)S(1)}, bf16[32,160,128]{2,1,0:T(8,128)(2,1)}, u32[]{:S(2)}, u32[]{:S(2)}) collective-permute-start(bf16[32,160,128]{2,1,0:T(8,128)(2,1)S(1)} %features.7.mixed_ref), channel_id=1, source_target_pairs={{0,1},{1,2},{2,3},{3,4},{4,5},{5,6},{6,7},{7,8},{8,9},{9,10},{10,1... | collective-permute-start | bytes 3932168 | tf_op jit(solution)/shard_map/ppermute | solution.py:367
  31.5 28.0 %all-to-all-start = ((bf16[32,96,128]{2,1,0:T(8,128)(2,1)}), bf16[32,96,128]{2,1,0:T(8,128)(2,1)}, u32[]{:S(2)}, u32[]{:S(2)}) async-start(bf16[32,96,128]{2,1,0:T(8,128)(2,1)} %convolve.2), calls=%async_computation | async-start | bytes 1572864 | tf_op jit(solution)/shard_map/all_to_all | solution.py:352
  59.5 36.5 %all-to-all-start.1 = ((bf16[32,160,128]{2,1,0:T(8,128)(2,1)}), bf16[32,160,128]{2,1,0:T(8,128)(2,1)S(1)}, u32[]{:S(2)}, u32[]{:S(2)}) async-start(bf16[32,160,128]{2,1,0:T(8,128)(2,1)} %convolve.3), calls=%async_computation.1 | async-start | bytes 2621440 | tf_op jit(solution)/shard_map/all_to_all | solution.py:352

commit v7 on v6

--- a/solution.py
+++ b/solution.py
@@ -11,6 +11,7 @@
 GROUP = 16
 LANES = 128
 HALO = 8
+TAIL = 6
 CUTS = (0, 96, 256)
 VMEM_LIMIT = 24 << 20
 
@@ -108,22 +109,53 @@
     )(place, lengths, short_filter, long_filter, *far(*streams))
 
 
-def last_kernel(*refs):
-    for index, ref in enumerate(refs[:-1]):
-        refs[-1][index] = ref[...][-HALO:]
-
-
-def last_rows(streams):
+def pack_kernel(first_ref, second_ref, value_ref, out_ref):
+    channels = first_ref.shape[1]
+    first, second, value = (ref[...].astype(jnp.float32)[-TAIL:] for ref in (first_ref, second_ref, value_ref))
+    spare = 3 * TAIL - 16
+    size = channels * spare // 16
+    out_ref[0, :, :channels] = jnp.concatenate([first, value, second[spare:]], 0).astype(jnp.bfloat16)
+    folded = [second[:spare, low : low + size] for low in range(0, channels, size)]
+    out_ref[0, :, channels:] = jnp.concatenate(folded, 0).astype(jnp.bfloat16)
+
+
+def pack_rows(streams):
     rows, channels = streams[0].shape
+    width = channels + channels * (3 * TAIL - 16) // 16
     return pl.pallas_call(
-        last_kernel,
+        pack_kernel,
         grid=(1,),
         in_specs=[pl.BlockSpec((16, channels), lambda i: (rows // 16 - 1, 0))] * len(streams),
-        out_specs=pl.BlockSpec((len(streams), HALO, channels), lambda i: (0, 0, 0)),
-        out_shape=jax.ShapeDtypeStruct((len(streams), HALO, channels), jnp.bfloat16),
+        out_specs=pl.BlockSpec((1, 16, width), lambda i: (0, 0, 0)),
+        out_shape=jax.ShapeDtypeStruct((1, 16, width), jnp.bfloat16),
         compiler_params=pltpu.CompilerParams(vmem_limit_bytes=VMEM_LIMIT),
-        name="last_rows",
+        name="pack_rows",
     )(*far(*streams))
+
+
+def unpack_kernel(packed_ref, out_ref):
+    channels = out_ref.shape[2]
+    spare = 3 * TAIL - 16
+    size = channels * spare // 16
+    packed = packed_ref[0].astype(jnp.float32)
+    out_ref[0, : HALO - TAIL] = jnp.zeros((HALO - TAIL, channels), jnp.float32)
+    out_ref[0, HALO - TAIL + spare :] = packed[2 * TAIL :, :channels]
+    for part in range(16 // spare):
+        out_ref[0, HALO - TAIL : HALO - TAIL + spare, part * size : (part + 1) * size] = packed[
+            part * spare : (part + 1) * spare, channels:
+        ]
+
+
+def unpack_rows(packed, channels):
+    return pl.pallas_call(
+        unpack_kernel,
+        in_specs=[VMEM_SPEC],
+        out_specs=VMEM_SPEC,
+        out_shape=pltpu.VMEM((1, HALO, channels), jnp.float32),
+        cost_estimate=pl.CostEstimate(flops=1 << 10, bytes_accessed=1 << 10, transcendentals=0),
+        compiler_params=pltpu.CompilerParams(vmem_limit_bytes=VMEM_LIMIT),
+        name="unpack_rows",
+    )(*near(packed))
 
 
 def gathered(owners, own_count, low, high):
@@ -148,18 +180,20 @@
     return columns + [[piece] for piece in whole]
 
 
-def feature_kernel(phase, jobs, tap_count, own_count, bundle, places, *refs):
+def feature_kernel(phase, jobs, tap_count, own_count, bundle, places, packed, brings, *refs):
     streams_ref, taps_ref, keep_ref, *refs = refs
     rim_ref, refs = (None, refs) if phase == "early" else (refs[0], refs[1:])
     early_ref, refs = (refs[0], refs[1:]) if phase == "late" else (None, refs)
-    far_ref, refs = (refs[0], refs[1:]) if None in places else (None, refs)
-    out_refs, padded_ref, refs = refs[: len(jobs)], refs[len(jobs)], refs[len(jobs) + 1 :]
+    far_ref, refs = (refs[0], refs[1:]) if brings else (None, refs)
+    out_refs, refs = refs[: len(jobs)], refs[len(jobs) :]
+    brought_ref, refs = (refs[0], refs[1:]) if brings else (None, refs)
+    padded_ref = refs[0]
     rows, tile = streams_ref.shape[-2:]
     tiled = len(streams_ref.shape) == 2
     width = bundle * own_count
     strip = 16
-    if far_ref is not None:
-        brought = pltpu.make_async_copy(far_ref, refs[0], refs[1])
+    if brings:
+        brought = pltpu.make_async_copy(far_ref, brought_ref.at[0], refs[1])
         brought.start()
 
     def run(job, out_ref):
@@ -189,14 +223,13 @@
                     held = slice(0, strip if phase == "late" else rows)
                     if tiled:
                         own = column_of(streams_ref, column, held)
-                    elif places[stream] is None:
-                        own = column_of(refs[0], column, held)
                     else:
                         own = column_of(streams_ref, column, places[stream], held)
                     padded_ref[number, slot, HALO : HALO + own.shape[0]] = own.astype(jnp.float32)
                     if phase != "early":
-                        rim = column_of(rim_ref, column, stream, slice(None)).astype(jnp.float32)
-                        padded_ref[number, slot, :HALO] = rim
+                        rim = column_of(rim_ref, column, 0, slice(None)).astype(jnp.float32)
+                        rim = rim[slot * TAIL : (slot + 1) * TAIL] if packed else rim[HALO - TAIL :]
+                        padded_ref[number, slot, HALO - TAIL : HALO] = rim
                     taps[number, slot] = column_of(taps_ref, column, stream, slice(None))
             results = [[] for _ in columns]
             for row in range(strip if phase == "early" else 0, strip if phase == "late" else rows, strip):
@@ -230,12 +263,12 @@
         lax.fori_loop(0, tile // width, one_bundle, 0, unroll=4 if phase == "late" else 2)
 
     for job, out_ref in zip(jobs, out_refs):
-        if far_ref is not None and None in [places[stream] for stream in job[0]]:
-            brought.wait()
         run(job, out_ref)
-
-
-def features(streams, places, jobs, rim, taps, keep, own_count, phase="whole", early=(), distant=()):
+    if brings:
+        brought.wait()
+
+
+def features(streams, places, jobs, rim, taps, keep, own_count, phase="whole", early=(), brings=()):
     rows, channels = streams.shape[-2:]
     owners = channels // own_count
     tiles = 1 if streams.ndim == 3 else max(1, channels // 2048)
@@ -251,25 +284,26 @@
     shapes = [
         (rows - 16, owners * (high - low)) if phase == "early" else (owners, high - low, rows) for _, low, high in jobs
     ]
+    shapes += [(1, *stream.shape) for stream in brings]
     given = [*(near if streams.ndim == 3 else far)(streams), *near(taps, keep)]
     given += near(*([] if phase == "early" else [rim]), *early)
     width = max(len(product) for product, _, _ in jobs)
     scratch = [pltpu.VMEM((max(len(job[2]) for job in found), width, HALO + rows, LANES), jnp.float32)]
-    if distant:
-        scratch += [pltpu.VMEM((rows, channels), jnp.bfloat16), pltpu.SemaphoreType.DMA]
+    scratch += [pltpu.SemaphoreType.DMA] * len(brings)
+    packed = rim is not None and rim.dtype == jnp.bfloat16
     return pl.pallas_call(
-        functools.partial(feature_kernel, phase, found, keep.shape[0] + 1, own_count, bundle, places),
+        functools.partial(feature_kernel, phase, found, keep.shape[0] + 1, own_count, bundle, places, packed, bool(brings)),
         grid=(tiles,),
         in_specs=[stream_spec]
         + [VMEM_SPEC] * (len(given) - 1)
-        + [pl.BlockSpec(memory_space=pltpu.HBM)] * len(distant),
-        out_specs=[VMEM_SPEC] * len(jobs),
+        + [pl.BlockSpec(memory_space=pltpu.HBM)] * len(brings),
+        out_specs=[VMEM_SPEC] * len(shapes),
         out_shape=[pltpu.VMEM(shape, jnp.bfloat16) for shape in shapes],
         scratch_shapes=scratch,
         cost_estimate=pl.CostEstimate(flops=1 << 10, bytes_accessed=1 << 10, transcendentals=0),
         compiler_params=pltpu.CompilerParams(vmem_limit_bytes=VMEM_LIMIT),
         name="features",
-    )(*given, *far(*distant))
+    )(*given, *far(*brings))
 
 
 def convolve_kernel(
@@ -340,10 +374,10 @@
     following = [(source, source + 1) for source in range(devices - 1)]
     streams = (first, second, value)
     cuts = CUTS if own_count == CUTS[-1] else (0, own_count)
-    last, lengths = lax.optimization_barrier((last_rows(streams), lengths))
+    last, lengths = lax.optimization_barrier((pack_rows(streams), lengths))
     rim = lax.ppermute(last, AXES, following)
     short_keep, long_keep, long_taps, short_taps, streams = prepare(
-        place, lengths, short_filter, long_filter, (first, second, value)
+        place, lengths, short_filter, long_filter, (first, value)
     )
     tables = (short_taps, short_keep, own_count)
     mix = lambda mixed, rims, gate, low: convolve(
@@ -351,22 +385,24 @@
     )
     relay = lambda part: lax.all_to_all(part, AXES, 0, 0, tiled=True)
     as_rows = lambda part: part.transpose(1, 0, 2).reshape(part.shape[1], -1)
-    places, mixed_of, gate_of = (0, None, 1), (0, 2), (1,)
+    mixed_of, gate_of = (0, 2), (1,)
     (low, cut), *rest = zip(cuts, cuts[1:])
     jobs = ((mixed_of, low, cut),)
-    early = features(streams, (0, 1, 2), jobs, None, *tables, "early")
-    (mixed,) = features(streams, (0, 1, 2), jobs, rim, *tables, "late", early)
+    early = features(streams, (0, None, 1), jobs, None, *tables, "early")
+    (mixed,) = features(streams, (0, None, 1), jobs, rim, *tables, "late", early)
     rims = lax.ppermute(mixed, AXES, following)
     if not rest:
+        rim = unpack_rows(rim, channels)
         (gate,) = features(second, (0, 0, 0), ((gate_of, low, cut),), rim, *tables)
         return as_rows(relay(mix(mixed, rims, gate, low)))
 
     rim, _ = lax.optimization_barrier((rim, mixed))
     jobs = ((mixed_of, cut, own_count),)
-    (high_mixed,) = features(streams, (0, 1, 2), jobs, rim, *tables)
+    high_mixed, nearby = features(streams, (0, None, 1), jobs, rim, *tables, brings=(second,))
     high_rims = lax.ppermute(high_mixed, AXES, following)
     rim, _ = lax.optimization_barrier((rim, high_mixed))
-    (gate,) = features(streams, (0, 1, 2), ((gate_of, low, cut),), rim, *tables)
+    rim = unpack_rows(rim, channels)
+    (gate,) = features(nearby, (0, 0, 0), ((gate_of, low, cut),), rim, *tables)
     low_part = mix(mixed, rims, gate, low)
     rim, _ = lax.optimization_barrier((rim, low_part))
     low_part = relay(low_part)

time: 97.8 us -> 96.7 us (0.989)
  transfers between devices with their start and end apart: 5 -> 5, of which waited for: 2 -> 2; matrix products, arithmetic and copies ran while one was open for 3% -> 3% of each run, Pallas kernels for 33% -> 32%
where the time goes in v7:
time: 96.7 us; the launch traced here: 96.2 us
  waiting for transfers between devices  37 us (38%)
  Pallas kernels  33.3 us (34%)
  starting transfers between devices  21.8 us (23%)
  local copies, waits for them, and re-layouts  3.95 us (4%)
    all_to_all x2, waiting for transfers between devices, on_device(): relay = lambda part: lax.all_to_all(part, AXES, 0, 0, tiled=True)  37 us
    pallas_call x5, Pallas kernels, features(): pl.pallas_call(functools.partial(feature_kernel, phase, found, keep.shape...  14.9 us
    pallas_call x2, Pallas kernels, convolve(): pl.pallas_call(functools.partial(convolve_kernel, tiled, first_channel //...  14.2 us
    all_to_all x2, starting transfers between devices, on_device(): relay = lambda part: lax.all_to_all(part, AXES, 0, 0, tiled=True)  11.7 us
    ppermute x1, starting transfers between devices, on_device(): rims = lax.ppermute(mixed, AXES, following)  4.54 us
    ppermute x1, starting transfers between devices, on_device(): high_rims = lax.ppermute(high_mixed, AXES, following)  3.21 us
    pallas_call x1, Pallas kernels, prepare(): pl.pallas_call(functools.partial(prepare_kernel, tile, len(streams)), in_...  2.92 us
    ppermute x1, starting transfers between devices, on_device(): rim = lax.ppermute(last, AXES, following)  2.38 us
  transfers between devices with their start and end apart: 5, of which 2 were waited for; matrix products, arithmetic and copies ran while one was open for 3% of the time, Pallas kernels for 32%

profile of v7, /device:TPU:0, one launch (start us, length us, event | category | flops | bytes accessed | tf_op | source)
XLA Modules:
  0.0 96.2 jit_solution(10832995521861336547)
XLA Ops:
  0.0 0.0 copy-start.2
  0.0 0.0 copy-start
  0.0 0.0 copy-start.1
  0.0 1.2 %pack_rows.1 = bf16[1,16,9216]{2,1,0:T(8,128)(2,1)S(1)} custom-call(bf16[128,8192]{1,0:T(8,128)(2,1)} %refs_0_.2, bf16[128,8192]{1,0:T(8,128)(2,1)} %refs_0_.3, bf16[128,8192]{1,0:T(8,128)(2,1)} %refs_1_.1), custom_call_target="tpu_custom_call" | custom-call | tf_op jit(solution)/shard_map/pack_rows/pallas_call | solution.py:125
  1.2 2.4 %collective-permute-start = (bf16[1,16,9216]{2,1,0:T(8,128)(2,1)S(1)}, bf16[1,16,9216]{2,1,0:T(8,128)(2,1)S(1)}, u32[]{:S(2)}, u32[]{:S(2)}) collective-permute-start(bf16[1,16,9216]{2,1,0:T(8,128)(2,1)S(1)} %pack_rows.1), channel_id=1, source_target_pairs={{0,1},{1,2},{2,3},{3,4},{4,5},{5,6},{6,7},{7,8},{8,9},{9,10},{10,1... | collective-permute-start | bytes 884744 | tf_op jit(solution)/shard_map/ppermute | solution.py:378
  3.6 0.0 copy-done.2
  3.6 0.0 copy-done
  3.7 0.0 copy-done.1
  3.7 2.9 %prepare.1 = (f32[6,128,128]{2,1,0:T(8,128)S(1)}, bf16[256,128]{1,0:T(8,128)(2,1)S(1)}, f32[512,128]{1,0:T(8,128)S(1)}, f32[3,8,8192]{2,1,0:T(8,128)S(1)}, bf16[2,128,8192]{2,1,0:T(8,128)(2,1)S(1)}) custom-call(s32[1]{0:T(128)} %bitcast.place_ref, s32[16]{0:T(128)S(1)} %copy-done.2, bf16[3,7,512]{2,1,0:T(8,128)(2,1)S(1)} %copy-done.1, ...), custom_call_target="tpu_custom_call" | custom-call | flops 1024 | bytes 1024 | tf_op jit(solution)/shard_map/prepare/pallas_call | solution.py:91
  6.6 2.9 %features.5.refs_4_ = bf16[112,3072]{1,0:T(8,128)(2,1)S(1)} custom-call(bf16[2,128,8192]{2,1,0:T(8,128)(2,1)S(1)} %get-tuple-element.18.refs_0_, f32[3,8,8192]{2,1,0:T(8,128)S(1)} %get-tuple-element.19.refs_1_, f32[6,128,128]{2,1,0:T(8,128)S(1)} %get-tuple-element.20.refs_2_), custom_call_target="tpu_custom_call" | custom-call | flops 1024 | bytes 1024 | tf_op jit(solution)/shard_map/features/pallas_call | solution.py:294
  9.5 0.0 collective-permute-done.refs_3_.packed_ref
  9.5 1.0 %features.6.mixed_ref = bf16[32,96,128]{2,1,0:T(8,128)(2,1)S(1)} custom-call(bf16[2,128,8192]{2,1,0:T(8,128)(2,1)S(1)} %get-tuple-element.18.refs_0_, f32[3,8,8192]{2,1,0:T(8,128)S(1)} %get-tuple-element.19.refs_1_, f32[6,128,128]{2,1,0:T(8,128)S(1)} %get-tuple-element.20.refs_2_, bf16[1,16,9216]{2,1,0:T(8,128)(2,1)S(1)} %collective-permute-done.refs_3_.packed_ref, ...), custom_call_target="tpu_custom_call" | custom-call | flops 1024 | bytes 1024 | tf_op jit(solution)/shard_map/features/pallas_call | solution.py:294
  10.5 4.5 %collective-permute-start.1 = (bf16[32,96,128]{2,1,0:T(8,128)(2,1)S(1)}, bf16[32,96,128]{2,1,0:T(8,128)(2,1)S(1)}, u32[]{:S(2)}, u32[]{:S(2)}) collective-permute-start(bf16[32,96,128]{2,1,0:T(8,128)(2,1)S(1)} %features.6.mixed_ref), channel_id=1, source_target_pairs={{0,1},{1,2},{2,3},{3,4},{4,5},{5,6},{6,7},{7,8},{8,9},{9,10},{10,1... | collective-permute-start | bytes 2359304 | tf_op jit(solution)/shard_map/ppermute | solution.py:393
  15.0 5.1 %features.7 = (bf16[32,160,128]{2,1,0:T(8,128)(2,1)S(1)}, bf16[1,128,8192]{2,1,0:T(8,128)(2,1)S(1)}) custom-call(bf16[2,128,8192]{2,1,0:T(8,128)(2,1)S(1)} %get-tuple-element.18.refs_0_, f32[3,8,8192]{2,1,0:T(8,128)S(1)} %get-tuple-element.19.refs_1_, f32[6,128,128]{2,1,0:T(8,128)S(1)} %get-tuple-element.20.refs_2_, ...), custom_call_target="tpu_custom_call" | custom-call | flops 1024 | bytes 1024 | tf_op jit(solution)/shard_map/features/pallas_call | solution.py:294
  20.1 3.2 %collective-permute-start.2 = (bf16[32,160,128]{2,1,0:T(8,128)(2,1)S(1)}, bf16[32,160,128]{2,1,0:T(8,128)(2,1)}, u32[]{:S(2)}, u32[]{:S(2)}) collective-permute-start(bf16[32,160,128]{2,1,0:T(8,128)(2,1)S(1)} %get-tuple-element.24.mixed_ref), channel_id=1, source_target_pairs={{0,1},{1,2},{2,3},{3,4},{4,5},{5,6},{6,7},{7,8},{8,9},{9,10},{10,1... | collective-permute-start | bytes 3932168 | tf_op jit(solution)/shard_map/ppermute | solution.py:402
  23.4 0.1 unpack_rows.1.refs_3_
  23.4 0.0 copy-start.3
  23.4 1.9 %features.8.gate_ref = bf16[32,96,128]{2,1,0:T(8,128)(2,1)S(1)} custom-call(bf16[1,128,8192]{2,1,0:T(8,128)(2,1)S(1)} %get-tuple-element.23.refs_0_, f32[3,8,8192]{2,1,0:T(8,128)S(1)} %get-tuple-element.19.refs_1_, f32[6,128,128]{2,1,0:T(8,128)S(1)} %get-tuple-element.20.refs_2_, f32[1,8,8192]{2,1,0:T(8,128)S(1)} %unpack_rows.1.refs_3_), custom_call_target="tpu_custom_call" | custom-call | flops 1024 | bytes 1024 | tf_op jit(solution)/shard_map/features/pallas_call | solution.py:294
  25.3 0.0 collective-permute-done.1.rim_ref
  25.3 0.0 copy-done.3
  25.3 5.2 %convolve.2 = bf16[32,96,128]{2,1,0:T(8,128)(2,1)} custom-call(bf16[32,96,128]{2,1,0:T(8,128)(2,1)S(1)} %features.6.mixed_ref, bf16[32,96,128]{2,1,0:T(8,128)(2,1)S(1)} %collective-permute-done.1.rim_ref, bf16[32,96,128]{2,1,0:T(8,128)(2,1)S(1)} %features.8.gate_ref, f32[32,1,256]{2,1,0:T(1,128)S(1)} %bitcast.14, f32[512,128]{1,0:T(8,128)S(1)} %get-tuple-element.26.taps_ref, ...), custom_call_target="tpu_custom_call" | custom-call | flops 137438953472 | bytes 1024 | tf_op jit(solution)/shard_map/convolve/pallas_call | solution.py:357
  30.6 7.3 %all-to-all-start = ((bf16[32,96,128]{2,1,0:T(8,128)(2,1)}), bf16[32,96,128]{2,1,0:T(8,128)(2,1)}, u32[]{:S(2)}, u32[]{:S(2)}) async-start(bf16[32,96,128]{2,1,0:T(8,128)(2,1)} %convolve.2), calls=%async_computation | async-start | bytes 1572864 | tf_op jit(solution)/shard_map/all_to_all | solution.py:386
  37.9 4.1 %features.9.gate_ref = bf16[32,160,128]{2,1,0:T(8,128)(2,1)S(1)} custom-call(bf16[128,8192]{1,0:T(8,128)(2,1)} %refs_0_.3, f32[3,8,8192]{2,1,0:T(8,128)S(1)} %get-tuple-element.19.refs_1_, f32[6,128,128]{2,1,0:T(8,128)S(1)} %get-tuple-element.20.refs_2_, f32[1,8,8192]{2,1,0:T(8,128)S(1)} %unpack_rows.1.refs_3_), custom_call_target="tpu_custom_call" | custom-call | flops 1024 | bytes 1024 | tf_op jit(solution)/shard_map/features/pallas_call | solution.py:294
  42.0 0.0 collective-permute-done.2.rim_ref
  42.0 8.9 %convolve.3 = bf16[32,160,128]{2,1,0:T(8,128)(2,1)} custom-call(bf16[32,160,128]{2,1,0:T(8,128)(2,1)S(1)} %get-tuple-element.24.mixed_ref, bf16[32,160,128]{2,1,0:T(8,128)(2,1)} %collective-permute-done.2.rim_ref, bf16[32,160,128]{2,1,0:T(8,128)(2,1)S(1)} %features.9.gate_ref, f32[32,1,256]{2,1,0:T(1,128)S(1)} %bitcast.15, ...), custom_call_target="tpu_custom_call" | custom-call | flops 137438953472 | bytes 1024 | tf_op jit(solution)/shard_map/convolve/pallas_call | solution.py:357
  50.9 7.6 %all-to-all-done = bf16[32,96,128]{2,1,0:T(8,128)(2,1)} async-done(((bf16[32,96,128]{2,1,0:T(8,128)(2,1)}), bf16[32,96,128]{2,1,0:T(8,128)(2,1)}, u32[]{:S(2)}, u32[]{:S(2)}) %all-to-all-start) | async-done | bytes 786464 | tf_op jit(solution)/shard_map/all_to_all | solution.py:386
  58.5 4.4 %all-to-all-start.1 = ((bf16[32,160,128]{2,1,0:T(8,128)(2,1)}), bf16[32,160,128]{2,1,0:T(8,128)(2,1)S(1)}, u32[]{:S(2)}, u32[]{:S(2)}) async-start(bf16[32,160,128]{2,1,0:T(8,128)(2,1)} %convolve.3), calls=%async_computation.1 | async-start | bytes 2621440 | tf_op jit(solution)/shard_map/all_to_all | solution.py:386
  62.9 1.2 %copy_bitcast_fusion = bf16[96,4096]{1,0:T(8,128)(2,1)S(1)} fusion(bf16[32,96,128]{2,1,0:T(8,128)(2,1)} %all-to-all-done), kind=kLoop, calls=%fused_computation.1 | loop fusion | bytes 1572864 | tf_op jit(solution)/shard_map/reshape | solution.py:387
  64.1 1.5 %dynamic_update_slice.6 = bf16[256,4096]{1,0:T(8,128)(2,1)} pad(bf16[96,4096]{1,0:T(8,128)(2,1)S(1)} %copy_bitcast_fusion, bf16[]{:T(256)} %constant.16.clone.1), padding=0_160x0_0 | pad | bytes 2883586 | tf_op jit(solution)/shard_map/dynamic_update_slice | solution.py:411
  65.6 29.4 %all-to-all-done.1 = bf16[32,160,128]{2,1,0:T(8,128)(2,1)S(1)} async-done(((bf16[32,160,128]{2,1,0:T(8,128)(2,1)}), bf16[32,160,128]{2,1,0:T(8,128)(2,1)S(1)}, u32[]{:S(2)}, u32[]{:S(2)}) %all-to-all-start.1) | async-done | bytes 1310752 | tf_op jit(solution)/shard_map/all_to_all | solution.py:386
  95.0 1.2 %bitcast_dynamic-update-slice_fusion = bf16[256,4096]{1,0:T(8,128)(2,1)} fusion(bf16[256,4096]{1,0:T(8,128)(2,1)} %dynamic_update_slice.6, bf16[32,160,128]{2,1,0:T(8,128)(2,1)S(1)} %all-to-all-done.1), kind=kLoop, calls=%fused_computation | loop fusion | bytes 2621440 | tf_op jit(solution)/shard_map/dynamic_update_slice | solution.py:414
Async XLA Ops:
  0.0 3.6 %copy-start.2 = (s32[16]{0:T(128)S(1)}, s32[16]{0:T(128)}, u32[]{:S(2)}) copy-start(s32[16]{0:T(128)} %lengths_ref) | copy-start | bytes 196
  0.0 3.6 %copy-start = (bf16[128,512]{1,0:T(8,128)(2,1)S(1)}, bf16[128,512]{1,0:T(8,128)(2,1)}, u32[]{:S(2)}) copy-start(bf16[128,512]{1,0:T(8,128)(2,1)} %long_ref.1) | copy-start | bytes 393220
  0.0 3.7 %copy-start.1 = (bf16[3,7,512]{2,1,0:T(8,128)(2,1)S(1)}, bf16[3,7,512]{2,1,0:T(8,128)(2,1)}, u32[]{:S(2)}) copy-start(bf16[3,7,512]{2,1,0:T(8,128)(2,1)} %short_ref.1) | copy-start | bytes 64516
  1.2 8.2 %collective-permute-start = (bf16[1,16,9216]{2,1,0:T(8,128)(2,1)S(1)}, bf16[1,16,9216]{2,1,0:T(8,128)(2,1)S(1)}, u32[]{:S(2)}, u32[]{:S(2)}) collective-permute-start(bf16[1,16,9216]{2,1,0:T(8,128)(2,1)S(1)} %pack_rows.1), channel_id=1, source_target_pairs={{0,1},{1,2},{2,3},{3,4},{4,5},{5,6},{6,7},{7,8},{8,9},{9,10},{10,1... | collective-permute-start | bytes 884744 | tf_op jit(solution)/shard_map/ppermute | solution.py:378
  10.5 14.8 %collective-permute-start.1 = (bf16[32,96,128]{2,1,0:T(8,128)(2,1)S(1)}, bf16[32,96,128]{2,1,0:T(8,128)(2,1)S(1)}, u32[]{:S(2)}, u32[]{:S(2)}) collective-permute-start(bf16[32,96,128]{2,1,0:T(8,128)(2,1)S(1)} %features.6.mixed_ref), channel_id=1, source_target_pairs={{0,1},{1,2},{2,3},{3,4},{4,5},{5,6},{6,7},{7,8},{8,9},{9,10},{10,1... | collective-permute-start | bytes 2359304 | tf_op jit(solution)/shard_map/ppermute | solution.py:393
  20.1 21.9 %collective-permute-start.2 = (bf16[32,160,128]{2,1,0:T(8,128)(2,1)S(1)}, bf16[32,160,128]{2,1,0:T(8,128)(2,1)}, u32[]{:S(2)}, u32[]{:S(2)}) collective-permute-start(bf16[32,160,128]{2,1,0:T(8,128)(2,1)S(1)} %get-tuple-element.24.mixed_ref), channel_id=1, source_target_pairs={{0,1},{1,2},{2,3},{3,4},{4,5},{5,6},{6,7},{7,8},{8,9},{9,10},{10,1... | collective-permute-start | bytes 3932168 | tf_op jit(solution)/shard_map/ppermute | solution.py:402
  23.4 1.9 %copy-start.3 = (f32[8192]{0:T(1024)S(1)}, f32[8192]{0:T(1024)}, u32[]{:S(2)}) copy-start(f32[8192]{0:T(1024)} %param.12) | copy-start | bytes 98308
  30.6 27.9 %all-to-all-start = ((bf16[32,96,128]{2,1,0:T(8,128)(2,1)}), bf16[32,96,128]{2,1,0:T(8,128)(2,1)}, u32[]{:S(2)}, u32[]{:S(2)}) async-start(bf16[32,96,128]{2,1,0:T(8,128)(2,1)} %convolve.2), calls=%async_computation | async-start | bytes 1572864 | tf_op jit(solution)/shard_map/all_to_all | solution.py:386
  58.5 36.5 %all-to-all-start.1 = ((bf16[32,160,128]{2,1,0:T(8,128)(2,1)}), bf16[32,160,128]{2,1,0:T(8,128)(2,1)S(1)}, u32[]{:S(2)}, u32[]{:S(2)}) async-start(bf16[32,160,128]{2,1,0:T(8,128)(2,1)} %convolve.3), calls=%async_computation.1 | async-start | bytes 2621440 | tf_op jit(solution)/shard_map/all_to_all | solution.py:386

commit v8 on v7

--- a/solution.py
+++ b/solution.py
@@ -306,18 +306,14 @@
     )(*given, *far(*brings))
 
 
-def convolve_kernel(
-    tiled, first_group, group_stride, mixed_ref, rim_ref, gate_ref, skip_ref, taps_ref, keep_ref, out_ref
-):
+def direct_kernel(first_channel, mixed_ref, skip_ref, out_ref):
     owners, count, rows = out_ref.shape
-    length = taps_ref.shape[1]
-
-    def one_owner(index, _):
-        owner = pl.program_id(0) * owners + index
+
+    def one_owner(owner, _):
         for low in range(0, count, 64):
             block = min(64, count - low)
             whole = pl.ds(low, block)
-            place = first_group * GROUP + low
+            place = first_channel + low
             skip = jnp.broadcast_to(skip_ref[owner][:, place : place + block], (block, block))
             row = lax.broadcasted_iota(jnp.int32, (block, block), 0)
             column = lax.broadcasted_iota(jnp.int32, (block, block), 1)
@@ -325,31 +321,58 @@
             gain_high = gain.astype(jnp.bfloat16)
             gain_low = (gain - gain_high.astype(jnp.float32)).astype(jnp.bfloat16)
             own_block = mixed_ref[owner, whole]
-            direct = jnp.dot(
+            out_ref[owner, whole] = jnp.dot(
                 jnp.concatenate([gain_high, gain_low], 1),
                 jnp.concatenate([own_block, own_block], 0),
                 preferred_element_type=jnp.float32,
             )
-            for unit in range(block // GROUP):
-                members = pl.ds(low + unit * GROUP, GROUP)
-                group = owner * group_stride + first_group + low // GROUP + unit
-                row = jnp.broadcast_to(taps_ref[pl.ds(group, 1)], (GROUP, length))
-                base = pltpu.roll(row, 0, 1, stride=1, stride_axis=0).astype(jnp.bfloat16)
-                strips = [base] + [pltpu.roll(base, shift, 1) for shift in range(GROUP, length, GROUP)]
-                circulant = jnp.concatenate(strips, 0)
-                weights = jnp.concatenate([circulant, circulant], 0) * keep_ref[...]
-                window = jnp.concatenate([rim_ref[index if tiled else owner, members], mixed_ref[owner, members]], 1)
-                total = jnp.dot(window, weights, preferred_element_type=jnp.float32)
-                total = total + direct[unit * GROUP : (unit + 1) * GROUP]
-                total = total * gate_ref[owner, members].astype(jnp.float32)
-                out_ref[index, members] = total.astype(jnp.bfloat16)
+        return 0
+
+    lax.fori_loop(0, owners, one_owner, 0, unroll=max(1, min(owners, 8)))
+
+
+def direct_terms(mixed, skip_gain, first_channel, own_count):
+    owners = mixed.shape[0]
+    return pl.pallas_call(
+        functools.partial(direct_kernel, first_channel),
+        in_specs=[VMEM_SPEC] * 2,
+        out_specs=VMEM_SPEC,
+        out_shape=pltpu.VMEM(mixed.shape, jnp.float32),
+        cost_estimate=pl.CostEstimate(flops=1 << 10, bytes_accessed=1 << 10, transcendentals=0),
+        compiler_params=pltpu.CompilerParams(vmem_limit_bytes=VMEM_LIMIT),
+        name="direct_terms",
+    )(*near(mixed), skip_gain.reshape(owners, 1, own_count))
+
+
+def convolve_kernel(
+    tiled, first_group, group_stride, mixed_ref, rim_ref, gate_ref, direct_ref, taps_ref, keep_ref, out_ref
+):
+    owners, count, rows = out_ref.shape
+    length = taps_ref.shape[1]
+
+    def one_owner(index, _):
+        owner = pl.program_id(0) * owners + index
+        for unit in range(count // GROUP):
+            members = pl.ds(unit * GROUP, GROUP)
+            group = owner * group_stride + first_group + unit
+            row = jnp.broadcast_to(taps_ref[pl.ds(group, 1)], (GROUP, length))
+            base = pltpu.roll(row, 0, 1, stride=1, stride_axis=0).astype(jnp.bfloat16)
+            strips = [base] + [pltpu.roll(base, shift, 1) for shift in range(GROUP, length, GROUP)]
+            circulant = jnp.concatenate(strips, 0)
+            weights = jnp.concatenate([circulant, circulant], 0) * keep_ref[...]
+            rim = rim_ref[index if tiled else owner, members]
+            window = jnp.concatenate([rim, mixed_ref[owner, members]], 1)
+            total = jnp.dot(window, weights, preferred_element_type=jnp.float32)
+            total = total + direct_ref[owner, members]
+            total = total * gate_ref[owner, members].astype(jnp.float32)
+            out_ref[index, members] = total.astype(jnp.bfloat16)
         return 0
 
     together = max(1, min(owners, 8))
     lax.fori_loop(0, owners, one_owner, 0, unroll=together)
 
 
-def convolve(mixed, rim, gate, skip_gain, taps, keep, first_channel, own_count):
+def convolve(mixed, rim, gate, direct, taps, keep, first_channel, own_count):
     owners, count, rows = mixed.shape
     tiled = first_channel > 0
     steps = min(owners, 2 if 2 * count <= own_count else 4)
@@ -363,7 +386,7 @@
         cost_estimate=pl.CostEstimate(flops=1 << 37, bytes_accessed=1 << 10, transcendentals=0),
         compiler_params=pltpu.CompilerParams(vmem_limit_bytes=VMEM_LIMIT),
         name="convolve",
-    )(*near(mixed), *(far if tiled else near)(rim), *near(gate), skip_gain.reshape(owners, 1, own_count), *near(taps, keep))
+    )(*near(mixed), *(far if tiled else near)(rim), *near(gate, direct, taps, keep))
 
 
 def on_device(first, second, value, short_filter, long_filter, skip_gain, lengths):
@@ -380,8 +403,8 @@
         place, lengths, short_filter, long_filter, (first, value)
     )
     tables = (short_taps, short_keep, own_count)
-    mix = lambda mixed, rims, gate, low: convolve(
-        mixed, rims, gate, skip_gain, long_taps, long_keep, low, own_count
+    mix = lambda mixed, rims, gate, direct, low: convolve(
+        mixed, rims, gate, direct, long_taps, long_keep, low, own_count
     )
     relay = lambda part: lax.all_to_all(part, AXES, 0, 0, tiled=True)
     as_rows = lambda part: part.transpose(1, 0, 2).reshape(part.shape[1], -1)
@@ -394,22 +417,25 @@
     if not rest:
         rim = unpack_rows(rim, channels)
         (gate,) = features(second, (0, 0, 0), ((gate_of, low, cut),), rim, *tables)
-        return as_rows(relay(mix(mixed, rims, gate, low)))
+        direct = direct_terms(mixed, skip_gain, low, own_count)
+        return as_rows(relay(mix(mixed, rims, gate, direct, low)))
 
     rim, _ = lax.optimization_barrier((rim, mixed))
     jobs = ((mixed_of, cut, own_count),)
     high_mixed, nearby = features(streams, (0, None, 1), jobs, rim, *tables, brings=(second,))
     high_rims = lax.ppermute(high_mixed, AXES, following)
-    rim, _ = lax.optimization_barrier((rim, high_mixed))
+    rim, skip_gain, _ = lax.optimization_barrier((rim, skip_gain, high_mixed))
     rim = unpack_rows(rim, channels)
     (gate,) = features(nearby, (0, 0, 0), ((gate_of, low, cut),), rim, *tables)
-    low_part = mix(mixed, rims, gate, low)
-    rim, _ = lax.optimization_barrier((rim, low_part))
+    direct = direct_terms(mixed, skip_gain, low, own_count)
+    low_part = mix(mixed, rims, gate, direct, low)
+    rim, skip_gain, _ = lax.optimization_barrier((rim, skip_gain, low_part))
     low_part = relay(low_part)
     (high_gate,) = features(second, (0, 0, 0), ((gate_of, cut, own_count),), rim, *tables)
     whole = jnp.zeros((own_count, devices * rows), jnp.bfloat16)
     whole = lax.dynamic_update_slice(whole, as_rows(low_part), (low, 0))
-    high_part = relay(mix(high_mixed, high_rims, high_gate, cut))
+    high_direct = direct_terms(high_mixed, skip_gain, cut, own_count)
+    high_part = relay(mix(high_mixed, high_rims, high_gate, high_direct, cut))
     whole = lax.optimization_barrier(whole)
     return lax.dynamic_update_slice(whole, as_rows(high_part), (cut, 0))
 

time: 96.7 us -> 96.8 us (level)
  Pallas kernels: 33.3 us -> 34.6 us
    pallas_call x0 -> x2, Pallas kernels: none -> 3.79 us  [direct_terms(): pl.pallas_call(functools.partial(direct_kernel, first_channel), in_specs=...]
    pallas_call x2, Pallas kernels: 14.2 us -> 11.6 us  [convolve(): pl.pallas_call(functools.partial(convolve_kernel, tiled, first_channel //...]
  transfers between devices with their start and end apart: 5 -> 5, of which waited for: 2 -> 2; matrix products, arithmetic and copies ran while one was open for 3% -> 3% of each run, Pallas kernels for 32% -> 34%
where the time goes in v8:
time: 96.8 us; the launch traced here: 96.3 us
  waiting for transfers between devices  36.5 us (38%)
  Pallas kernels  34.6 us (36%)
  starting transfers between devices  21 us (22%)
  local copies, waits for them, and re-layouts  3.95 us (4%)
    all_to_all x2, waiting for transfers between devices, on_device(): relay = lambda part: lax.all_to_all(part, AXES, 0, 0, tiled=True)  36.5 us
    pallas_call x5, Pallas kernels, features(): pl.pallas_call(functools.partial(feature_kernel, phase, found, keep.shape...  14.9 us
    pallas_call x2, Pallas kernels, convolve(): pl.pallas_call(functools.partial(convolve_kernel, tiled, first_channel //...  11.6 us
    all_to_all x2, starting transfers between devices, on_device(): relay = lambda part: lax.all_to_all(part, AXES, 0, 0, tiled=True)  10.9 us
    ppermute x1, starting transfers between devices, on_device(): rims = lax.ppermute(mixed, AXES, following)  4.54 us
    pallas_call x2, Pallas kernels, direct_terms(): pl.pallas_call(functools.partial(direct_kernel, first_channel), in_specs=...  3.79 us
    ppermute x1, starting transfers between devices, on_device(): high_rims = lax.ppermute(high_mixed, AXES, following)  3.21 us
    pallas_call x1, Pallas kernels, prepare(): pl.pallas_call(functools.partial(prepare_kernel, tile, len(streams)), in_...  2.92 us
  transfers between devices with their start and end apart: 5, of which 2 were waited for; matrix products, arithmetic and copies ran while one was open for 3% of the time, Pallas kernels for 34%

profile of v8, /device:TPU:0, one launch (start us, length us, event | category | flops | bytes accessed | tf_op | source)
XLA Modules:
  0.0 96.3 jit_solution(1784100019256636146)
XLA Ops:
  0.0 0.0 copy-start.3
  0.0 0.0 copy-start.2
  0.0 0.0 copy-start.1
  0.0 1.2 %pack_rows.1 = bf16[1,16,9216]{2,1,0:T(8,128)(2,1)S(1)} custom-call(bf16[128,8192]{1,0:T(8,128)(2,1)} %refs_0_.2, bf16[128,8192]{1,0:T(8,128)(2,1)} %refs_0_.3, bf16[128,8192]{1,0:T(8,128)(2,1)} %refs_1_.1), custom_call_target="tpu_custom_call" | custom-call | tf_op jit(solution)/shard_map/pack_rows/pallas_call | solution.py:125
  1.2 2.4 %collective-permute-start = (bf16[1,16,9216]{2,1,0:T(8,128)(2,1)S(1)}, bf16[1,16,9216]{2,1,0:T(8,128)(2,1)S(1)}, u32[]{:S(2)}, u32[]{:S(2)}) collective-permute-start(bf16[1,16,9216]{2,1,0:T(8,128)(2,1)S(1)} %pack_rows.1), channel_id=1, source_target_pairs={{0,1},{1,2},{2,3},{3,4},{4,5},{5,6},{6,7},{7,8},{8,9},{9,10},{10,1... | collective-permute-start | bytes 884744 | tf_op jit(solution)/shard_map/ppermute | solution.py:401
  3.6 0.0 copy-done.3
  3.6 0.0 copy-done.2
  3.7 0.0 copy-done.1
  3.7 2.9 %prepare.1 = (f32[6,128,128]{2,1,0:T(8,128)S(1)}, bf16[256,128]{1,0:T(8,128)(2,1)S(1)}, f32[512,128]{1,0:T(8,128)S(1)}, f32[3,8,8192]{2,1,0:T(8,128)S(1)}, bf16[2,128,8192]{2,1,0:T(8,128)(2,1)S(1)}) custom-call(s32[1]{0:T(128)} %bitcast.place_ref, s32[16]{0:T(128)S(1)} %copy-done.3, bf16[3,7,512]{2,1,0:T(8,128)(2,1)S(1)} %copy-done.2, ...), custom_call_target="tpu_custom_call" | custom-call | flops 1024 | bytes 1024 | tf_op jit(solution)/shard_map/prepare/pallas_call | solution.py:91
  6.6 2.9 %features.5.refs_4_ = bf16[112,3072]{1,0:T(8,128)(2,1)S(1)} custom-call(bf16[2,128,8192]{2,1,0:T(8,128)(2,1)S(1)} %get-tuple-element.20.refs_0_, f32[3,8,8192]{2,1,0:T(8,128)S(1)} %get-tuple-element.21.refs_1_, f32[6,128,128]{2,1,0:T(8,128)S(1)} %get-tuple-element.22.refs_2_), custom_call_target="tpu_custom_call" | custom-call | flops 1024 | bytes 1024 | tf_op jit(solution)/shard_map/features/pallas_call | solution.py:294
  9.5 0.0 collective-permute-done.refs_3_.packed_ref
  9.5 1.0 %features.6.mixed_ref = bf16[32,96,128]{2,1,0:T(8,128)(2,1)S(1)} custom-call(bf16[2,128,8192]{2,1,0:T(8,128)(2,1)S(1)} %get-tuple-element.20.refs_0_, f32[3,8,8192]{2,1,0:T(8,128)S(1)} %get-tuple-element.21.refs_1_, f32[6,128,128]{2,1,0:T(8,128)S(1)} %get-tuple-element.22.refs_2_, bf16[1,16,9216]{2,1,0:T(8,128)(2,1)S(1)} %collective-permute-done.refs_3_.packed_ref, ...), custom_call_target="tpu_custom_call" | custom-call | flops 1024 | bytes 1024 | tf_op jit(solution)/shard_map/features/pallas_call | solution.py:294
  10.5 0.0 copy-start
  10.5 4.5 %collective-permute-start.1 = (bf16[32,96,128]{2,1,0:T(8,128)(2,1)S(1)}, bf16[32,96,128]{2,1,0:T(8,128)(2,1)S(1)}, u32[]{:S(2)}, u32[]{:S(2)}) collective-permute-start(bf16[32,96,128]{2,1,0:T(8,128)(2,1)S(1)} %features.6.mixed_ref), channel_id=1, source_target_pairs={{0,1},{1,2},{2,3},{3,4},{4,5},{5,6},{6,7},{7,8},{8,9},{9,10},{10,1... | collective-permute-start | bytes 2359304 | tf_op jit(solution)/shard_map/ppermute | solution.py:416
  15.0 5.1 %features.7 = (bf16[32,160,128]{2,1,0:T(8,128)(2,1)S(1)}, bf16[1,128,8192]{2,1,0:T(8,128)(2,1)S(1)}) custom-call(bf16[2,128,8192]{2,1,0:T(8,128)(2,1)S(1)} %get-tuple-element.20.refs_0_, f32[3,8,8192]{2,1,0:T(8,128)S(1)} %get-tuple-element.21.refs_1_, f32[6,128,128]{2,1,0:T(8,128)S(1)} %get-tuple-element.22.refs_2_, ...), custom_call_target="tpu_custom_call" | custom-call | flops 1024 | bytes 1024 | tf_op jit(solution)/shard_map/features/pallas_call | solution.py:294
  20.2 3.2 %collective-permute-start.2 = (bf16[32,160,128]{2,1,0:T(8,128)(2,1)S(1)}, bf16[32,160,128]{2,1,0:T(8,128)(2,1)}, u32[]{:S(2)}, u32[]{:S(2)}) collective-permute-start(bf16[32,160,128]{2,1,0:T(8,128)(2,1)S(1)} %get-tuple-element.26.mixed_ref), channel_id=1, source_target_pairs={{0,1},{1,2},{2,3},{3,4},{4,5},{5,6},{6,7},{7,8},{8,9},{9,10},{10,1... | collective-permute-start | bytes 3932168 | tf_op jit(solution)/shard_map/ppermute | solution.py:426
  23.4 0.0 copy-done
  23.4 1.7 %direct_terms.2.direct_ref = f32[32,96,128]{2,1,0:T(8,128)S(1)} custom-call(bf16[32,96,128]{2,1,0:T(8,128)(2,1)S(1)} %features.6.mixed_ref, f32[32,1,256]{2,1,0:T(1,128)S(1)} %bitcast.15), custom_call_target="tpu_custom_call" | custom-call | flops 1024 | bytes 1024 | tf_op jit(solution)/shard_map/direct_terms/pallas_call | solution.py:336
  25.0 0.1 unpack_rows.1.refs_3_
  25.1 1.9 %features.8.gate_ref = bf16[32,96,128]{2,1,0:T(8,128)(2,1)S(1)} custom-call(bf16[1,128,8192]{2,1,0:T(8,128)(2,1)S(1)} %get-tuple-element.25.refs_0_, f32[3,8,8192]{2,1,0:T(8,128)S(1)} %get-tuple-element.21.refs_1_, f32[6,128,128]{2,1,0:T(8,128)S(1)} %get-tuple-element.22.refs_2_, f32[1,8,8192]{2,1,0:T(8,128)S(1)} %unpack_rows.1.refs_3_), custom_call_target="tpu_custom_call" | custom-call | flops 1024 | bytes 1024 | tf_op jit(solution)/shard_map/features/pallas_call | solution.py:294
  27.0 0.0 collective-permute-done.1.rim_ref
  27.0 4.4 %convolve.2 = bf16[32,96,128]{2,1,0:T(8,128)(2,1)} custom-call(bf16[32,96,128]{2,1,0:T(8,128)(2,1)S(1)} %features.6.mixed_ref, bf16[32,96,128]{2,1,0:T(8,128)(2,1)S(1)} %collective-permute-done.1.rim_ref, bf16[32,96,128]{2,1,0:T(8,128)(2,1)S(1)} %features.8.gate_ref, f32[32,96,128]{2,1,0:T(8,128)S(1)} %direct_terms.2.direct_ref, ...), custom_call_target="tpu_custom_call" | custom-call | flops 137438953472 | bytes 1024 | tf_op jit(solution)/shard_map/convolve/pallas_call | solution.py:380
  31.4 5.7 %all-to-all-start = ((bf16[32,96,128]{2,1,0:T(8,128)(2,1)}), bf16[32,96,128]{2,1,0:T(8,128)(2,1)}, u32[]{:S(2)}, u32[]{:S(2)}) async-start(bf16[32,96,128]{2,1,0:T(8,128)(2,1)} %convolve.2), calls=%async_computation | async-start | bytes 1572864 | tf_op jit(solution)/shard_map/all_to_all | solution.py:409
  37.1 2.1 %direct_terms.3.direct_ref = f32[32,160,128]{2,1,0:T(8,128)S(1)} custom-call(bf16[32,160,128]{2,1,0:T(8,128)(2,1)S(1)} %get-tuple-element.26.mixed_ref, f32[32,1,256]{2,1,0:T(1,128)S(1)} %bitcast.16), custom_call_target="tpu_custom_call" | custom-call | flops 1024 | bytes 1024 | tf_op jit(solution)/shard_map/direct_terms/pallas_call | solution.py:336
  39.2 4.1 %features.9.gate_ref = bf16[32,160,128]{2,1,0:T(8,128)(2,1)S(1)} custom-call(bf16[128,8192]{1,0:T(8,128)(2,1)} %refs_0_.3, f32[3,8,8192]{2,1,0:T(8,128)S(1)} %get-tuple-element.21.refs_1_, f32[6,128,128]{2,1,0:T(8,128)S(1)} %get-tuple-element.22.refs_2_, f32[1,8,8192]{2,1,0:T(8,128)S(1)} %unpack_rows.1.refs_3_), custom_call_target="tpu_custom_call" | custom-call | flops 1024 | bytes 1024 | tf_op jit(solution)/shard_map/features/pallas_call | solution.py:294
  43.3 0.0 collective-permute-done.2.rim_ref
  43.3 7.2 %convolve.3 = bf16[32,160,128]{2,1,0:T(8,128)(2,1)} custom-call(bf16[32,160,128]{2,1,0:T(8,128)(2,1)S(1)} %get-tuple-element.26.mixed_ref, bf16[32,160,128]{2,1,0:T(8,128)(2,1)} %collective-permute-done.2.rim_ref, bf16[32,160,128]{2,1,0:T(8,128)(2,1)S(1)} %features.9.gate_ref, f32[32,160,128]{2,1,0:T(8,128)S(1)} %direct_terms.3.direct_ref, ...), custom_call_target="tpu_custom_call" | custom-call | flops 137438953472 | bytes 1024 | tf_op jit(solution)/shard_map/convolve/pallas_call | solution.py:380
  50.6 7.1 %all-to-all-done = bf16[32,96,128]{2,1,0:T(8,128)(2,1)} async-done(((bf16[32,96,128]{2,1,0:T(8,128)(2,1)}), bf16[32,96,128]{2,1,0:T(8,128)(2,1)}, u32[]{:S(2)}, u32[]{:S(2)}) %all-to-all-start) | async-done | bytes 786464 | tf_op jit(solution)/shard_map/all_to_all | solution.py:409
  57.7 5.2 %all-to-all-start.1 = ((bf16[32,160,128]{2,1,0:T(8,128)(2,1)}), bf16[32,160,128]{2,1,0:T(8,128)(2,1)S(1)}, u32[]{:S(2)}, u32[]{:S(2)}) async-start(bf16[32,160,128]{2,1,0:T(8,128)(2,1)} %convolve.3), calls=%async_computation.1 | async-start | bytes 2621440 | tf_op jit(solution)/shard_map/all_to_all | solution.py:409
  62.9 1.2 %copy_bitcast_fusion = bf16[96,4096]{1,0:T(8,128)(2,1)S(1)} fusion(bf16[32,96,128]{2,1,0:T(8,128)(2,1)} %all-to-all-done), kind=kLoop, calls=%fused_computation.1 | loop fusion | bytes 1572864 | tf_op jit(solution)/shard_map/reshape | solution.py:410
  64.1 1.5 %dynamic_update_slice.6 = bf16[256,4096]{1,0:T(8,128)(2,1)} pad(bf16[96,4096]{1,0:T(8,128)(2,1)S(1)} %copy_bitcast_fusion, bf16[]{:T(256)} %constant.16.clone.1), padding=0_160x0_0 | pad | bytes 2883586 | tf_op jit(solution)/shard_map/dynamic_update_slice | solution.py:436
  65.7 29.4 %all-to-all-done.1 = bf16[32,160,128]{2,1,0:T(8,128)(2,1)S(1)} async-done(((bf16[32,160,128]{2,1,0:T(8,128)(2,1)}), bf16[32,160,128]{2,1,0:T(8,128)(2,1)S(1)}, u32[]{:S(2)}, u32[]{:S(2)}) %all-to-all-start.1) | async-done | bytes 1310752 | tf_op jit(solution)/shard_map/all_to_all | solution.py:409
  95.1 1.2 %bitcast_dynamic-update-slice_fusion = bf16[256,4096]{1,0:T(8,128)(2,1)} fusion(bf16[256,4096]{1,0:T(8,128)(2,1)} %dynamic_update_slice.6, bf16[32,160,128]{2,1,0:T(8,128)(2,1)S(1)} %all-to-all-done.1), kind=kLoop, calls=%fused_computation | loop fusion | bytes 2621440 | tf_op jit(solution)/shard_map/dynamic_update_slice | solution.py:440
Async XLA Ops:
  0.0 3.6 %copy-start.3 = (s32[16]{0:T(128)S(1)}, s32[16]{0:T(128)}, u32[]{:S(2)}) copy-start(s32[16]{0:T(128)} %lengths_ref) | copy-start | bytes 196
  0.0 3.6 %copy-start.2 = (bf16[3,7,512]{2,1,0:T(8,128)(2,1)S(1)}, bf16[3,7,512]{2,1,0:T(8,128)(2,1)}, u32[]{:S(2)}) copy-start(bf16[3,7,512]{2,1,0:T(8,128)(2,1)} %short_ref.1) | copy-start | bytes 64516
  0.0 3.7 %copy-start.1 = (bf16[128,512]{1,0:T(8,128)(2,1)S(1)}, bf16[128,512]{1,0:T(8,128)(2,1)}, u32[]{:S(2)}) copy-start(bf16[128,512]{1,0:T(8,128)(2,1)} %long_ref.1) | copy-start | bytes 393220
  1.2 8.2 %collective-permute-start = (bf16[1,16,9216]{2,1,0:T(8,128)(2,1)S(1)}, bf16[1,16,9216]{2,1,0:T(8,128)(2,1)S(1)}, u32[]{:S(2)}, u32[]{:S(2)}) collective-permute-start(bf16[1,16,9216]{2,1,0:T(8,128)(2,1)S(1)} %pack_rows.1), channel_id=1, source_target_pairs={{0,1},{1,2},{2,3},{3,4},{4,5},{5,6},{6,7},{7,8},{8,9},{9,10},{10,1... | collective-permute-start | bytes 884744 | tf_op jit(solution)/shard_map/ppermute | solution.py:401
  10.5 12.9 %copy-start = (f32[8192]{0:T(1024)S(1)}, f32[8192]{0:T(1024)}, u32[]{:S(2)}) copy-start(f32[8192]{0:T(1024)} %param.12) | copy-start | bytes 98308
  10.5 16.5 %collective-permute-start.1 = (bf16[32,96,128]{2,1,0:T(8,128)(2,1)S(1)}, bf16[32,96,128]{2,1,0:T(8,128)(2,1)S(1)}, u32[]{:S(2)}, u32[]{:S(2)}) collective-permute-start(bf16[32,96,128]{2,1,0:T(8,128)(2,1)S(1)} %features.6.mixed_ref), channel_id=1, source_target_pairs={{0,1},{1,2},{2,3},{3,4},{4,5},{5,6},{6,7},{7,8},{8,9},{9,10},{10,1... | collective-permute-start | bytes 2359304 | tf_op jit(solution)/shard_map/ppermute | solution.py:416
  20.2 23.2 %collective-permute-start.2 = (bf16[32,160,128]{2,1,0:T(8,128)(2,1)S(1)}, bf16[32,160,128]{2,1,0:T(8,128)(2,1)}, u32[]{:S(2)}, u32[]{:S(2)}) collective-permute-start(bf16[32,160,128]{2,1,0:T(8,128)(2,1)S(1)} %get-tuple-element.26.mixed_ref), channel_id=1, source_target_pairs={{0,1},{1,2},{2,3},{3,4},{4,5},{5,6},{6,7},{7,8},{8,9},{9,10},{10,1... | collective-permute-start | bytes 3932168 | tf_op jit(solution)/shard_map/ppermute | solution.py:426
  31.4 26.3 %all-to-all-start = ((bf16[32,96,128]{2,1,0:T(8,128)(2,1)}), bf16[32,96,128]{2,1,0:T(8,128)(2,1)}, u32[]{:S(2)}, u32[]{:S(2)}) async-start(bf16[32,96,128]{2,1,0:T(8,128)(2,1)} %convolve.2), calls=%async_computation | async-start | bytes 1572864 | tf_op jit(solution)/shard_map/all_to_all | solution.py:409
  57.7 37.4 %all-to-all-start.1 = ((bf16[32,160,128]{2,1,0:T(8,128)(2,1)}), bf16[32,160,128]{2,1,0:T(8,128)(2,1)S(1)}, u32[]{:S(2)}, u32[]{:S(2)}) async-start(bf16[32,160,128]{2,1,0:T(8,128)(2,1)} %convolve.3), calls=%async_computation.1 | async-start | bytes 2621440 | tf_op jit(solution)/shard_map/all_to_all | solution.py:409

commit v9 on v8

--- a/solution.py
+++ b/solution.py
@@ -126,8 +126,8 @@
         pack_kernel,
         grid=(1,),
         in_specs=[pl.BlockSpec((16, channels), lambda i: (rows // 16 - 1, 0))] * len(streams),
-        out_specs=pl.BlockSpec((1, 16, width), lambda i: (0, 0, 0)),
-        out_shape=jax.ShapeDtypeStruct((1, 16, width), jnp.bfloat16),
+        out_specs=VMEM_SPEC,
+        out_shape=pltpu.VMEM((1, 16, width), jnp.bfloat16),
         compiler_params=pltpu.CompilerParams(vmem_limit_bytes=VMEM_LIMIT),
         name="pack_rows",
     )(*far(*streams))

time: 96.8 us -> 96.8 us (level)
  no operation moved by 1% of the time
where the time goes in v9:
time: 96.8 us; the launch traced here: 96.3 us
  waiting for transfers between devices  36.5 us (38%)
  Pallas kernels  34.6 us (36%)
  starting transfers between devices  21 us (22%)
  local copies, waits for them, and re-layouts  3.95 us (4%)
    all_to_all x2, waiting for transfers between devices, on_device(): relay = lambda part: lax.all_to_all(part, AXES, 0, 0, tiled=True)  36.5 us
    pallas_call x5, Pallas kernels, features(): pl.pallas_call(functools.partial(feature_kernel, phase, found, keep.shape...  14.9 us
    pallas_call x2, Pallas kernels, convolve(): pl.pallas_call(functools.partial(convolve_kernel, tiled, first_channel //...  11.6 us
    all_to_all x2, starting transfers between devices, on_device(): relay = lambda part: lax.all_to_all(part, AXES, 0, 0, tiled=True)  10.9 us
    ppermute x1, starting transfers between devices, on_device(): rims = lax.ppermute(mixed, AXES, following)  4.54 us
    pallas_call x2, Pallas kernels, direct_terms(): pl.pallas_call(functools.partial(direct_kernel, first_channel), in_specs=...  3.79 us
    ppermute x1, starting transfers between devices, on_device(): high_rims = lax.ppermute(high_mixed, AXES, following)  3.21 us
    pallas_call x1, Pallas kernels, prepare(): pl.pallas_call(functools.partial(prepare_kernel, tile, len(streams)), in_...  2.92 us
  transfers between devices with their start and end apart: 5, of which 2 were waited for; matrix products, arithmetic and copies ran while one was open for 3% of the time, Pallas kernels for 34%

profile of v9, /device:TPU:0, one launch (start us, length us, event | category | flops | bytes accessed | tf_op | source)
XLA Modules:
  0.0 96.3 jit_solution(1784100019256636146)
XLA Ops:
  0.0 0.0 copy-start.3
  0.0 0.0 copy-start.2
  0.0 0.0 copy-start.1
  0.0 1.2 %pack_rows.1 = bf16[1,16,9216]{2,1,0:T(8,128)(2,1)S(1)} custom-call(bf16[128,8192]{1,0:T(8,128)(2,1)} %refs_0_.2, bf16[128,8192]{1,0:T(8,128)(2,1)} %refs_0_.3, bf16[128,8192]{1,0:T(8,128)(2,1)} %refs_1_.1), custom_call_target="tpu_custom_call" | custom-call | tf_op jit(solution)/shard_map/pack_rows/pallas_call | solution.py:125
  1.2 2.4 %collective-permute-start = (bf16[1,16,9216]{2,1,0:T(8,128)(2,1)S(1)}, bf16[1,16,9216]{2,1,0:T(8,128)(2,1)S(1)}, u32[]{:S(2)}, u32[]{:S(2)}) collective-permute-start(bf16[1,16,9216]{2,1,0:T(8,128)(2,1)S(1)} %pack_rows.1), channel_id=1, source_target_pairs={{0,1},{1,2},{2,3},{3,4},{4,5},{5,6},{6,7},{7,8},{8,9},{9,10},{10,1... | collective-permute-start | bytes 884744 | tf_op jit(solution)/shard_map/ppermute | solution.py:401
  3.6 0.0 copy-done.3
  3.6 0.0 copy-done.2
  3.7 0.0 copy-done.1
  3.7 2.9 %prepare.1 = (f32[6,128,128]{2,1,0:T(8,128)S(1)}, bf16[256,128]{1,0:T(8,128)(2,1)S(1)}, f32[512,128]{1,0:T(8,128)S(1)}, f32[3,8,8192]{2,1,0:T(8,128)S(1)}, bf16[2,128,8192]{2,1,0:T(8,128)(2,1)S(1)}) custom-call(s32[1]{0:T(128)} %bitcast.place_ref, s32[16]{0:T(128)S(1)} %copy-done.3, bf16[3,7,512]{2,1,0:T(8,128)(2,1)S(1)} %copy-done.2, ...), custom_call_target="tpu_custom_call" | custom-call | flops 1024 | bytes 1024 | tf_op jit(solution)/shard_map/prepare/pallas_call | solution.py:91
  6.6 2.9 %features.5.refs_4_ = bf16[112,3072]{1,0:T(8,128)(2,1)S(1)} custom-call(bf16[2,128,8192]{2,1,0:T(8,128)(2,1)S(1)} %get-tuple-element.20.refs_0_, f32[3,8,8192]{2,1,0:T(8,128)S(1)} %get-tuple-element.21.refs_1_, f32[6,128,128]{2,1,0:T(8,128)S(1)} %get-tuple-element.22.refs_2_), custom_call_target="tpu_custom_call" | custom-call | flops 1024 | bytes 1024 | tf_op jit(solution)/shard_map/features/pallas_call | solution.py:294
  9.5 0.0 collective-permute-done.refs_3_.packed_ref
  9.5 1.0 %features.6.mixed_ref = bf16[32,96,128]{2,1,0:T(8,128)(2,1)S(1)} custom-call(bf16[2,128,8192]{2,1,0:T(8,128)(2,1)S(1)} %get-tuple-element.20.refs_0_, f32[3,8,8192]{2,1,0:T(8,128)S(1)} %get-tuple-element.21.refs_1_, f32[6,128,128]{2,1,0:T(8,128)S(1)} %get-tuple-element.22.refs_2_, bf16[1,16,9216]{2,1,0:T(8,128)(2,1)S(1)} %collective-permute-done.refs_3_.packed_ref, ...), custom_call_target="tpu_custom_call" | custom-call | flops 1024 | bytes 1024 | tf_op jit(solution)/shard_map/features/pallas_call | solution.py:294
  10.5 0.0 copy-start
  10.5 4.5 %collective-permute-start.1 = (bf16[32,96,128]{2,1,0:T(8,128)(2,1)S(1)}, bf16[32,96,128]{2,1,0:T(8,128)(2,1)S(1)}, u32[]{:S(2)}, u32[]{:S(2)}) collective-permute-start(bf16[32,96,128]{2,1,0:T(8,128)(2,1)S(1)} %features.6.mixed_ref), channel_id=1, source_target_pairs={{0,1},{1,2},{2,3},{3,4},{4,5},{5,6},{6,7},{7,8},{8,9},{9,10},{10,1... | collective-permute-start | bytes 2359304 | tf_op jit(solution)/shard_map/ppermute | solution.py:416
  15.0 5.1 %features.7 = (bf16[32,160,128]{2,1,0:T(8,128)(2,1)S(1)}, bf16[1,128,8192]{2,1,0:T(8,128)(2,1)S(1)}) custom-call(bf16[2,128,8192]{2,1,0:T(8,128)(2,1)S(1)} %get-tuple-element.20.refs_0_, f32[3,8,8192]{2,1,0:T(8,128)S(1)} %get-tuple-element.21.refs_1_, f32[6,128,128]{2,1,0:T(8,128)S(1)} %get-tuple-element.22.refs_2_, ...), custom_call_target="tpu_custom_call" | custom-call | flops 1024 | bytes 1024 | tf_op jit(solution)/shard_map/features/pallas_call | solution.py:294
  20.2 3.2 %collective-permute-start.2 = (bf16[32,160,128]{2,1,0:T(8,128)(2,1)S(1)}, bf16[32,160,128]{2,1,0:T(8,128)(2,1)}, u32[]{:S(2)}, u32[]{:S(2)}) collective-permute-start(bf16[32,160,128]{2,1,0:T(8,128)(2,1)S(1)} %get-tuple-element.26.mixed_ref), channel_id=1, source_target_pairs={{0,1},{1,2},{2,3},{3,4},{4,5},{5,6},{6,7},{7,8},{8,9},{9,10},{10,1... | collective-permute-start | bytes 3932168 | tf_op jit(solution)/shard_map/ppermute | solution.py:426
  23.4 0.0 copy-done
  23.4 1.7 %direct_terms.2.direct_ref = f32[32,96,128]{2,1,0:T(8,128)S(1)} custom-call(bf16[32,96,128]{2,1,0:T(8,128)(2,1)S(1)} %features.6.mixed_ref, f32[32,1,256]{2,1,0:T(1,128)S(1)} %bitcast.15), custom_call_target="tpu_custom_call" | custom-call | flops 1024 | bytes 1024 | tf_op jit(solution)/shard_map/direct_terms/pallas_call | solution.py:336
  25.0 0.1 unpack_rows.1.refs_3_
  25.1 1.9 %features.8.gate_ref = bf16[32,96,128]{2,1,0:T(8,128)(2,1)S(1)} custom-call(bf16[1,128,8192]{2,1,0:T(8,128)(2,1)S(1)} %get-tuple-element.25.refs_0_, f32[3,8,8192]{2,1,0:T(8,128)S(1)} %get-tuple-element.21.refs_1_, f32[6,128,128]{2,1,0:T(8,128)S(1)} %get-tuple-element.22.refs_2_, f32[1,8,8192]{2,1,0:T(8,128)S(1)} %unpack_rows.1.refs_3_), custom_call_target="tpu_custom_call" | custom-call | flops 1024 | bytes 1024 | tf_op jit(solution)/shard_map/features/pallas_call | solution.py:294
  27.0 0.0 collective-permute-done.1.rim_ref
  27.0 4.4 %convolve.2 = bf16[32,96,128]{2,1,0:T(8,128)(2,1)} custom-call(bf16[32,96,128]{2,1,0:T(8,128)(2,1)S(1)} %features.6.mixed_ref, bf16[32,96,128]{2,1,0:T(8,128)(2,1)S(1)} %collective-permute-done.1.rim_ref, bf16[32,96,128]{2,1,0:T(8,128)(2,1)S(1)} %features.8.gate_ref, f32[32,96,128]{2,1,0:T(8,128)S(1)} %direct_terms.2.direct_ref, ...), custom_call_target="tpu_custom_call" | custom-call | flops 137438953472 | bytes 1024 | tf_op jit(solution)/shard_map/convolve/pallas_call | solution.py:380
  31.4 5.7 %all-to-all-start = ((bf16[32,96,128]{2,1,0:T(8,128)(2,1)}), bf16[32,96,128]{2,1,0:T(8,128)(2,1)}, u32[]{:S(2)}, u32[]{:S(2)}) async-start(bf16[32,96,128]{2,1,0:T(8,128)(2,1)} %convolve.2), calls=%async_computation | async-start | bytes 1572864 | tf_op jit(solution)/shard_map/all_to_all | solution.py:409
  37.1 2.1 %direct_terms.3.direct_ref = f32[32,160,128]{2,1,0:T(8,128)S(1)} custom-call(bf16[32,160,128]{2,1,0:T(8,128)(2,1)S(1)} %get-tuple-element.26.mixed_ref, f32[32,1,256]{2,1,0:T(1,128)S(1)} %bitcast.16), custom_call_target="tpu_custom_call" | custom-call | flops 1024 | bytes 1024 | tf_op jit(solution)/shard_map/direct_terms/pallas_call | solution.py:336
  39.2 4.1 %features.9.gate_ref = bf16[32,160,128]{2,1,0:T(8,128)(2,1)S(1)} custom-call(bf16[128,8192]{1,0:T(8,128)(2,1)} %refs_0_.3, f32[3,8,8192]{2,1,0:T(8,128)S(1)} %get-tuple-element.21.refs_1_, f32[6,128,128]{2,1,0:T(8,128)S(1)} %get-tuple-element.22.refs_2_, f32[1,8,8192]{2,1,0:T(8,128)S(1)} %unpack_rows.1.refs_3_), custom_call_target="tpu_custom_call" | custom-call | flops 1024 | bytes 1024 | tf_op jit(solution)/shard_map/features/pallas_call | solution.py:294
  43.3 0.0 collective-permute-done.2.rim_ref
  43.3 7.2 %convolve.3 = bf16[32,160,128]{2,1,0:T(8,128)(2,1)} custom-call(bf16[32,160,128]{2,1,0:T(8,128)(2,1)S(1)} %get-tuple-element.26.mixed_ref, bf16[32,160,128]{2,1,0:T(8,128)(2,1)} %collective-permute-done.2.rim_ref, bf16[32,160,128]{2,1,0:T(8,128)(2,1)S(1)} %features.9.gate_ref, f32[32,160,128]{2,1,0:T(8,128)S(1)} %direct_terms.3.direct_ref, ...), custom_call_target="tpu_custom_call" | custom-call | flops 137438953472 | bytes 1024 | tf_op jit(solution)/shard_map/convolve/pallas_call | solution.py:380
  50.6 7.1 %all-to-all-done = bf16[32,96,128]{2,1,0:T(8,128)(2,1)} async-done(((bf16[32,96,128]{2,1,0:T(8,128)(2,1)}), bf16[32,96,128]{2,1,0:T(8,128)(2,1)}, u32[]{:S(2)}, u32[]{:S(2)}) %all-to-all-start) | async-done | bytes 786464 | tf_op jit(solution)/shard_map/all_to_all | solution.py:409
  57.7 5.2 %all-to-all-start.1 = ((bf16[32,160,128]{2,1,0:T(8,128)(2,1)}), bf16[32,160,128]{2,1,0:T(8,128)(2,1)S(1)}, u32[]{:S(2)}, u32[]{:S(2)}) async-start(bf16[32,160,128]{2,1,0:T(8,128)(2,1)} %convolve.3), calls=%async_computation.1 | async-start | bytes 2621440 | tf_op jit(solution)/shard_map/all_to_all | solution.py:409
  62.9 1.2 %copy_bitcast_fusion = bf16[96,4096]{1,0:T(8,128)(2,1)S(1)} fusion(bf16[32,96,128]{2,1,0:T(8,128)(2,1)} %all-to-all-done), kind=kLoop, calls=%fused_computation.1 | loop fusion | bytes 1572864 | tf_op jit(solution)/shard_map/reshape | solution.py:410
  64.1 1.5 %dynamic_update_slice.6 = bf16[256,4096]{1,0:T(8,128)(2,1)} pad(bf16[96,4096]{1,0:T(8,128)(2,1)S(1)} %copy_bitcast_fusion, bf16[]{:T(256)} %constant.16.clone.1), padding=0_160x0_0 | pad | bytes 2883586 | tf_op jit(solution)/shard_map/dynamic_update_slice | solution.py:436
  65.7 29.4 %all-to-all-done.1 = bf16[32,160,128]{2,1,0:T(8,128)(2,1)S(1)} async-done(((bf16[32,160,128]{2,1,0:T(8,128)(2,1)}), bf16[32,160,128]{2,1,0:T(8,128)(2,1)S(1)}, u32[]{:S(2)}, u32[]{:S(2)}) %all-to-all-start.1) | async-done | bytes 1310752 | tf_op jit(solution)/shard_map/all_to_all | solution.py:409
  95.1 1.2 %bitcast_dynamic-update-slice_fusion = bf16[256,4096]{1,0:T(8,128)(2,1)} fusion(bf16[256,4096]{1,0:T(8,128)(2,1)} %dynamic_update_slice.6, bf16[32,160,128]{2,1,0:T(8,128)(2,1)S(1)} %all-to-all-done.1), kind=kLoop, calls=%fused_computation | loop fusion | bytes 2621440 | tf_op jit(solution)/shard_map/dynamic_update_slice | solution.py:440
Async XLA Ops:
  0.0 3.6 %copy-start.3 = (s32[16]{0:T(128)S(1)}, s32[16]{0:T(128)}, u32[]{:S(2)}) copy-start(s32[16]{0:T(128)} %lengths_ref) | copy-start | bytes 196
  0.0 3.6 %copy-start.2 = (bf16[3,7,512]{2,1,0:T(8,128)(2,1)S(1)}, bf16[3,7,512]{2,1,0:T(8,128)(2,1)}, u32[]{:S(2)}) copy-start(bf16[3,7,512]{2,1,0:T(8,128)(2,1)} %short_ref.1) | copy-start | bytes 64516
  0.0 3.7 %copy-start.1 = (bf16[128,512]{1,0:T(8,128)(2,1)S(1)}, bf16[128,512]{1,0:T(8,128)(2,1)}, u32[]{:S(2)}) copy-start(bf16[128,512]{1,0:T(8,128)(2,1)} %long_ref.1) | copy-start | bytes 393220
  1.2 8.2 %collective-permute-start = (bf16[1,16,9216]{2,1,0:T(8,128)(2,1)S(1)}, bf16[1,16,9216]{2,1,0:T(8,128)(2,1)S(1)}, u32[]{:S(2)}, u32[]{:S(2)}) collective-permute-start(bf16[1,16,9216]{2,1,0:T(8,128)(2,1)S(1)} %pack_rows.1), channel_id=1, source_target_pairs={{0,1},{1,2},{2,3},{3,4},{4,5},{5,6},{6,7},{7,8},{8,9},{9,10},{10,1... | collective-permute-start | bytes 884744 | tf_op jit(solution)/shard_map/ppermute | solution.py:401
  10.5 12.9 %copy-start = (f32[8192]{0:T(1024)S(1)}, f32[8192]{0:T(1024)}, u32[]{:S(2)}) copy-start(f32[8192]{0:T(1024)} %param.12) | copy-start | bytes 98308
  10.5 16.5 %collective-permute-start.1 = (bf16[32,96,128]{2,1,0:T(8,128)(2,1)S(1)}, bf16[32,96,128]{2,1,0:T(8,128)(2,1)S(1)}, u32[]{:S(2)}, u32[]{:S(2)}) collective-permute-start(bf16[32,96,128]{2,1,0:T(8,128)(2,1)S(1)} %features.6.mixed_ref), channel_id=1, source_target_pairs={{0,1},{1,2},{2,3},{3,4},{4,5},{5,6},{6,7},{7,8},{8,9},{9,10},{10,1... | collective-permute-start | bytes 2359304 | tf_op jit(solution)/shard_map/ppermute | solution.py:416
  20.2 23.2 %collective-permute-start.2 = (bf16[32,160,128]{2,1,0:T(8,128)(2,1)S(1)}, bf16[32,160,128]{2,1,0:T(8,128)(2,1)}, u32[]{:S(2)}, u32[]{:S(2)}) collective-permute-start(bf16[32,160,128]{2,1,0:T(8,128)(2,1)S(1)} %get-tuple-element.26.mixed_ref), channel_id=1, source_target_pairs={{0,1},{1,2},{2,3},{3,4},{4,5},{5,6},{6,7},{7,8},{8,9},{9,10},{10,1... | collective-permute-start | bytes 3932168 | tf_op jit(solution)/shard_map/ppermute | solution.py:426
  31.4 26.3 %all-to-all-start = ((bf16[32,96,128]{2,1,0:T(8,128)(2,1)}), bf16[32,96,128]{2,1,0:T(8,128)(2,1)}, u32[]{:S(2)}, u32[]{:S(2)}) async-start(bf16[32,96,128]{2,1,0:T(8,128)(2,1)} %convolve.2), calls=%async_computation | async-start | bytes 1572864 | tf_op jit(solution)/shard_map/all_to_all | solution.py:409
  57.7 37.4 %all-to-all-start.1 = ((bf16[32,160,128]{2,1,0:T(8,128)(2,1)}), bf16[32,160,128]{2,1,0:T(8,128)(2,1)S(1)}, u32[]{:S(2)}, u32[]{:S(2)}) async-start(bf16[32,160,128]{2,1,0:T(8,128)(2,1)} %convolve.3), calls=%async_computation.1 | async-start | bytes 2621440 | tf_op jit(solution)/shard_map/all_to_all | solution.py:409

commit v10 on v7

--- a/solution.py
+++ b/solution.py
@@ -352,7 +352,7 @@
 def convolve(mixed, rim, gate, skip_gain, taps, keep, first_channel, own_count):
     owners, count, rows = mixed.shape
     tiled = first_channel > 0
-    steps = min(owners, 2 if 2 * count <= own_count else 4)
+    steps = min(owners, 4)
     part_spec = pl.BlockSpec((owners // steps, count, rows), lambda i: (i, 0, 0))
     return pl.pallas_call(
         functools.partial(convolve_kernel, tiled, first_channel // GROUP, own_count // GROUP),

time: 96.7 us -> 96.7 us (level)
  no operation moved by 1% of the time
where the time goes in v10:
time: 96.7 us; the launch traced here: 96.2 us
  waiting for transfers between devices  37 us (38%)
  Pallas kernels  33.2 us (34%)
  starting transfers between devices  21.9 us (23%)
  local copies, waits for them, and re-layouts  3.95 us (4%)
    all_to_all x2, waiting for transfers between devices, on_device(): relay = lambda part: lax.all_to_all(part, AXES, 0, 0, tiled=True)  37 us
    pallas_call x5, Pallas kernels, features(): pl.pallas_call(functools.partial(feature_kernel, phase, found, keep.shape...  14.9 us
    pallas_call x2, Pallas kernels, convolve(): pl.pallas_call(functools.partial(convolve_kernel, tiled, first_channel //...  14.1 us
    all_to_all x2, starting transfers between devices, on_device(): relay = lambda part: lax.all_to_all(part, AXES, 0, 0, tiled=True)  11.8 us
    ppermute x1, starting transfers between devices, on_device(): rims = lax.ppermute(mixed, AXES, following)  4.54 us
    ppermute x1, starting transfers between devices, on_device(): high_rims = lax.ppermute(high_mixed, AXES, following)  3.21 us
    pallas_call x1, Pallas kernels, prepare(): pl.pallas_call(functools.partial(prepare_kernel, tile, len(streams)), in_...  2.92 us
    ppermute x1, starting transfers between devices, on_device(): rim = lax.ppermute(last, AXES, following)  2.38 us
  transfers between devices with their start and end apart: 5, of which 2 were waited for; matrix products, arithmetic and copies ran while one was open for 3% of the time, Pallas kernels for 32%

profile of v10, /device:TPU:0, one launch (start us, length us, event | category | flops | bytes accessed | tf_op | source)
XLA Modules:
  0.0 96.2 jit_solution(15878785703845080301)
XLA Ops:
  0.0 0.0 copy-start.2
  0.0 0.0 copy-start
  0.0 0.0 copy-start.1
  0.0 1.2 %pack_rows.1 = bf16[1,16,9216]{2,1,0:T(8,128)(2,1)S(1)} custom-call(bf16[128,8192]{1,0:T(8,128)(2,1)} %refs_0_.2, bf16[128,8192]{1,0:T(8,128)(2,1)} %refs_0_.3, bf16[128,8192]{1,0:T(8,128)(2,1)} %refs_1_.1), custom_call_target="tpu_custom_call" | custom-call | tf_op jit(solution)/shard_map/pack_rows/pallas_call | solution.py:125
  1.2 2.4 %collective-permute-start = (bf16[1,16,9216]{2,1,0:T(8,128)(2,1)S(1)}, bf16[1,16,9216]{2,1,0:T(8,128)(2,1)S(1)}, u32[]{:S(2)}, u32[]{:S(2)}) collective-permute-start(bf16[1,16,9216]{2,1,0:T(8,128)(2,1)S(1)} %pack_rows.1), channel_id=1, source_target_pairs={{0,1},{1,2},{2,3},{3,4},{4,5},{5,6},{6,7},{7,8},{8,9},{9,10},{10,1... | collective-permute-start | bytes 884744 | tf_op jit(solution)/shard_map/ppermute | solution.py:378
  3.6 0.0 copy-done.2
  3.6 0.0 copy-done
  3.7 0.0 copy-done.1
  3.7 2.9 %prepare.1 = (f32[6,128,128]{2,1,0:T(8,128)S(1)}, bf16[256,128]{1,0:T(8,128)(2,1)S(1)}, f32[512,128]{1,0:T(8,128)S(1)}, f32[3,8,8192]{2,1,0:T(8,128)S(1)}, bf16[2,128,8192]{2,1,0:T(8,128)(2,1)S(1)}) custom-call(s32[1]{0:T(128)} %bitcast.place_ref, s32[16]{0:T(128)S(1)} %copy-done.2, bf16[3,7,512]{2,1,0:T(8,128)(2,1)S(1)} %copy-done.1, ...), custom_call_target="tpu_custom_call" | custom-call | flops 1024 | bytes 1024 | tf_op jit(solution)/shard_map/prepare/pallas_call | solution.py:91
  6.6 2.9 %features.5.refs_4_ = bf16[112,3072]{1,0:T(8,128)(2,1)S(1)} custom-call(bf16[2,128,8192]{2,1,0:T(8,128)(2,1)S(1)} %get-tuple-element.18.refs_0_, f32[3,8,8192]{2,1,0:T(8,128)S(1)} %get-tuple-element.19.refs_1_, f32[6,128,128]{2,1,0:T(8,128)S(1)} %get-tuple-element.20.refs_2_), custom_call_target="tpu_custom_call" | custom-call | flops 1024 | bytes 1024 | tf_op jit(solution)/shard_map/features/pallas_call | solution.py:294
  9.5 0.0 collective-permute-done.refs_3_.packed_ref
  9.5 1.0 %features.6.mixed_ref = bf16[32,96,128]{2,1,0:T(8,128)(2,1)S(1)} custom-call(bf16[2,128,8192]{2,1,0:T(8,128)(2,1)S(1)} %get-tuple-element.18.refs_0_, f32[3,8,8192]{2,1,0:T(8,128)S(1)} %get-tuple-element.19.refs_1_, f32[6,128,128]{2,1,0:T(8,128)S(1)} %get-tuple-element.20.refs_2_, bf16[1,16,9216]{2,1,0:T(8,128)(2,1)S(1)} %collective-permute-done.refs_3_.packed_ref, ...), custom_call_target="tpu_custom_call" | custom-call | flops 1024 | bytes 1024 | tf_op jit(solution)/shard_map/features/pallas_call | solution.py:294
  10.5 4.5 %collective-permute-start.1 = (bf16[32,96,128]{2,1,0:T(8,128)(2,1)S(1)}, bf16[32,96,128]{2,1,0:T(8,128)(2,1)S(1)}, u32[]{:S(2)}, u32[]{:S(2)}) collective-permute-start(bf16[32,96,128]{2,1,0:T(8,128)(2,1)S(1)} %features.6.mixed_ref), channel_id=1, source_target_pairs={{0,1},{1,2},{2,3},{3,4},{4,5},{5,6},{6,7},{7,8},{8,9},{9,10},{10,1... | collective-permute-start | bytes 2359304 | tf_op jit(solution)/shard_map/ppermute | solution.py:393
  15.0 5.1 %features.7 = (bf16[32,160,128]{2,1,0:T(8,128)(2,1)S(1)}, bf16[1,128,8192]{2,1,0:T(8,128)(2,1)S(1)}) custom-call(bf16[2,128,8192]{2,1,0:T(8,128)(2,1)S(1)} %get-tuple-element.18.refs_0_, f32[3,8,8192]{2,1,0:T(8,128)S(1)} %get-tuple-element.19.refs_1_, f32[6,128,128]{2,1,0:T(8,128)S(1)} %get-tuple-element.20.refs_2_, ...), custom_call_target="tpu_custom_call" | custom-call | flops 1024 | bytes 1024 | tf_op jit(solution)/shard_map/features/pallas_call | solution.py:294
  20.1 3.2 %collective-permute-start.2 = (bf16[32,160,128]{2,1,0:T(8,128)(2,1)S(1)}, bf16[32,160,128]{2,1,0:T(8,128)(2,1)}, u32[]{:S(2)}, u32[]{:S(2)}) collective-permute-start(bf16[32,160,128]{2,1,0:T(8,128)(2,1)S(1)} %get-tuple-element.24.mixed_ref), channel_id=1, source_target_pairs={{0,1},{1,2},{2,3},{3,4},{4,5},{5,6},{6,7},{7,8},{8,9},{9,10},{10,1... | collective-permute-start | bytes 3932168 | tf_op jit(solution)/shard_map/ppermute | solution.py:402
  23.4 0.1 unpack_rows.1.refs_3_
  23.4 0.0 copy-start.3
  23.4 1.9 %features.8.gate_ref = bf16[32,96,128]{2,1,0:T(8,128)(2,1)S(1)} custom-call(bf16[1,128,8192]{2,1,0:T(8,128)(2,1)S(1)} %get-tuple-element.23.refs_0_, f32[3,8,8192]{2,1,0:T(8,128)S(1)} %get-tuple-element.19.refs_1_, f32[6,128,128]{2,1,0:T(8,128)S(1)} %get-tuple-element.20.refs_2_, f32[1,8,8192]{2,1,0:T(8,128)S(1)} %unpack_rows.1.refs_3_), custom_call_target="tpu_custom_call" | custom-call | flops 1024 | bytes 1024 | tf_op jit(solution)/shard_map/features/pallas_call | solution.py:294
  25.3 0.0 collective-permute-done.1.rim_ref
  25.3 0.0 copy-done.3
  25.3 5.2 %convolve.2 = bf16[32,96,128]{2,1,0:T(8,128)(2,1)} custom-call(bf16[32,96,128]{2,1,0:T(8,128)(2,1)S(1)} %features.6.mixed_ref, bf16[32,96,128]{2,1,0:T(8,128)(2,1)S(1)} %collective-permute-done.1.rim_ref, bf16[32,96,128]{2,1,0:T(8,128)(2,1)S(1)} %features.8.gate_ref, f32[32,1,256]{2,1,0:T(1,128)S(1)} %bitcast.14, f32[512,128]{1,0:T(8,128)S(1)} %get-tuple-element.26.taps_ref, ...), custom_call_target="tpu_custom_call" | custom-call | flops 137438953472 | bytes 1024 | tf_op jit(solution)/shard_map/convolve/pallas_call | solution.py:357
  30.5 7.3 %all-to-all-start = ((bf16[32,96,128]{2,1,0:T(8,128)(2,1)}), bf16[32,96,128]{2,1,0:T(8,128)(2,1)}, u32[]{:S(2)}, u32[]{:S(2)}) async-start(bf16[32,96,128]{2,1,0:T(8,128)(2,1)} %convolve.2), calls=%async_computation | async-start | bytes 1572864 | tf_op jit(solution)/shard_map/all_to_all | solution.py:386
  37.9 4.1 %features.9.gate_ref = bf16[32,160,128]{2,1,0:T(8,128)(2,1)S(1)} custom-call(bf16[128,8192]{1,0:T(8,128)(2,1)} %refs_0_.3, f32[3,8,8192]{2,1,0:T(8,128)S(1)} %get-tuple-element.19.refs_1_, f32[6,128,128]{2,1,0:T(8,128)S(1)} %get-tuple-element.20.refs_2_, f32[1,8,8192]{2,1,0:T(8,128)S(1)} %unpack_rows.1.refs_3_), custom_call_target="tpu_custom_call" | custom-call | flops 1024 | bytes 1024 | tf_op jit(solution)/shard_map/features/pallas_call | solution.py:294
  41.9 0.0 collective-permute-done.2.rim_ref
  42.0 8.9 %convolve.3 = bf16[32,160,128]{2,1,0:T(8,128)(2,1)} custom-call(bf16[32,160,128]{2,1,0:T(8,128)(2,1)S(1)} %get-tuple-element.24.mixed_ref, bf16[32,160,128]{2,1,0:T(8,128)(2,1)} %collective-permute-done.2.rim_ref, bf16[32,160,128]{2,1,0:T(8,128)(2,1)S(1)} %features.9.gate_ref, f32[32,1,256]{2,1,0:T(1,128)S(1)} %bitcast.15, ...), custom_call_target="tpu_custom_call" | custom-call | flops 137438953472 | bytes 1024 | tf_op jit(solution)/shard_map/convolve/pallas_call | solution.py:357
  50.9 7.6 %all-to-all-done = bf16[32,96,128]{2,1,0:T(8,128)(2,1)} async-done(((bf16[32,96,128]{2,1,0:T(8,128)(2,1)}), bf16[32,96,128]{2,1,0:T(8,128)(2,1)}, u32[]{:S(2)}, u32[]{:S(2)}) %all-to-all-start) | async-done | bytes 786464 | tf_op jit(solution)/shard_map/all_to_all | solution.py:386
  58.5 4.4 %all-to-all-start.1 = ((bf16[32,160,128]{2,1,0:T(8,128)(2,1)}), bf16[32,160,128]{2,1,0:T(8,128)(2,1)S(1)}, u32[]{:S(2)}, u32[]{:S(2)}) async-start(bf16[32,160,128]{2,1,0:T(8,128)(2,1)} %convolve.3), calls=%async_computation.1 | async-start | bytes 2621440 | tf_op jit(solution)/shard_map/all_to_all | solution.py:386
  62.9 1.2 %copy_bitcast_fusion = bf16[96,4096]{1,0:T(8,128)(2,1)S(1)} fusion(bf16[32,96,128]{2,1,0:T(8,128)(2,1)} %all-to-all-done), kind=kLoop, calls=%fused_computation.1 | loop fusion | bytes 1572864 | tf_op jit(solution)/shard_map/reshape | solution.py:387
  64.1 1.5 %dynamic_update_slice.6 = bf16[256,4096]{1,0:T(8,128)(2,1)} pad(bf16[96,4096]{1,0:T(8,128)(2,1)S(1)} %copy_bitcast_fusion, bf16[]{:T(256)} %constant.16.clone.1), padding=0_160x0_0 | pad | bytes 2883586 | tf_op jit(solution)/shard_map/dynamic_update_slice | solution.py:411
  65.6 29.4 %all-to-all-done.1 = bf16[32,160,128]{2,1,0:T(8,128)(2,1)S(1)} async-done(((bf16[32,160,128]{2,1,0:T(8,128)(2,1)}), bf16[32,160,128]{2,1,0:T(8,128)(2,1)S(1)}, u32[]{:S(2)}, u32[]{:S(2)}) %all-to-all-start.1) | async-done | bytes 1310752 | tf_op jit(solution)/shard_map/all_to_all | solution.py:386
  95.0 1.2 %bitcast_dynamic-update-slice_fusion = bf16[256,4096]{1,0:T(8,128)(2,1)} fusion(bf16[256,4096]{1,0:T(8,128)(2,1)} %dynamic_update_slice.6, bf16[32,160,128]{2,1,0:T(8,128)(2,1)S(1)} %all-to-all-done.1), kind=kLoop, calls=%fused_computation | loop fusion | bytes 2621440 | tf_op jit(solution)/shard_map/dynamic_update_slice | solution.py:414
Async XLA Ops:
  0.0 3.6 %copy-start.2 = (s32[16]{0:T(128)S(1)}, s32[16]{0:T(128)}, u32[]{:S(2)}) copy-start(s32[16]{0:T(128)} %lengths_ref) | copy-start | bytes 196
  0.0 3.6 %copy-start = (bf16[128,512]{1,0:T(8,128)(2,1)S(1)}, bf16[128,512]{1,0:T(8,128)(2,1)}, u32[]{:S(2)}) copy-start(bf16[128,512]{1,0:T(8,128)(2,1)} %long_ref.1) | copy-start | bytes 393220
  0.0 3.7 %copy-start.1 = (bf16[3,7,512]{2,1,0:T(8,128)(2,1)S(1)}, bf16[3,7,512]{2,1,0:T(8,128)(2,1)}, u32[]{:S(2)}) copy-start(bf16[3,7,512]{2,1,0:T(8,128)(2,1)} %short_ref.1) | copy-start | bytes 64516
  1.2 8.2 %collective-permute-start = (bf16[1,16,9216]{2,1,0:T(8,128)(2,1)S(1)}, bf16[1,16,9216]{2,1,0:T(8,128)(2,1)S(1)}, u32[]{:S(2)}, u32[]{:S(2)}) collective-permute-start(bf16[1,16,9216]{2,1,0:T(8,128)(2,1)S(1)} %pack_rows.1), channel_id=1, source_target_pairs={{0,1},{1,2},{2,3},{3,4},{4,5},{5,6},{6,7},{7,8},{8,9},{9,10},{10,1... | collective-permute-start | bytes 884744 | tf_op jit(solution)/shard_map/ppermute | solution.py:378
  10.5 14.8 %collective-permute-start.1 = (bf16[32,96,128]{2,1,0:T(8,128)(2,1)S(1)}, bf16[32,96,128]{2,1,0:T(8,128)(2,1)S(1)}, u32[]{:S(2)}, u32[]{:S(2)}) collective-permute-start(bf16[32,96,128]{2,1,0:T(8,128)(2,1)S(1)} %features.6.mixed_ref), channel_id=1, source_target_pairs={{0,1},{1,2},{2,3},{3,4},{4,5},{5,6},{6,7},{7,8},{8,9},{9,10},{10,1... | collective-permute-start | bytes 2359304 | tf_op jit(solution)/shard_map/ppermute | solution.py:393
  20.1 21.8 %collective-permute-start.2 = (bf16[32,160,128]{2,1,0:T(8,128)(2,1)S(1)}, bf16[32,160,128]{2,1,0:T(8,128)(2,1)}, u32[]{:S(2)}, u32[]{:S(2)}) collective-permute-start(bf16[32,160,128]{2,1,0:T(8,128)(2,1)S(1)} %get-tuple-element.24.mixed_ref), channel_id=1, source_target_pairs={{0,1},{1,2},{2,3},{3,4},{4,5},{5,6},{6,7},{7,8},{8,9},{9,10},{10,1... | collective-permute-start | bytes 3932168 | tf_op jit(solution)/shard_map/ppermute | solution.py:402
  23.4 1.9 %copy-start.3 = (f32[8192]{0:T(1024)S(1)}, f32[8192]{0:T(1024)}, u32[]{:S(2)}) copy-start(f32[8192]{0:T(1024)} %param.12) | copy-start | bytes 98308
  30.5 28.0 %all-to-all-start = ((bf16[32,96,128]{2,1,0:T(8,128)(2,1)}), bf16[32,96,128]{2,1,0:T(8,128)(2,1)}, u32[]{:S(2)}, u32[]{:S(2)}) async-start(bf16[32,96,128]{2,1,0:T(8,128)(2,1)} %convolve.2), calls=%async_computation | async-start | bytes 1572864 | tf_op jit(solution)/shard_map/all_to_all | solution.py:386
  58.5 36.6 %all-to-all-start.1 = ((bf16[32,160,128]{2,1,0:T(8,128)(2,1)}), bf16[32,160,128]{2,1,0:T(8,128)(2,1)S(1)}, u32[]{:S(2)}, u32[]{:S(2)}) async-start(bf16[32,160,128]{2,1,0:T(8,128)(2,1)} %convolve.3), calls=%async_computation.1 | async-start | bytes 2621440 | tf_op jit(solution)/shard_map/all_to_all | solution.py:386
